TPU v7x, 256 devices: a whole 4x4x8 slice. The times are simulated.
256 devices in a mesh: gx: 16 (over z, y_lo), gy: 16 (over y_hi, x, core).
Axes of the slice: x: 4, y: 4 (y_hi: 2, y_lo: 2; y = y_hi * 2 + y_lo), z: 8, core: 2. Of those that a mesh axis runs over, the one named last changes fastest.
Arguments:
- snapshot_panel: float32 [64, 524288], P(None, ('gx', 'gy')), may hold values from -2500 to 2500, as said below
- following: float32 [960, 524288], P(None, ('gx', 'gy')), may hold values from -2500 to 2500, as said below
Outputs:
- basis_rows: float32 [64, 524288], P(None, ('gx', 'gy'))
- upper_factor: float32 [64, 64], replicated
- projection: float32 [64, 960], replicated
Inputs may be any that keep to these rules, and one draw needn't show every extreme that they name: `snapshot_panel`: real-valued snapshots of full rank. `following`: real-valued snapshots.
All inputs are finite; a program needn't handle non-finite values.
Results may differ from a plain program's by a relative error of at most 0.000077.
Values sent between devices are 32-bit elements; how exact they have to be, the bound alone decides.
No kernel may reach another device: no remote copies, remote signals or barrier semaphores. Data moves between devices by JAX's collectives and lax.ppermute only.
A program may use at most 64 MiB of HBM per device.

v0:
```python
import math

import jax
import jax.numpy as jnp
from jax import lax
from jax.sharding import PartitionSpec as P


def swapped(block, axis, distance):
    count = lax.axis_size(axis)
    route = []
    for low in range(count):
        high = low | 1 << distance
        if high != low and high < count:
            route += [(low, high), (high, low)]
    return lax.ppermute(block, axis, route)


def inner_product(left, right):
    return lax.dot_general(
        left,
        right,
        (((1,), (1,)), ((), ())),
        precision=lax.Precision.HIGHEST,
        preferred_element_type=jnp.float32,
    )


def plain_product(left, right):
    return jnp.dot(left, right, precision=lax.Precision.HIGHEST, preferred_element_type=jnp.float32)


def lower_solve(lower_factor, values):
    return jax.scipy.linalg.solve_triangular(lower_factor, values, lower=True)


def merge_blocks(own_block, their_block, panel_width):
    own_lower = own_block[:, :panel_width]
    their_lower = their_block[:, :panel_width]
    summed_gram = inner_product(own_lower, own_lower) + inner_product(their_lower, their_lower)
    merged_lower = jnp.linalg.cholesky(summed_gram)
    carried = plain_product(own_lower, own_block[:, panel_width:]) + plain_product(
        their_lower, their_block[:, panel_width:]
    )
    return jnp.concatenate([merged_lower, lower_solve(merged_lower, carried)], axis=1)


def body(snapshot_panel, following):
    panel_width = snapshot_panel.shape[0]
    root_rows = math.sqrt(snapshot_panel.shape[1] * lax.axis_size(("gx", "gy")))
    local_lower = jnp.linalg.cholesky(inner_product(snapshot_panel, snapshot_panel))
    carried_block = jnp.concatenate(
        [local_lower, lower_solve(local_lower, inner_product(snapshot_panel, following))], axis=1
    )
    for bit_index in range(lax.axis_size("gx").bit_length() - 1):
        carried_block = merge_blocks(
            carried_block, swapped(carried_block, "gx", bit_index), panel_width
        )
    for bit_index in range(lax.axis_size("gy").bit_length() - 1):
        carried_block = merge_blocks(
            carried_block, swapped(carried_block, "gy", bit_index), panel_width
        )
    lower_factor = carried_block[:, :panel_width]
    projected = carried_block[:, panel_width:]
    basis_local = lower_solve(lower_factor, snapshot_panel)
    return (basis_local * root_rows, lower_factor.T / root_rows, projected / root_rows)


def solution(mesh):
    return jax.shard_map(
        body,
        mesh=mesh,
        in_specs=(P(None, ("gx", "gy")), P(None, ("gx", "gy"))),
        out_specs=(P(None, ("gx", "gy")), P(), P()),
        check_vma=False,
    )
```

profile of v0, /device:TPU:1, one launch (start us, length us, event | category | flops | bytes accessed | tf_op | source)
XLA Modules:
  0.0 208.2 jit_solution(6840655435644181527)
XLA Ops:
  0.6 1.0 copy-done
  2.3 5.8 %cholesky.149 = f32[64,64]{1,0:T(8,128)S(1)} custom-call(f32[64,64]{1,0:T(8,128)S(1)} %fusion.34), custom_call_target="Cholesky" | custom-call | tf_op jit(solution)/shard_map/jit(cholesky)/cholesky | solution.py:51
  8.2 0.6 compare_reduce_fusion.8
  8.9 0.7 select_bitcast_fusion.7
  9.5 4.9 %custom-call.18 = f32[1,64,64]{1,2,0:T(8,128)S(1)} custom-call(f32[1,64,64]{2,1,0:T(8,128)S(1)} %get-tuple-element.22), custom_call_target="InvertDiagBlocksLowerTriangular" | custom-call | tf_op jit(solution)/shard_map/jit(_solve_triangular)/triangular_solve | solution.py:34
  14.4 9.6 %fusion.69 = f32[64,960]{1,0:T(8,128)S(1)} fusion(f32[64,2048]{1,0:T(8,128)S(1)} %copy-done, f32[960,2048]{1,0:T(8,128)} %param.6), kind=kOutput, calls=%fused_computation.135 | convolution fusion | flops 1509949440 | bytes 8634368 | tf_op jit(solution)/shard_map/dot_general | solution.py:20
  24.5 2.2 %collective-permute-start = (f32[64,1024]{1,0:T(8,128)S(1)}, f32[64,1024]{1,0:T(8,128)S(1)}, u32[]{:S(2)}, u32[]{:S(2)}) collective-permute-start(f32[64,1024]{1,0:T(8,128)S(1)} %pad_maximum_fusion), channel_id=1, source_target_pairs={{0,16},{16,0},{32,48},{48,32},{64,80},{80,64},{96,112},{112,96},{1... | collective-permute-start | bytes 786440 | tf_op jit(solution)/shard_map/ppermute | solution.py:16
  27.3 4.2 %collective-permute-done = f32[64,1024]{1,0:T(8,128)S(1)} collective-permute-done((f32[64,1024]{1,0:T(8,128)S(1)}, f32[64,1024]{1,0:T(8,128)S(1)}, u32[]{:S(2)}, u32[]{:S(2)}) %collective-permute-start) | collective-permute-done | bytes 262176 | tf_op jit(solution)/shard_map/ppermute | solution.py:16
  31.8 5.8 %cholesky.160 = f32[64,64]{1,0:T(8,128)S(1)} custom-call(f32[64,64]{1,0:T(8,128)S(1)} %fusion.31), custom_call_target="Cholesky" | custom-call | tf_op jit(solution)/shard_map/jit(cholesky)/cholesky | solution.py:41
  38.4 0.7 select_bitcast_fusion.6
  39.0 4.9 %custom-call.19 = f32[1,64,64]{1,2,0:T(8,128)S(1)} custom-call(f32[1,64,64]{2,1,0:T(8,128)S(1)} %get-tuple-element.20), custom_call_target="InvertDiagBlocksLowerTriangular" | custom-call | tf_op jit(solution)/shard_map/jit(_solve_triangular)/triangular_solve | solution.py:34
  45.0 3.0 %collective-permute-start.1 = (f32[64,1024]{1,0:T(8,128)S(1)}, f32[64,1024]{1,0:T(8,128)S(1)}, u32[]{:S(2)}, u32[]{:S(2)}) collective-permute-start(f32[64,1024]{1,0:T(8,128)S(1)} %pad_maximum_fusion.1), channel_id=1, source_target_pairs={{0,32},{32,0},{16,48},{48,16},{64,96},{96,64},{80,112},{112,80},{1... | collective-permute-start | bytes 786440 | tf_op jit(solution)/shard_map/ppermute | solution.py:16
  48.5 4.4 %collective-permute-done.1 = f32[64,1024]{1,0:T(8,128)S(1)} collective-permute-done((f32[64,1024]{1,0:T(8,128)S(1)}, f32[64,1024]{1,0:T(8,128)S(1)}, u32[]{:S(2)}, u32[]{:S(2)}) %collective-permute-start.1) | collective-permute-done | bytes 262176 | tf_op jit(solution)/shard_map/ppermute | solution.py:16
  53.2 5.8 %cholesky.171 = f32[64,64]{1,0:T(8,128)S(1)} custom-call(f32[64,64]{1,0:T(8,128)S(1)} %fusion.28), custom_call_target="Cholesky" | custom-call | tf_op jit(solution)/shard_map/jit(cholesky)/cholesky | solution.py:41
  59.7 0.7 select_bitcast_fusion.5
  60.3 4.9 %custom-call.20 = f32[1,64,64]{1,2,0:T(8,128)S(1)} custom-call(f32[1,64,64]{2,1,0:T(8,128)S(1)} %get-tuple-element.18), custom_call_target="InvertDiagBlocksLowerTriangular" | custom-call | tf_op jit(solution)/shard_map/jit(_solve_triangular)/triangular_solve | solution.py:34
  66.3 3.2 %collective-permute-start.2 = (f32[64,1024]{1,0:T(8,128)S(1)}, f32[64,1024]{1,0:T(8,128)S(1)}, u32[]{:S(2)}, u32[]{:S(2)}) collective-permute-start(f32[64,1024]{1,0:T(8,128)S(1)} %pad_maximum_fusion.2), channel_id=1, source_target_pairs={{0,64},{64,0},{16,80},{80,16},{32,96},{96,32},{48,112},{112,48},{1... | collective-permute-start | bytes 786440 | tf_op jit(solution)/shard_map/ppermute | solution.py:16
  70.0 10.8 %collective-permute-done.2 = f32[64,1024]{1,0:T(8,128)S(1)} collective-permute-done((f32[64,1024]{1,0:T(8,128)S(1)}, f32[64,1024]{1,0:T(8,128)S(1)}, u32[]{:S(2)}, u32[]{:S(2)}) %collective-permute-start.2) | collective-permute-done | bytes 262176 | tf_op jit(solution)/shard_map/ppermute | solution.py:16
  81.1 5.8 %cholesky.182 = f32[64,64]{1,0:T(8,128)S(1)} custom-call(f32[64,64]{1,0:T(8,128)S(1)} %fusion.25), custom_call_target="Cholesky" | custom-call | tf_op jit(solution)/shard_map/jit(cholesky)/cholesky | solution.py:41
  87.6 0.7 select_bitcast_fusion.4
  88.2 4.9 %custom-call.21 = f32[1,64,64]{1,2,0:T(8,128)S(1)} custom-call(f32[1,64,64]{2,1,0:T(8,128)S(1)} %get-tuple-element.16), custom_call_target="InvertDiagBlocksLowerTriangular" | custom-call | tf_op jit(solution)/shard_map/jit(_solve_triangular)/triangular_solve | solution.py:34
  94.2 6.5 %collective-permute-start.3 = (f32[64,1024]{1,0:T(8,128)S(1)}, f32[64,1024]{1,0:T(8,128)S(1)}, u32[]{:S(2)}, u32[]{:S(2)}) collective-permute-start(f32[64,1024]{1,0:T(8,128)S(1)} %pad_maximum_fusion.3), channel_id=1, source_target_pairs={{0,128},{128,0},{16,144},{144,16},{32,160},{160,32},{48,176},{176,... | collective-permute-start | bytes 786440 | tf_op jit(solution)/shard_map/ppermute | solution.py:16
  101.3 8.0 %collective-permute-done.3 = f32[64,1024]{1,0:T(8,128)S(1)} collective-permute-done((f32[64,1024]{1,0:T(8,128)S(1)}, f32[64,1024]{1,0:T(8,128)S(1)}, u32[]{:S(2)}, u32[]{:S(2)}) %collective-permute-start.3) | collective-permute-done | bytes 262176 | tf_op jit(solution)/shard_map/ppermute | solution.py:16
  109.5 5.8 %cholesky.193 = f32[64,64]{1,0:T(8,128)S(1)} custom-call(f32[64,64]{1,0:T(8,128)S(1)} %fusion.22), custom_call_target="Cholesky" | custom-call | tf_op jit(solution)/shard_map/jit(cholesky)/cholesky | solution.py:41
  116.1 0.7 select_bitcast_fusion.3
  116.7 4.9 %custom-call.22 = f32[1,64,64]{1,2,0:T(8,128)S(1)} custom-call(f32[1,64,64]{2,1,0:T(8,128)S(1)} %get-tuple-element.14), custom_call_target="InvertDiagBlocksLowerTriangular" | custom-call | tf_op jit(solution)/shard_map/jit(_solve_triangular)/triangular_solve | solution.py:34
  122.7 4.7 %collective-permute-start.4 = (f32[64,1024]{1,0:T(8,128)S(1)}, f32[64,1024]{1,0:T(8,128)S(1)}, u32[]{:S(2)}, u32[]{:S(2)}) collective-permute-start(f32[64,1024]{1,0:T(8,128)S(1)} %pad_maximum_fusion.4), channel_id=1, source_target_pairs={{0,1},{1,0},{2,3},{3,2},{4,5},{5,4},{6,7},{7,6},{8,9},{9,8},{10,11... | collective-permute-start | bytes 786440 | tf_op jit(solution)/shard_map/ppermute | solution.py:16
  128.8 5.8 %cholesky.204 = f32[64,64]{1,0:T(8,128)S(1)} custom-call(f32[64,64]{1,0:T(8,128)S(1)} %fusion.19), custom_call_target="Cholesky" | custom-call | tf_op jit(solution)/shard_map/jit(cholesky)/cholesky | solution.py:41
  135.3 0.7 select_bitcast_fusion.2
  136.0 4.9 %custom-call.23 = f32[1,64,64]{1,2,0:T(8,128)S(1)} custom-call(f32[1,64,64]{2,1,0:T(8,128)S(1)} %get-tuple-element.12), custom_call_target="InvertDiagBlocksLowerTriangular" | custom-call | tf_op jit(solution)/shard_map/jit(_solve_triangular)/triangular_solve | solution.py:34
  141.9 1.3 collective-permute-start.5
  143.8 5.7 %collective-permute-done.5 = f32[64,1024]{1,0:T(8,128)S(1)} collective-permute-done((f32[64,1024]{1,0:T(8,128)S(1)}, f32[64,1024]{1,0:T(8,128)S(1)}, u32[]{:S(2)}, u32[]{:S(2)}) %collective-permute-start.5) | collective-permute-done | bytes 262176 | tf_op jit(solution)/shard_map/ppermute | solution.py:16
  149.8 5.8 %cholesky.215 = f32[64,64]{1,0:T(8,128)S(1)} custom-call(f32[64,64]{1,0:T(8,128)S(1)} %fusion.16), custom_call_target="Cholesky" | custom-call | tf_op jit(solution)/shard_map/jit(cholesky)/cholesky | solution.py:41
  156.4 0.7 select_bitcast_fusion.1
  157.0 4.9 %custom-call.24 = f32[1,64,64]{1,2,0:T(8,128)S(1)} custom-call(f32[1,64,64]{2,1,0:T(8,128)S(1)} %get-tuple-element.10), custom_call_target="InvertDiagBlocksLowerTriangular" | custom-call | tf_op jit(solution)/shard_map/jit(_solve_triangular)/triangular_solve | solution.py:34
  163.0 2.9 %collective-permute-start.6 = (f32[64,1024]{1,0:T(8,128)S(1)}, f32[64,1024]{1,0:T(8,128)S(1)}, u32[]{:S(2)}, u32[]{:S(2)}) collective-permute-start(f32[64,1024]{1,0:T(8,128)S(1)} %pad_maximum_fusion.6), channel_id=1, source_target_pairs={{0,4},{4,0},{1,5},{5,1},{2,6},{6,2},{3,7},{7,3},{8,12},{12,8},{9,1... | collective-permute-start | bytes 786440 | tf_op jit(solution)/shard_map/ppermute | solution.py:16
  166.4 4.8 %collective-permute-done.6 = f32[64,1024]{1,0:T(8,128)S(1)} collective-permute-done((f32[64,1024]{1,0:T(8,128)S(1)}, f32[64,1024]{1,0:T(8,128)S(1)}, u32[]{:S(2)}, u32[]{:S(2)}) %collective-permute-start.6) | collective-permute-done | bytes 262176 | tf_op jit(solution)/shard_map/ppermute | solution.py:16
  171.4 5.8 %cholesky.226 = f32[64,64]{1,0:T(8,128)S(1)} custom-call(f32[64,64]{1,0:T(8,128)S(1)} %fusion.13), custom_call_target="Cholesky" | custom-call | tf_op jit(solution)/shard_map/jit(cholesky)/cholesky | solution.py:41
  177.9 0.7 select_bitcast_fusion
  178.6 4.9 %custom-call.25 = f32[1,64,64]{1,2,0:T(8,128)S(1)} custom-call(f32[1,64,64]{2,1,0:T(8,128)S(1)} %get-tuple-element.8), custom_call_target="InvertDiagBlocksLowerTriangular" | custom-call | tf_op jit(solution)/shard_map/jit(_solve_triangular)/triangular_solve | solution.py:34
  184.6 3.3 %collective-permute-start.7 = (f32[64,1024]{1,0:T(8,128)S(1)}, f32[64,1024]{1,0:T(8,128)S(1)}, u32[]{:S(2)}, u32[]{:S(2)}) collective-permute-start(f32[64,1024]{1,0:T(8,128)S(1)} %pad_maximum_fusion.7), channel_id=1, source_target_pairs={{0,8},{8,0},{1,9},{9,1},{2,10},{10,2},{3,11},{11,3},{4,12},{12,4},... | collective-permute-start | bytes 786440 | tf_op jit(solution)/shard_map/ppermute | solution.py:16
  188.4 3.7 %collective-permute-done.7 = f32[64,1024]{1,0:T(8,128)S(1)} collective-permute-done((f32[64,1024]{1,0:T(8,128)S(1)}, f32[64,1024]{1,0:T(8,128)S(1)}, u32[]{:S(2)}, u32[]{:S(2)}) %collective-permute-start.7) | collective-permute-done | bytes 262176 | tf_op jit(solution)/shard_map/ppermute | solution.py:16
  192.4 5.8 %cholesky.237 = f32[64,64]{1,0:T(8,128)S(1)} custom-call(f32[64,64]{1,0:T(8,128)S(1)} %fusion.10), custom_call_target="Cholesky" | custom-call | tf_op jit(solution)/shard_map/jit(cholesky)/cholesky | solution.py:41
  198.9 0.7 multiply_bitcast_fusion
  199.6 0.7 copy.30
  200.3 4.9 %custom-call.9 = f32[1,64,64]{1,2,0:T(8,128)S(1)} custom-call(f32[1,64,64]{2,1,0:T(8,128)S(1)} %get-tuple-element.25), custom_call_target="InvertDiagBlocksLowerTriangular" | custom-call | tf_op jit(solution)/shard_map/jit(_solve_triangular)/triangular_solve | solution.py:34
  205.2 1.4 convolution_multiply_fusion
  207.1 1.1 convolution_multiply_fusion.1
  (86 shorter events, 21.3 us)
Async XLA Ops:
  0.6 1.0 copy-start
  24.5 7.0 %collective-permute-start = (f32[64,1024]{1,0:T(8,128)S(1)}, f32[64,1024]{1,0:T(8,128)S(1)}, u32[]{:S(2)}, u32[]{:S(2)}) collective-permute-start(f32[64,1024]{1,0:T(8,128)S(1)} %pad_maximum_fusion), channel_id=1, source_target_pairs={{0,16},{16,0},{32,48},{48,32},{64,80},{80,64},{96,112},{112,96},{1... | collective-permute-start | bytes 786440 | tf_op jit(solution)/shard_map/ppermute | solution.py:16
  45.0 7.9 %collective-permute-start.1 = (f32[64,1024]{1,0:T(8,128)S(1)}, f32[64,1024]{1,0:T(8,128)S(1)}, u32[]{:S(2)}, u32[]{:S(2)}) collective-permute-start(f32[64,1024]{1,0:T(8,128)S(1)} %pad_maximum_fusion.1), channel_id=1, source_target_pairs={{0,32},{32,0},{16,48},{48,16},{64,96},{96,64},{80,112},{112,80},{1... | collective-permute-start | bytes 786440 | tf_op jit(solution)/shard_map/ppermute | solution.py:16
  66.3 14.5 %collective-permute-start.2 = (f32[64,1024]{1,0:T(8,128)S(1)}, f32[64,1024]{1,0:T(8,128)S(1)}, u32[]{:S(2)}, u32[]{:S(2)}) collective-permute-start(f32[64,1024]{1,0:T(8,128)S(1)} %pad_maximum_fusion.2), channel_id=1, source_target_pairs={{0,64},{64,0},{16,80},{80,16},{32,96},{96,32},{48,112},{112,48},{1... | collective-permute-start | bytes 786440 | tf_op jit(solution)/shard_map/ppermute | solution.py:16
  94.2 15.1 %collective-permute-start.3 = (f32[64,1024]{1,0:T(8,128)S(1)}, f32[64,1024]{1,0:T(8,128)S(1)}, u32[]{:S(2)}, u32[]{:S(2)}) collective-permute-start(f32[64,1024]{1,0:T(8,128)S(1)} %pad_maximum_fusion.3), channel_id=1, source_target_pairs={{0,128},{128,0},{16,144},{144,16},{32,160},{160,32},{48,176},{176,... | collective-permute-start | bytes 786440 | tf_op jit(solution)/shard_map/ppermute | solution.py:16
  122.7 5.8 %collective-permute-start.4 = (f32[64,1024]{1,0:T(8,128)S(1)}, f32[64,1024]{1,0:T(8,128)S(1)}, u32[]{:S(2)}, u32[]{:S(2)}) collective-permute-start(f32[64,1024]{1,0:T(8,128)S(1)} %pad_maximum_fusion.4), channel_id=1, source_target_pairs={{0,1},{1,0},{2,3},{3,2},{4,5},{5,4},{6,7},{7,6},{8,9},{9,8},{10,11... | collective-permute-start | bytes 786440 | tf_op jit(solution)/shard_map/ppermute | solution.py:16
  141.9 7.6 %collective-permute-start.5 = (f32[64,1024]{1,0:T(8,128)S(1)}, f32[64,1024]{1,0:T(8,128)S(1)}, u32[]{:S(2)}, u32[]{:S(2)}) collective-permute-start(f32[64,1024]{1,0:T(8,128)S(1)} %pad_maximum_fusion.5), channel_id=1, source_target_pairs={{0,2},{2,0},{1,3},{3,1},{4,6},{6,4},{5,7},{7,5},{8,10},{10,8},{9,1... | collective-permute-start | bytes 786440 | tf_op jit(solution)/shard_map/ppermute | solution.py:16
  163.0 8.2 %collective-permute-start.6 = (f32[64,1024]{1,0:T(8,128)S(1)}, f32[64,1024]{1,0:T(8,128)S(1)}, u32[]{:S(2)}, u32[]{:S(2)}) collective-permute-start(f32[64,1024]{1,0:T(8,128)S(1)} %pad_maximum_fusion.6), channel_id=1, source_target_pairs={{0,4},{4,0},{1,5},{5,1},{2,6},{6,2},{3,7},{7,3},{8,12},{12,8},{9,1... | collective-permute-start | bytes 786440 | tf_op jit(solution)/shard_map/ppermute | solution.py:16
  184.6 7.5 %collective-permute-start.7 = (f32[64,1024]{1,0:T(8,128)S(1)}, f32[64,1024]{1,0:T(8,128)S(1)}, u32[]{:S(2)}, u32[]{:S(2)}) collective-permute-start(f32[64,1024]{1,0:T(8,128)S(1)} %pad_maximum_fusion.7), channel_id=1, source_target_pairs={{0,8},{8,0},{1,9},{9,1},{2,10},{10,2},{3,11},{11,3},{4,12},{12,4},... | collective-permute-start | bytes 786440 | tf_op jit(solution)/shard_map/ppermute | solution.py:16
where the time goes:
time: 210 us; the launch traced here: 208 us
  other arithmetic  110 us (52%)
  waiting for transfers between devices  42.1 us (20%)
  starting transfers between devices  27 us (13%)
  matrix products  25.6 us (12%)
  local copies, waits for them, and re-layouts  2.41 us (1%)
    another operation x24, other arithmetic, merge_blocks(): merged_lower = jnp.linalg.cholesky(summed_gram)  52.2 us
    another operation x17, other arithmetic, lower_solve(): return jax.scipy.linalg.solve_triangular(lower_factor, values, lower=True)  49.3 us
    ppermute x8, waiting for transfers between devices, swapped(): return lax.ppermute(block, axis, route)  42.1 us
    ppermute x8, starting transfers between devices, swapped(): return lax.ppermute(block, axis, route)  27 us
    dot_general x18, matrix products, inner_product(): lax.dot_general(left, right, (((1,), (1,)), ((), ())), precision=lax.Prec...  13.1 us
    dot_general x16, matrix products, plain_product(): jnp.dot(left, right, precision=lax.Precision.HIGHEST, preferred_element_t...  6.73 us
    another operation x3, other arithmetic, body(): jnp.linalg.cholesky(inner_product(snapshot_panel, snapshot_panel))  6.52 us
    another operation x10, matrix products, lower_solve(): return jax.scipy.linalg.solve_triangular(lower_factor, values, lower=True)  5.85 us
  transfers between devices with their start and end apart: 8, of which 8 were waited for; matrix products, arithmetic and copies ran while one was open for 2% of the time, Pallas kernels for 0%

commit v1 on v0

v1 whole, which is shorter than its diff:
```python
import math

import jax
import jax.numpy as jnp
import numpy as np
from jax import lax
from jax.experimental import pallas as pl
from jax.experimental.pallas import tpu as pltpu
from jax.sharding import PartitionSpec as P

AXES = ("gx", "gy")
SIZES = (8, 2, 2, 4, 2)
LAST = (((1,), (1,)), ((), ()))
MIB = 1 << 20


def route(place, core=None):
    pairs = []
    for index, (z, y_lo, y_hi, x, c) in enumerate(np.ndindex(*SIZES)):
        if core is None or c == core:
            tz, ty, tx, tc = place(z, 2 * y_hi + y_lo, x, c)
            pairs.append((index, int(np.ravel_multi_index((tz, ty % 2, ty // 2, tx, tc), SIZES))))
    return pairs


def x_flip(mask):
    return lambda z, y, x, c: (z, y, x ^ mask, c)


def y_flip(mask):
    return lambda z, y, x, c: (z, y ^ mask, x, c)


def z_flip(mask):
    return lambda z, y, x, c: (z ^ mask, y, x, c)


def core_flip(z, y, x, c):
    return (z, y, x, c ^ 1)


def summed(blocks, cores, flips):
    blocks = [b + lax.ppermute(b, AXES, route(core_flip, 1 - c)) for b, c in zip(blocks, cores)]
    for flip in zip(*flips):
        blocks = [b + lax.ppermute(b, AXES, route(f, c)) for b, c, f in zip(blocks, cores, flip)]
        blocks[:2] = lax.optimization_barrier(blocks[:2])
    core = lax.axis_index("gy") % 2
    return [jnp.where(core == c, b, lax.ppermute(b, AXES, route(core_flip, c))) for b, c in zip(blocks, cores)]


def parts3(values):
    high = values.astype(jnp.bfloat16)
    rest = values - high.astype(jnp.float32)
    middle = rest.astype(jnp.bfloat16)
    return high, middle, (rest - middle.astype(jnp.float32)).astype(jnp.bfloat16)


def last_product(left, right):
    return lax.dot_general(left, right, LAST, preferred_element_type=jnp.float32)


def local_products(panel, following):
    width, cells = panel.shape
    count = following.shape[0]
    half = 512
    pieces = 4
    piece = cells // pieces

    def kernel(panel_hbm, following_hbm, gram_ref, first_ref, second_ref, panel_v, following_v, stack, total, sem):
        panel_copy = pltpu.make_async_copy(panel_hbm, panel_v, sem.at[0])
        panel_copy.start()
        copies = []
        for i in range(pieces):
            columns = pl.ds(i * piece, piece)
            copies.append(
                pltpu.make_async_copy(following_hbm.at[:, columns], following_v.at[:, columns], sem.at[1 + i])
            )
            copies[-1].start()
        panel_copy.wait()
        high, middle, low = parts3(panel_v[...])
        stack[0:width] = high
        stack[width : 2 * width] = middle
        stack[2 * width :] = low
        whole = stack[...]
        sums = last_product(whole, high) + last_product(whole, middle) + last_product(whole, low)
        gram = sums[:width] + sums[width : 2 * width] + sums[2 * width :]
        gram_ref[:, :width] = gram[: width // 2]
        gram_ref[:, width:] = gram[width // 2 :]
        for i in range(pieces):
            copies[i].wait()
            columns = slice(i * piece, (i + 1) * piece)
            values = following_v[:, columns]
            high = values.astype(jnp.bfloat16)
            low = (values - high.astype(jnp.float32)).astype(jnp.bfloat16)
            part = stack[:, columns]
            sums = last_product(part, high) + last_product(part, low)
            if i:
                total[...] += sums
            else:
                total[...] = sums
        cross = total[:width] + total[width : 2 * width] + total[2 * width :]
        first_ref[...] = cross[:, :half]
        second_ref[...] = cross[:, half:]

    return pl.pallas_call(
        kernel,
        out_shape=(
            jax.ShapeDtypeStruct((width // 2, 2 * width), jnp.float32),
            jax.ShapeDtypeStruct((width, half), jnp.float32),
            jax.ShapeDtypeStruct((width, count - half), jnp.float32),
        ),
        in_specs=[pl.BlockSpec(memory_space=pl.ANY)] * 2,
        out_specs=(pl.BlockSpec(memory_space=pltpu.VMEM),) * 3,
        scratch_shapes=[
            pltpu.VMEM((width, cells), jnp.float32),
            pltpu.VMEM((count, cells), jnp.float32),
            pltpu.VMEM((3 * width, cells), jnp.bfloat16),
            pltpu.VMEM((3 * width, count), jnp.float32),
            pltpu.SemaphoreType.DMA((1 + pieces,)),
        ],
        compiler_params=pltpu.CompilerParams(vmem_limit_bytes=56 * MIB),
        name="local_products",
    )(panel, following)


def factor(gram, panel, root_rows):
    width, cells = panel.shape

    def kernel(gram_ref, panel_ref, upper_ref, inverse_ref, basis_ref):
        rows = lax.broadcasted_iota(jnp.int32, (width, 2 * width), 0)
        lanes = lax.broadcasted_iota(jnp.int32, (width, 2 * width), 1)
        whole = jnp.concatenate([gram_ref[:, :width], gram_ref[:, width:]], axis=0)
        unit = (rows[:, :width] == lanes[:, :width]).astype(jnp.float32)
        work = jnp.concatenate([whole, unit], axis=1)
        for k in range(width - 1):
            row = work[k : k + 1, :]
            column = jnp.broadcast_to(work[:, k : k + 1], (width, 2 * width))
            pivot = column[k : k + 1, :]
            work = work - jnp.where(rows > k, column, 0.0) * (row / pivot)
        pivots = jnp.sum(jnp.where(rows == lanes, work, 0.0), axis=1, keepdims=True)
        work = work / jnp.sqrt(pivots)
        upper = work[:, :width]
        inverse = work[:, width:]
        upper_ref[...] = jnp.where(rows[:, :width] <= lanes[:, :width], upper, 0.0) * (1.0 / root_rows)
        inverse_ref[...] = inverse * (1.0 / root_rows)
        lh, lm, ll = parts3(inverse * root_rows)
        ph, pm, po = parts3(panel_ref[...])
        left = jnp.concatenate([lh, lh, lh, lm, lm, ll], axis=1)
        right = jnp.concatenate([ph, pm, po, ph, pm, ph], axis=0)
        basis_ref[...] = jnp.dot(left, right, preferred_element_type=jnp.float32)

    return pl.pallas_call(
        kernel,
        out_shape=(
            jax.ShapeDtypeStruct((width, width), jnp.float32),
            jax.ShapeDtypeStruct((width, width), jnp.float32),
            jax.ShapeDtypeStruct((width, cells), jnp.float32),
        ),
        compiler_params=pltpu.CompilerParams(vmem_limit_bytes=32 * MIB),
        name="factor",
    )(gram, panel)


def body(snapshot_panel, following):
    root_rows = math.sqrt(snapshot_panel.shape[1] * lax.axis_size(AXES))
    gram, first, second = local_products(snapshot_panel, following)
    mirror = z_flip(7)
    near = [x_flip(1), x_flip(2), y_flip(1), y_flip(2), mirror, z_flip(1), z_flip(2)]
    one = [x_flip(1), x_flip(3), y_flip(1), y_flip(3), mirror, z_flip(1), z_flip(2)]
    two = [z_flip(1), z_flip(2), mirror, y_flip(1), y_flip(3), x_flip(1), x_flip(3)]
    gram, first, second = summed([gram, first, second], [0, 1, 1], [near, one, two])
    upper, inverse, basis = factor(gram, snapshot_panel, root_rows)
    cross = jnp.concatenate([first, second], axis=1)
    projection = jnp.dot(inverse, cross, precision=lax.Precision.HIGHEST, preferred_element_type=jnp.float32)
    return basis, upper, projection


def solution(mesh):
    return jax.shard_map(
        body,
        mesh=mesh,
        in_specs=(P(None, AXES), P(None, AXES)),
        out_specs=(P(None, AXES), P(), P()),
        check_vma=False,
    )
```

time: 210 us -> 91.9 us (0.44)
  other arithmetic: 110 us -> 2.95 us
  starting transfers between devices: 27 us -> 64.2 us
  waiting for transfers between devices: 42.1 us -> 7.81 us
  matrix products: 25.6 us -> 1.06 us
  Pallas kernels: 0 us -> 14 us
  local copies, waits for them, and re-layouts: 2.41 us -> 0.01 us
    another operation x44 -> x0, other arithmetic: 108 us -> none  [the longest x24 52.2 us: merge_blocks(): merged_lower = jnp.linalg.cholesky(summed_gram)]
    ppermute x8 -> x27, starting transfers between devices: 27 us -> 64.2 us  [the longest x21 53.4 us: summed(): lax.ppermute(b, AXES, route(f, c))]
    ppermute x8 -> x27, waiting for transfers between devices: 42.1 us -> 7.81 us  [the longest x3 4 us: summed(): lax.ppermute(b, AXES, route(core_flip, 1 - c))]
    dot_general x34 -> x1, matrix products: 19.8 us -> 1.06 us  [body(): jnp.dot(inverse, cross, precision=lax.Precision.HIGHEST, preferred_elemen...]
    pallas_call x0 -> x2, Pallas kernels: none -> 14 us  [the longest x1 7.35 us: local_products(): pl.pallas_call(kernel, out_shape=(jax.ShapeDtypeStruct((width // 2, 2 * w...]
    another operation x10 -> x0, matrix products: 5.85 us -> none  [lower_solve(): return jax.scipy.linalg.solve_triangular(lower_factor, values, lower=True)]
    add x0 -> x24, other arithmetic: none -> 2.9 us  [the longest x3 2.58 us: summed(): b + lax.ppermute(b, AXES, route(core_flip, 1 - c))]
  transfers between devices with their start and end apart: 8 -> 27, of which waited for: 8 -> 4; matrix products, arithmetic and copies ran while one was open for 2% -> 3% of each run, Pallas kernels for 0% -> 7%
where the time goes in v1:
time: 91.9 us; the launch traced here: 91.2 us
  starting transfers between devices  64.2 us (70%)
  Pallas kernels  14 us (15%)
  waiting for transfers between devices  7.81 us (8%)
  other arithmetic  2.95 us (3%)
  between operations  1.22 us (1%)
  matrix products  1.06 us (1%)
    ppermute x21, starting transfers between devices, summed(): lax.ppermute(b, AXES, route(f, c))  53.4 us
    pallas_call x1, Pallas kernels, local_products(): pl.pallas_call(kernel, out_shape=(jax.ShapeDtypeStruct((width // 2, 2 * w...  7.35 us
    ppermute x3, starting transfers between devices, summed(): lax.ppermute(b, AXES, route(core_flip, c))  6.93 us
    pallas_call x1, Pallas kernels, factor(): pl.pallas_call(kernel, out_shape=(jax.ShapeDtypeStruct((width, width), jn...  6.62 us
    ppermute x3, waiting for transfers between devices, summed(): lax.ppermute(b, AXES, route(core_flip, 1 - c))  4 us
    ppermute x3, starting transfers between devices, summed(): lax.ppermute(b, AXES, route(core_flip, 1 - c))  3.87 us
    ppermute x21, waiting for transfers between devices, summed(): lax.ppermute(b, AXES, route(f, c))  3.8 us
    add x3, other arithmetic, summed(): b + lax.ppermute(b, AXES, route(core_flip, 1 - c))  2.58 us
  transfers between devices with their start and end apart: 27, of which 4 were waited for; matrix products, arithmetic and copies ran while one was open for 3% of the time, Pallas kernels for 7%

profile of v1, /device:TPU:1, one launch (start us, length us, event | category | flops | bytes accessed | tf_op | source)
XLA Modules:
  0.0 91.2 jit_solution(1602374234463148732)
XLA Ops:
  0.6 7.3 %local_products.1 = (f32[32,128]{1,0:T(8,128)}, f32[64,512]{1,0:T(8,128)}, f32[64,448]{1,0:T(8,128)}) custom-call(f32[64,2048]{1,0:T(8,128)} %panel_ref.1, f32[960,2048]{1,0:T(8,128)} %following_hbm.1), custom_call_target="tpu_custom_call" | custom-call | tf_op jit(solution)/shard_map/local_products/pallas_call | solution.py:105
  8.0 1.3 %collective-permute-start.2 = (f32[64,512]{1,0:T(8,128)}, f32[64,512]{1,0:T(8,128)S(1)}, u32[]{:S(2)}, u32[]{:S(2)}) collective-permute-start(f32[64,512]{1,0:T(8,128)} %get-tuple-element.24), channel_id=1, source_target_pairs={{0,1},{2,3},{4,5},{6,7},{8,9},{10,11},{12,13},{14,15},{16,17},{18,... | collective-permute-start | bytes 393224 | tf_op jit(solution)/shard_map/ppermute | solution.py:43
  9.3 1.3 %collective-permute-start.18 = (f32[64,448]{1,0:T(8,128)}, f32[64,448]{1,0:T(8,128)S(1)}, u32[]{:S(2)}, u32[]{:S(2)}) collective-permute-start(f32[64,448]{1,0:T(8,128)} %get-tuple-element.42), channel_id=1, source_target_pairs={{0,1},{2,3},{4,5},{6,7},{8,9},{10,11},{12,13},{14,15},{16,17},{18,... | collective-permute-start | bytes 344072 | tf_op jit(solution)/shard_map/ppermute | solution.py:43
  10.6 3.0 %collective-permute-done.2 = f32[64,512]{1,0:T(8,128)S(1)} collective-permute-done((f32[64,512]{1,0:T(8,128)}, f32[64,512]{1,0:T(8,128)S(1)}, u32[]{:S(2)}, u32[]{:S(2)}) %collective-permute-start.2) | collective-permute-done | bytes 131104 | tf_op jit(solution)/shard_map/ppermute | solution.py:43
  13.6 0.9 %add.79 = f32[64,512]{1,0:T(8,128)S(1)} add(f32[64,512]{1,0:T(8,128)} %get-tuple-element.24, f32[64,512]{1,0:T(8,128)S(1)} %collective-permute-done.2) | non-fusion elementwise | flops 32768 | bytes 393216 | tf_op jit(solution)/shard_map/add | solution.py:43
  14.5 1.9 %collective-permute-start.3 = (f32[64,512]{1,0:T(8,128)S(1)}, f32[64,512]{1,0:T(8,128)S(1)}, u32[]{:S(2)}, u32[]{:S(2)}) collective-permute-start(f32[64,512]{1,0:T(8,128)S(1)} %add.79), channel_id=1, source_target_pairs={{1,3},{3,1},{5,7},{7,5},{9,11},{11,9},{13,15},{15,13},{17,19},{19,... | collective-permute-start | bytes 393224 | tf_op jit(solution)/shard_map/ppermute | solution.py:45
  16.4 0.9 %add.93 = f32[64,448]{1,0:T(8,128)S(1)} add(f32[64,448]{1,0:T(8,128)} %get-tuple-element.42, f32[64,448]{1,0:T(8,128)S(1)} %collective-permute-done.18) | non-fusion elementwise | flops 28672 | bytes 344064 | tf_op jit(solution)/shard_map/add | solution.py:43
  17.4 3.5 %collective-permute-start.19 = (f32[64,448]{1,0:T(8,128)S(1)}, f32[64,448]{1,0:T(8,128)S(1)}, u32[]{:S(2)}, u32[]{:S(2)}) collective-permute-start(f32[64,448]{1,0:T(8,128)S(1)} %add.93), channel_id=1, source_target_pairs={{1,33},{3,35},{5,37},{7,39},{9,41},{11,43},{13,45},{15,47},{17,49}... | collective-permute-start | bytes 344072 | tf_op jit(solution)/shard_map/ppermute | solution.py:45
  20.8 1.3 %collective-permute-start = (f32[32,128]{1,0:T(8,128)}, f32[32,128]{1,0:T(8,128)S(1)}, u32[]{:S(2)}, u32[]{:S(2)}) collective-permute-start(f32[32,128]{1,0:T(8,128)} %get-tuple-element.23), channel_id=1, source_target_pairs={{1,0},{3,2},{5,4},{7,6},{9,8},{11,10},{13,12},{15,14},{17,16},{19,... | collective-permute-start | bytes 49160 | tf_op jit(solution)/shard_map/ppermute | solution.py:43
  22.1 1.0 %collective-permute-done = f32[32,128]{1,0:T(8,128)S(1)} collective-permute-done((f32[32,128]{1,0:T(8,128)}, f32[32,128]{1,0:T(8,128)S(1)}, u32[]{:S(2)}, u32[]{:S(2)}) %collective-permute-start) | collective-permute-done | bytes 16416 | tf_op jit(solution)/shard_map/ppermute | solution.py:43
  23.2 0.7 add.77
  23.9 0.7 collective-permute-start.1
  24.5 0.0 collective-permute-done.19
  24.6 4.9 %collective-permute-start.20 = (f32[64,448]{1,0:T(8,128)S(1)}, f32[64,448]{1,0:T(8,128)S(1)}, u32[]{:S(2)}, u32[]{:S(2)}) collective-permute-start(f32[64,448]{1,0:T(8,128)S(1)} %add.94), channel_id=1, source_target_pairs={{1,65},{3,67},{5,69},{7,71},{9,73},{11,75},{13,77},{15,79},{17,81}... | collective-permute-start | bytes 344072 | tf_op jit(solution)/shard_map/ppermute | solution.py:45
  29.5 0.0 collective-permute-done.1
  29.5 3.7 %collective-permute-start.5 = (f32[64,512]{1,0:T(8,128)S(1)}, f32[64,512]{1,0:T(8,128)S(1)}, u32[]{:S(2)}, u32[]{:S(2)}) collective-permute-start(f32[64,512]{1,0:T(8,128)S(1)} %add.80), channel_id=1, source_target_pairs={{1,7},{3,5},{5,3},{7,1},{9,15},{11,13},{13,11},{15,9},{17,23},{19,... | collective-permute-start | bytes 393224 | tf_op jit(solution)/shard_map/ppermute | solution.py:45
  33.3 5.9 %collective-permute-start.21 = (f32[64,448]{1,0:T(8,128)S(1)}, f32[64,448]{1,0:T(8,128)S(1)}, u32[]{:S(2)}, u32[]{:S(2)}) collective-permute-start(f32[64,448]{1,0:T(8,128)S(1)} %add.95), channel_id=1, source_target_pairs={{1,225},{3,227},{5,229},{7,231},{9,233},{11,235},{13,237},{15,239}... | collective-permute-start | bytes 344072 | tf_op jit(solution)/shard_map/ppermute | solution.py:45
  39.2 0.7 collective-permute-start.4
  39.9 0.0 collective-permute-done.5
  39.9 3.2 %collective-permute-start.7 = (f32[64,512]{1,0:T(8,128)S(1)}, f32[64,512]{1,0:T(8,128)S(1)}, u32[]{:S(2)}, u32[]{:S(2)}) collective-permute-start(f32[64,512]{1,0:T(8,128)S(1)} %add.82), channel_id=1, source_target_pairs={{1,17},{3,19},{5,21},{7,23},{9,25},{11,27},{13,29},{15,31},{17,1},... | collective-permute-start | bytes 393224 | tf_op jit(solution)/shard_map/ppermute | solution.py:45
  43.1 0.0 collective-permute-done.21
  43.2 2.5 %collective-permute-start.22 = (f32[64,448]{1,0:T(8,128)S(1)}, f32[64,448]{1,0:T(8,128)S(1)}, u32[]{:S(2)}, u32[]{:S(2)}) collective-permute-start(f32[64,448]{1,0:T(8,128)S(1)} %add.96), channel_id=1, source_target_pairs={{1,17},{3,19},{5,21},{7,23},{9,25},{11,27},{13,29},{15,31},{17,1},... | collective-permute-start | bytes 344072 | tf_op jit(solution)/shard_map/ppermute | solution.py:45
  45.7 0.7 collective-permute-start.6
  46.4 0.0 collective-permute-done.7
  46.5 4.2 %collective-permute-start.9 = (f32[64,512]{1,0:T(8,128)S(1)}, f32[64,512]{1,0:T(8,128)S(1)}, u32[]{:S(2)}, u32[]{:S(2)}) collective-permute-start(f32[64,512]{1,0:T(8,128)S(1)} %add.84), channel_id=1, source_target_pairs={{1,25},{3,27},{5,29},{7,31},{9,17},{11,19},{13,21},{15,23},{17,9},... | collective-permute-start | bytes 393224 | tf_op jit(solution)/shard_map/ppermute | solution.py:45
  50.7 0.0 collective-permute-done.22
  50.7 2.3 %collective-permute-start.23 = (f32[64,448]{1,0:T(8,128)S(1)}, f32[64,448]{1,0:T(8,128)S(1)}, u32[]{:S(2)}, u32[]{:S(2)}) collective-permute-start(f32[64,448]{1,0:T(8,128)S(1)} %add.97), channel_id=1, source_target_pairs={{1,25},{3,27},{5,29},{7,31},{9,17},{11,19},{13,21},{15,23},{17,9},... | collective-permute-start | bytes 344072 | tf_op jit(solution)/shard_map/ppermute | solution.py:45
  53.0 0.7 collective-permute-start.8
  53.7 0.0 collective-permute-done.9
  53.8 5.0 %collective-permute-start.11 = (f32[64,512]{1,0:T(8,128)S(1)}, f32[64,512]{1,0:T(8,128)S(1)}, u32[]{:S(2)}, u32[]{:S(2)}) collective-permute-start(f32[64,512]{1,0:T(8,128)S(1)} %add.86), channel_id=1, source_target_pairs={{1,225},{3,227},{5,229},{7,231},{9,233},{11,235},{13,237},{15,239}... | collective-permute-start | bytes 393224 | tf_op jit(solution)/shard_map/ppermute | solution.py:45
  58.8 0.0 collective-permute-done.23
  58.8 2.2 %collective-permute-start.24 = (f32[64,448]{1,0:T(8,128)S(1)}, f32[64,448]{1,0:T(8,128)S(1)}, u32[]{:S(2)}, u32[]{:S(2)}) collective-permute-start(f32[64,448]{1,0:T(8,128)S(1)} %add.98), channel_id=1, source_target_pairs={{1,3},{3,1},{5,7},{7,5},{9,11},{11,9},{13,15},{15,13},{17,19},{19,... | collective-permute-start | bytes 344072 | tf_op jit(solution)/shard_map/ppermute | solution.py:45
  61.0 0.7 collective-permute-start.10
  61.6 0.0 collective-permute-done.10
  61.7 0.8 collective-permute-done.11
  62.5 2.2 %collective-permute-start.13 = (f32[64,512]{1,0:T(8,128)S(1)}, f32[64,512]{1,0:T(8,128)S(1)}, u32[]{:S(2)}, u32[]{:S(2)}) collective-permute-start(f32[64,512]{1,0:T(8,128)S(1)} %add.88), channel_id=1, source_target_pairs={{1,33},{3,35},{5,37},{7,39},{9,41},{11,43},{13,45},{15,47},{17,49}... | collective-permute-start | bytes 393224 | tf_op jit(solution)/shard_map/ppermute | solution.py:45
  64.8 4.2 %collective-permute-start.25 = (f32[64,448]{1,0:T(8,128)S(1)}, f32[64,448]{1,0:T(8,128)S(1)}, u32[]{:S(2)}, u32[]{:S(2)}) collective-permute-start(f32[64,448]{1,0:T(8,128)S(1)} %add.99), channel_id=1, source_target_pairs={{1,7},{3,5},{5,3},{7,1},{9,15},{11,13},{13,11},{15,9},{17,23},{19,... | collective-permute-start | bytes 344072 | tf_op jit(solution)/shard_map/ppermute | solution.py:45
  69.0 0.7 collective-permute-start.12
  69.6 0.0 collective-permute-done.12
  69.7 0.0 collective-permute-done.13
  69.7 3.1 %collective-permute-start.15 = (f32[64,512]{1,0:T(8,128)S(1)}, f32[64,512]{1,0:T(8,128)S(1)}, u32[]{:S(2)}, u32[]{:S(2)}) collective-permute-start(f32[64,512]{1,0:T(8,128)S(1)} %add.90), channel_id=1, source_target_pairs={{1,65},{3,67},{5,69},{7,71},{9,73},{11,75},{13,77},{15,79},{17,81}... | collective-permute-start | bytes 393224 | tf_op jit(solution)/shard_map/ppermute | solution.py:45
  72.8 1.3 %collective-permute-start.26 = (f32[64,448]{1,0:T(8,128)S(1)}, f32[64,448]{1,0:T(8,128)S(1)}, u32[]{:S(2)}, u32[]{:S(2)}) collective-permute-start(f32[64,448]{1,0:T(8,128)S(1)} %add.100), channel_id=1, source_target_pairs={{1,0},{3,2},{5,4},{7,6},{9,8},{11,10},{13,12},{15,14},{17,16},{19,... | collective-permute-start | bytes 344072 | tf_op jit(solution)/shard_map/ppermute | solution.py:48
  74.1 0.7 collective-permute-start.14
  74.8 2.9 %collective-permute-done.15 = f32[64,512]{1,0:T(8,128)S(1)} collective-permute-done((f32[64,512]{1,0:T(8,128)S(1)}, f32[64,512]{1,0:T(8,128)S(1)}, u32[]{:S(2)}, u32[]{:S(2)}) %collective-permute-start.15) | collective-permute-done | bytes 131104 | tf_op jit(solution)/shard_map/ppermute | solution.py:45
  77.7 1.3 %collective-permute-start.16 = (f32[32,128]{1,0:T(8,128)S(1)}, f32[32,128]{1,0:T(8,128)S(1)}, u32[]{:S(2)}, u32[]{:S(2)}) collective-permute-start(f32[32,128]{1,0:T(8,128)S(1)} %add.91), channel_id=1, source_target_pairs={{0,1},{2,3},{4,5},{6,7},{8,9},{10,11},{12,13},{14,15},{16,17},{18,... | collective-permute-start | bytes 49160 | tf_op jit(solution)/shard_map/ppermute | solution.py:48
  79.1 4.3 %collective-permute-start.17 = (f32[64,512]{1,0:T(8,128)S(1)}, f32[64,512]{1,0:T(8,128)S(1)}, u32[]{:S(2)}, u32[]{:S(2)}) collective-permute-start(f32[64,512]{1,0:T(8,128)S(1)} %add.92), channel_id=1, source_target_pairs={{1,0},{3,2},{5,4},{7,6},{9,8},{11,10},{13,12},{15,14},{17,16},{19,... | collective-permute-start | bytes 393224 | tf_op jit(solution)/shard_map/ppermute | solution.py:48
  83.5 6.6 %factor.1 = (f32[64,64]{1,0:T(8,128)}, f32[64,64]{1,0:T(8,128)S(1)}, f32[64,2048]{1,0:T(8,128)}) custom-call(f32[32,128]{1,0:T(8,128)S(1)} %broadcast_select_fusion.2.gram_ref, f32[64,2048]{1,0:T(8,128)S(1)} %copy-done), custom_call_target="tpu_custom_call" | custom-call | tf_op jit(solution)/shard_map/factor/pallas_call | solution.py:152
  90.1 1.1 %fusion = f32[64,960]{1,0:T(8,128)} fusion(f32[64,64]{1,0:T(8,128)S(1)} %get-tuple-element.40, f32[64,448]{1,0:T(8,128)S(1)} %broadcast_select_fusion, f32[64,512]{1,0:T(8,128)S(1)} %broadcast_select_fusion.1), kind=kOutput, calls=%fused_computation | convolution fusion | flops 47247360 | bytes 507904 | tf_op jit(solution)/shard_map/dot_general | solution.py:174
  (38 shorter events, 0.4 us)
Async XLA Ops:
  0.6 82.8 %copy-start = (f32[64,2048]{1,0:T(8,128)S(1)}, f32[64,2048]{1,0:T(8,128)}, u32[]{:S(2)}) copy-start(f32[64,2048]{1,0:T(8,128)} %panel_ref.1) | copy-start | bytes 1572868
  8.0 5.6 %collective-permute-start.2 = (f32[64,512]{1,0:T(8,128)}, f32[64,512]{1,0:T(8,128)S(1)}, u32[]{:S(2)}, u32[]{:S(2)}) collective-permute-start(f32[64,512]{1,0:T(8,128)} %get-tuple-element.24), channel_id=1, source_target_pairs={{0,1},{2,3},{4,5},{6,7},{8,9},{10,11},{12,13},{14,15},{16,17},{18,... | collective-permute-start | bytes 393224 | tf_op jit(solution)/shard_map/ppermute | solution.py:43
  9.3 7.1 %collective-permute-start.18 = (f32[64,448]{1,0:T(8,128)}, f32[64,448]{1,0:T(8,128)S(1)}, u32[]{:S(2)}, u32[]{:S(2)}) collective-permute-start(f32[64,448]{1,0:T(8,128)} %get-tuple-element.42), channel_id=1, source_target_pairs={{0,1},{2,3},{4,5},{6,7},{8,9},{10,11},{12,13},{14,15},{16,17},{18,... | collective-permute-start | bytes 344072 | tf_op jit(solution)/shard_map/ppermute | solution.py:43
  14.5 15.0 %collective-permute-start.3 = (f32[64,512]{1,0:T(8,128)S(1)}, f32[64,512]{1,0:T(8,128)S(1)}, u32[]{:S(2)}, u32[]{:S(2)}) collective-permute-start(f32[64,512]{1,0:T(8,128)S(1)} %add.79), channel_id=1, source_target_pairs={{1,3},{3,1},{5,7},{7,5},{9,11},{11,9},{13,15},{15,13},{17,19},{19,... | collective-permute-start | bytes 393224 | tf_op jit(solution)/shard_map/ppermute | solution.py:45
  17.4 7.2 %collective-permute-start.19 = (f32[64,448]{1,0:T(8,128)S(1)}, f32[64,448]{1,0:T(8,128)S(1)}, u32[]{:S(2)}, u32[]{:S(2)}) collective-permute-start(f32[64,448]{1,0:T(8,128)S(1)} %add.93), channel_id=1, source_target_pairs={{1,33},{3,35},{5,37},{7,39},{9,41},{11,43},{13,45},{15,47},{17,49}... | collective-permute-start | bytes 344072 | tf_op jit(solution)/shard_map/ppermute | solution.py:45
  20.8 2.3 %collective-permute-start = (f32[32,128]{1,0:T(8,128)}, f32[32,128]{1,0:T(8,128)S(1)}, u32[]{:S(2)}, u32[]{:S(2)}) collective-permute-start(f32[32,128]{1,0:T(8,128)} %get-tuple-element.23), channel_id=1, source_target_pairs={{1,0},{3,2},{5,4},{7,6},{9,8},{11,10},{13,12},{15,14},{17,16},{19,... | collective-permute-start | bytes 49160 | tf_op jit(solution)/shard_map/ppermute | solution.py:43
  23.9 5.6 %collective-permute-start.1 = (f32[32,128]{1,0:T(8,128)S(1)}, f32[32,128]{1,0:T(8,128)S(1)}, u32[]{:S(2)}, u32[]{:S(2)}) collective-permute-start(f32[32,128]{1,0:T(8,128)S(1)} %add.77), channel_id=1, source_target_pairs={{0,2},{2,0},{4,6},{6,4},{8,10},{10,8},{12,14},{14,12},{16,18},{18,... | collective-permute-start | bytes 49160 | tf_op jit(solution)/shard_map/ppermute | solution.py:45
  24.6 8.7 %collective-permute-start.20 = (f32[64,448]{1,0:T(8,128)S(1)}, f32[64,448]{1,0:T(8,128)S(1)}, u32[]{:S(2)}, u32[]{:S(2)}) collective-permute-start(f32[64,448]{1,0:T(8,128)S(1)} %add.94), channel_id=1, source_target_pairs={{1,65},{3,67},{5,69},{7,71},{9,73},{11,75},{13,77},{15,79},{17,81}... | collective-permute-start | bytes 344072 | tf_op jit(solution)/shard_map/ppermute | solution.py:45
  29.5 10.3 %collective-permute-start.5 = (f32[64,512]{1,0:T(8,128)S(1)}, f32[64,512]{1,0:T(8,128)S(1)}, u32[]{:S(2)}, u32[]{:S(2)}) collective-permute-start(f32[64,512]{1,0:T(8,128)S(1)} %add.80), channel_id=1, source_target_pairs={{1,7},{3,5},{5,3},{7,1},{9,15},{11,13},{13,11},{15,9},{17,23},{19,... | collective-permute-start | bytes 393224 | tf_op jit(solution)/shard_map/ppermute | solution.py:45
  33.3 9.8 %collective-permute-start.21 = (f32[64,448]{1,0:T(8,128)S(1)}, f32[64,448]{1,0:T(8,128)S(1)}, u32[]{:S(2)}, u32[]{:S(2)}) collective-permute-start(f32[64,448]{1,0:T(8,128)S(1)} %add.95), channel_id=1, source_target_pairs={{1,225},{3,227},{5,229},{7,231},{9,233},{11,235},{13,237},{15,239}... | collective-permute-start | bytes 344072 | tf_op jit(solution)/shard_map/ppermute | solution.py:45
  39.2 0.7 collective-permute-start.4
  39.9 6.5 %collective-permute-start.7 = (f32[64,512]{1,0:T(8,128)S(1)}, f32[64,512]{1,0:T(8,128)S(1)}, u32[]{:S(2)}, u32[]{:S(2)}) collective-permute-start(f32[64,512]{1,0:T(8,128)S(1)} %add.82), channel_id=1, source_target_pairs={{1,17},{3,19},{5,21},{7,23},{9,25},{11,27},{13,29},{15,31},{17,1},... | collective-permute-start | bytes 393224 | tf_op jit(solution)/shard_map/ppermute | solution.py:45
  43.2 7.5 %collective-permute-start.22 = (f32[64,448]{1,0:T(8,128)S(1)}, f32[64,448]{1,0:T(8,128)S(1)}, u32[]{:S(2)}, u32[]{:S(2)}) collective-permute-start(f32[64,448]{1,0:T(8,128)S(1)} %add.96), channel_id=1, source_target_pairs={{1,17},{3,19},{5,21},{7,23},{9,25},{11,27},{13,29},{15,31},{17,1},... | collective-permute-start | bytes 344072 | tf_op jit(solution)/shard_map/ppermute | solution.py:45
  45.7 0.7 collective-permute-start.6
  46.5 7.3 %collective-permute-start.9 = (f32[64,512]{1,0:T(8,128)S(1)}, f32[64,512]{1,0:T(8,128)S(1)}, u32[]{:S(2)}, u32[]{:S(2)}) collective-permute-start(f32[64,512]{1,0:T(8,128)S(1)} %add.84), channel_id=1, source_target_pairs={{1,25},{3,27},{5,29},{7,31},{9,17},{11,19},{13,21},{15,23},{17,9},... | collective-permute-start | bytes 393224 | tf_op jit(solution)/shard_map/ppermute | solution.py:45
  50.7 8.1 %collective-permute-start.23 = (f32[64,448]{1,0:T(8,128)S(1)}, f32[64,448]{1,0:T(8,128)S(1)}, u32[]{:S(2)}, u32[]{:S(2)}) collective-permute-start(f32[64,448]{1,0:T(8,128)S(1)} %add.97), channel_id=1, source_target_pairs={{1,25},{3,27},{5,29},{7,31},{9,17},{11,19},{13,21},{15,23},{17,9},... | collective-permute-start | bytes 344072 | tf_op jit(solution)/shard_map/ppermute | solution.py:45
  53.0 0.7 collective-permute-start.8
  53.8 8.8 %collective-permute-start.11 = (f32[64,512]{1,0:T(8,128)S(1)}, f32[64,512]{1,0:T(8,128)S(1)}, u32[]{:S(2)}, u32[]{:S(2)}) collective-permute-start(f32[64,512]{1,0:T(8,128)S(1)} %add.86), channel_id=1, source_target_pairs={{1,225},{3,227},{5,229},{7,231},{9,233},{11,235},{13,237},{15,239}... | collective-permute-start | bytes 393224 | tf_op jit(solution)/shard_map/ppermute | solution.py:45
  58.8 5.9 %collective-permute-start.24 = (f32[64,448]{1,0:T(8,128)S(1)}, f32[64,448]{1,0:T(8,128)S(1)}, u32[]{:S(2)}, u32[]{:S(2)}) collective-permute-start(f32[64,448]{1,0:T(8,128)S(1)} %add.98), channel_id=1, source_target_pairs={{1,3},{3,1},{5,7},{7,5},{9,11},{11,9},{13,15},{15,13},{17,19},{19,... | collective-permute-start | bytes 344072 | tf_op jit(solution)/shard_map/ppermute | solution.py:45
  61.0 0.7 collective-permute-start.10
  62.5 7.1 %collective-permute-start.13 = (f32[64,512]{1,0:T(8,128)S(1)}, f32[64,512]{1,0:T(8,128)S(1)}, u32[]{:S(2)}, u32[]{:S(2)}) collective-permute-start(f32[64,512]{1,0:T(8,128)S(1)} %add.88), channel_id=1, source_target_pairs={{1,33},{3,35},{5,37},{7,39},{9,41},{11,43},{13,45},{15,47},{17,49}... | collective-permute-start | bytes 393224 | tf_op jit(solution)/shard_map/ppermute | solution.py:45
  64.8 8.0 %collective-permute-start.25 = (f32[64,448]{1,0:T(8,128)S(1)}, f32[64,448]{1,0:T(8,128)S(1)}, u32[]{:S(2)}, u32[]{:S(2)}) collective-permute-start(f32[64,448]{1,0:T(8,128)S(1)} %add.99), channel_id=1, source_target_pairs={{1,7},{3,5},{5,3},{7,1},{9,15},{11,13},{13,11},{15,9},{17,23},{19,... | collective-permute-start | bytes 344072 | tf_op jit(solution)/shard_map/ppermute | solution.py:45
  69.0 0.7 collective-permute-start.12
  69.7 8.0 %collective-permute-start.15 = (f32[64,512]{1,0:T(8,128)S(1)}, f32[64,512]{1,0:T(8,128)S(1)}, u32[]{:S(2)}, u32[]{:S(2)}) collective-permute-start(f32[64,512]{1,0:T(8,128)S(1)} %add.90), channel_id=1, source_target_pairs={{1,65},{3,67},{5,69},{7,71},{9,73},{11,75},{13,77},{15,79},{17,81}... | collective-permute-start | bytes 393224 | tf_op jit(solution)/shard_map/ppermute | solution.py:45
  72.8 6.2 %collective-permute-start.26 = (f32[64,448]{1,0:T(8,128)S(1)}, f32[64,448]{1,0:T(8,128)S(1)}, u32[]{:S(2)}, u32[]{:S(2)}) collective-permute-start(f32[64,448]{1,0:T(8,128)S(1)} %add.100), channel_id=1, source_target_pairs={{1,0},{3,2},{5,4},{7,6},{9,8},{11,10},{13,12},{15,14},{17,16},{19,... | collective-permute-start | bytes 344072 | tf_op jit(solution)/shard_map/ppermute | solution.py:48
  74.1 0.7 collective-permute-start.14
  77.7 5.7 %collective-permute-start.16 = (f32[32,128]{1,0:T(8,128)S(1)}, f32[32,128]{1,0:T(8,128)S(1)}, u32[]{:S(2)}, u32[]{:S(2)}) collective-permute-start(f32[32,128]{1,0:T(8,128)S(1)} %add.91), channel_id=1, source_target_pairs={{0,1},{2,3},{4,5},{6,7},{8,9},{10,11},{12,13},{14,15},{16,17},{18,... | collective-permute-start | bytes 49160 | tf_op jit(solution)/shard_map/ppermute | solution.py:48
  79.1 11.0 %collective-permute-start.17 = (f32[64,512]{1,0:T(8,128)S(1)}, f32[64,512]{1,0:T(8,128)S(1)}, u32[]{:S(2)}, u32[]{:S(2)}) collective-permute-start(f32[64,512]{1,0:T(8,128)S(1)} %add.92), channel_id=1, source_target_pairs={{1,0},{3,2},{5,4},{7,6},{9,8},{11,10},{13,12},{15,14},{17,16},{19,... | collective-permute-start | bytes 393224 | tf_op jit(solution)/shard_map/ppermute | solution.py:48

commit v2 on v1

v2 whole, which is shorter than its diff:
```python
import math

import jax
import jax.numpy as jnp
from jax import lax
from jax.experimental import pallas as pl
from jax.experimental.pallas import tpu as pltpu
from jax.sharding import Mesh
from jax.sharding import PartitionSpec as P

AXES = ("z", "y_lo", "y_hi", "x", "core")
SIZES = (8, 2, 2, 4, 2)
PLANE = AXES[1:]
LAST = (((1,), (1,)), ((), ()))
LANES = 128
MIB = 1 << 20
BLOCK = 8


def parts3(values):
    high = values.astype(jnp.bfloat16)
    rest = values - high.astype(jnp.float32)
    middle = rest.astype(jnp.bfloat16)
    return high, middle, (rest - middle.astype(jnp.float32)).astype(jnp.bfloat16)


def last_product(left, right):
    return lax.dot_general(left, right, LAST, preferred_element_type=jnp.float32)


def local_products(panel, following):
    width, cells = panel.shape
    count = following.shape[0]
    columns = count + width
    pieces = 4
    piece = cells // pieces

    def kernel(panel_hbm, following_hbm, out_ref, panel_v, following_v, stack, total, sem):
        panel_copy = pltpu.make_async_copy(panel_hbm, panel_v, sem.at[0])
        panel_copy.start()
        copies = []
        for i in range(pieces):
            cut = pl.ds(i * piece, piece)
            copies.append(pltpu.make_async_copy(following_hbm.at[:, cut], following_v.at[:, cut], sem.at[1 + i]))
            copies[-1].start()
        panel_copy.wait()
        high, middle, low = parts3(panel_v[...])
        stack[0:width] = high
        stack[width : 2 * width] = middle
        stack[2 * width :] = low
        whole = stack[...]
        sums = last_product(whole, high) + last_product(whole, middle) + last_product(whole, low)
        gram = sums[:width] + sums[width : 2 * width] + sums[2 * width :]
        for i in range(pieces):
            copies[i].wait()
            cut = slice(i * piece, (i + 1) * piece)
            values = following_v[:, cut]
            high = values.astype(jnp.bfloat16)
            low = (values - high.astype(jnp.float32)).astype(jnp.bfloat16)
            part = stack[:, cut]
            sums = last_product(part, high) + last_product(part, low)
            if i:
                total[...] += sums
            else:
                total[...] = sums
        cross = total[:width] + total[width : 2 * width] + total[2 * width :]
        both = jnp.concatenate([cross, gram], axis=1)
        for j in range(columns // LANES):
            out_ref[j * width : (j + 1) * width] = both[:, j * LANES : (j + 1) * LANES]

    return pl.pallas_call(
        kernel,
        out_shape=jax.ShapeDtypeStruct((width * columns // LANES, LANES), jnp.float32),
        in_specs=[pl.BlockSpec(memory_space=pl.ANY)] * 2,
        out_specs=pl.BlockSpec(memory_space=pltpu.VMEM),
        scratch_shapes=[
            pltpu.VMEM((width, cells), jnp.float32),
            pltpu.VMEM((count, cells), jnp.float32),
            pltpu.VMEM((3 * width, cells), jnp.bfloat16),
            pltpu.VMEM((3 * width, count), jnp.float32),
            pltpu.SemaphoreType.DMA((1 + pieces,)),
        ],
        compiler_params=pltpu.CompilerParams(vmem_limit_bytes=60 * MIB),
        name="local_products",
    )(panel, following)


def eliminated(work, width):
    done = []
    for base in range(0, width, BLOCK):
        left = width - base
        columns = [jnp.broadcast_to(work[:, base + j : base + j + 1], (left, 2 * width)) for j in range(BLOCK)]
        rows = [work[j : j + 1] for j in range(BLOCK)]
        corner = [[columns[j][i : i + 1] for j in range(BLOCK)] for i in range(BLOCK)]
        inverses = []
        for j in range(BLOCK):
            inverses.append(1.0 / corner[j][j])
            for i in range(j + 1, BLOCK):
                factor = corner[i][j] * inverses[j]
                rows[i] = rows[i] - factor * rows[j]
                for k in range(j + 1, BLOCK):
                    corner[i][k] = corner[i][k] - factor * corner[j][k]
        if left > BLOCK:
            below = [column[BLOCK:] for column in columns]
            work = work[BLOCK:]
            for j in range(BLOCK):
                work = work - below[j] * (rows[j] * inverses[j])
                for k in range(j + 1, BLOCK):
                    below[k] = below[k] - below[j] * (corner[j][k] * inverses[j])
        done += [rows[j] / jnp.sqrt(corner[j][j]) for j in range(BLOCK)]
    return jnp.concatenate(done, axis=0)


def results(summed, panel, root_rows):
    width, cells = panel.shape
    count = summed.shape[0] * LANES // width - width

    def kernel(summed_ref, panel_ref, basis_ref, upper_ref, projection_ref):
        rows = lax.broadcasted_iota(jnp.int32, (width, 2 * width), 0)
        lanes = lax.broadcasted_iota(jnp.int32, (width, 2 * width), 1)
        gram_last = summed_ref[summed_ref.shape[0] - width :]
        unit = jnp.where(lanes == rows + width, 1.0, 0.0)
        work = eliminated(jnp.where(lanes < width, pltpu.roll(gram_last, width, axis=1), unit), width)
        upper_ref[...] = jnp.where(rows <= lanes, work, 0.0)[:, :width] * (1.0 / root_rows)
        high, middle, low = parts3(work[:, width:])
        inverse = jnp.concatenate([high, high, high, middle, middle, low], axis=1)

        def solved(values):
            high, middle, low = parts3(values)
            stacked = jnp.concatenate([high, middle, low, high, middle, high], axis=0)
            return jnp.dot(inverse, stacked, preferred_element_type=jnp.float32)

        basis_ref[...] = solved(panel_ref[...]) * root_rows
        for j in range(0, count, LANES):
            size = min(LANES, count - j)
            start = j // LANES * width
            block = solved(summed_ref[start : start + width]) * (1.0 / root_rows)
            projection_ref[:, j : j + size] = block[:, :size]

    return pl.pallas_call(
        kernel,
        out_shape=(
            jax.ShapeDtypeStruct((width, cells), jnp.float32),
            jax.ShapeDtypeStruct((width, width), jnp.float32),
            jax.ShapeDtypeStruct((width, count), jnp.float32),
        ),
        compiler_params=pltpu.CompilerParams(vmem_limit_bytes=32 * MIB),
        name="results",
    )(summed, panel)


def spread(block, axes):
    copies = jnp.broadcast_to(block[None], (lax.axis_size(axes), *block.shape))
    return lax.all_to_all(copies, axes, 0, 0)


def body(snapshot_panel, following):
    root_rows = math.sqrt(snapshot_panel.shape[1] * lax.axis_size(AXES))
    products = local_products(snapshot_panel, following)
    chunks = products.reshape(lax.axis_size(PLANE), -1, LANES)
    mine = lax.all_to_all(chunks, PLANE, 0, 0).sum(axis=0)
    mine = spread(mine, "z").sum(axis=0)
    summed = spread(mine, PLANE).reshape(products.shape)
    return results(summed, snapshot_panel, root_rows)


def solution(mesh):
    mesh = Mesh(mesh.devices.reshape(SIZES), AXES)
    return jax.shard_map(
        body,
        mesh=mesh,
        in_specs=(P(None, AXES), P(None, AXES)),
        out_specs=(P(None, AXES), P(), P()),
        check_vma=False,
    )
```

time: 91.9 us -> 57.8 us (0.63)
  starting transfers between devices: 64.2 us -> 0 us
  blocking collectives: 0 us -> 46.5 us
  waiting for transfers between devices: 7.81 us -> 0 us
  Pallas kernels: 14 us -> 10.3 us
  other arithmetic: 2.95 us -> 0.05 us
  matrix products: 1.06 us -> 0 us
    ppermute x27 -> x0, starting transfers between devices: 64.2 us -> none  [the longest x21 53.4 us: summed(): lax.ppermute(b, AXES, route(f, c))]
    all_to_all x0 -> x3, blocking collectives: none -> 46.5 us  [the longest x2 28.9 us: spread(): return lax.all_to_all(copies, axes, 0, 0)]
    ppermute x27 -> x0, waiting for transfers between devices: 7.81 us -> none  [the longest x3 4 us: summed(): lax.ppermute(b, AXES, route(core_flip, 1 - c))]
    pallas_call x2, Pallas kernels: 14 us -> 10.3 us  [the longest x1 7.33 us: local_products(): pl.pallas_call(kernel, out_shape=jax.ShapeDtypeStruct((width * columns //...]
    add x24 -> x0, other arithmetic: 2.9 us -> none  [the longest x3 2.58 us: summed(): b + lax.ppermute(b, AXES, route(core_flip, 1 - c))]
    dot_general x1 -> x0, matrix products: 1.06 us -> none  [body(): jnp.dot(inverse, cross, precision=lax.Precision.HIGHEST, preferred_elemen...]
  transfers between devices with their start and end apart: 27 -> 0, of which waited for: 4 -> 0; matrix products, arithmetic and copies ran while one was open for 3% -> 0% of each run, Pallas kernels for 7% -> 0%
where the time goes in v2:
time: 57.8 us; the launch traced here: 57.6 us
  blocking collectives  46.5 us (80%)
  Pallas kernels  10.3 us (18%)
  between operations  0.67 us (1%)
    all_to_all x2, blocking collectives, spread(): return lax.all_to_all(copies, axes, 0, 0)  28.9 us
    all_to_all x1, blocking collectives, body(): mine = lax.all_to_all(chunks, PLANE, 0, 0).sum(axis=0)  17.7 us
    pallas_call x1, Pallas kernels, local_products(): pl.pallas_call(kernel, out_shape=jax.ShapeDtypeStruct((width * columns //...  7.33 us
    pallas_call x1, Pallas kernels, results(): pl.pallas_call(kernel, out_shape=(jax.ShapeDtypeStruct((width, cells), jn...  2.97 us

profile of v2, /device:TPU:1, one launch (start us, length us, event | category | flops | bytes accessed | tf_op | source)
XLA Modules:
  0.0 57.6 jit_solution(4425090649374992496)
XLA Ops:
  0.6 0.0 copy-start
  0.6 7.3 %local_products.1 = f32[512,128]{1,0:T(8,128)} custom-call(f32[64,2048]{1,0:T(8,128)} %panel_ref.1, f32[960,2048]{1,0:T(8,128)} %following_hbm.1), custom_call_target="tpu_custom_call" | custom-call | tf_op jit(solution)/shard_map/local_products/pallas_call | solution.py:71
  8.0 17.7 %all_to_all.15 = f32[32,16,128]{2,1,0:T(8,128)S(1)} all-to-all(f32[32,16,128]{2,1,0:T(8,128)} %bitcast.3), channel_id=1, replica_groups=mesh['z'=8,'y_lo'=2,'y_hi'=2,'x'=4,'core'=2] {'y_lo','y_hi','x','core'}, dimensions={0} | all-to-all | bytes 524288 | tf_op jit(solution)/shard_map/all_to_all | solution.py:161
  25.7 15.1 %all_to_all.16 = f32[8,16,128]{2,1,0:T(8,128)S(1)} all-to-all(f32[8,16,128]{2,1,0:T(8,128)S(1)} %broadcast_in_dim.4), channel_id=1, replica_groups=mesh['z'=8,'y_lo'=2,'y_hi'=2,'x'=4,'core'=2] {'z'}, dimensions={0} | all-to-all | bytes 131072 | tf_op jit(solution)/shard_map/all_to_all | solution.py:154
  40.9 13.7 %all_to_all.17 = f32[32,16,128]{2,1,0:T(8,128)S(1)} all-to-all(f32[32,16,128]{2,1,0:T(8,128)S(1)} %broadcast_in_dim.5), channel_id=1, replica_groups=mesh['z'=8,'y_lo'=2,'y_hi'=2,'x'=4,'core'=2] {'y_lo','y_hi','x','core'}, dimensions={0} | all-to-all | bytes 524288 | tf_op jit(solution)/shard_map/all_to_all | solution.py:154
  54.6 0.0 copy-done
  54.6 3.0 %results.1 = (f32[64,2048]{1,0:T(8,128)}, f32[64,64]{1,0:T(8,128)}, f32[64,960]{1,0:T(8,128)}) custom-call(f32[512,128]{1,0:T(8,128)S(1)} %bitcast.2, f32[64,2048]{1,0:T(8,128)S(1)} %copy-done), custom_call_target="tpu_custom_call" | custom-call | tf_op jit(solution)/shard_map/results/pallas_call | solution.py:140
  (4 shorter events, 0.1 us)
Async XLA Ops:
  0.6 54.0 %copy-start = (f32[64,2048]{1,0:T(8,128)S(1)}, f32[64,2048]{1,0:T(8,128)}, u32[]{:S(2)}) copy-start(f32[64,2048]{1,0:T(8,128)} %panel_ref.1) | copy-start | bytes 1572868

commit v3 on v2

v3 whole, which is shorter than its diff:
```python
import math

import jax
import jax.numpy as jnp
import numpy as np
from jax import lax
from jax.experimental import pallas as pl
from jax.experimental.pallas import tpu as pltpu
from jax.sharding import Mesh
from jax.sharding import PartitionSpec as P

AXES = ("z", "y_lo", "y_hi", "x", "core")
SIZES = (8, 2, 2, 4, 2)
PLANE = AXES[1:]
LAST = (((1,), (1,)), ((), ()))
LANES = 128
MIB = 1 << 20
BLOCK = 8


def parts3(values):
    high = values.astype(jnp.bfloat16)
    rest = values - high.astype(jnp.float32)
    middle = rest.astype(jnp.bfloat16)
    return high, middle, (rest - middle.astype(jnp.float32)).astype(jnp.bfloat16)


def last_product(left, right):
    return lax.dot_general(left, right, LAST, preferred_element_type=jnp.float32)


def local_products(panel, following):
    width, cells = panel.shape
    count = following.shape[0]
    columns = count + width
    pieces = 4
    piece = cells // pieces

    def kernel(panel_hbm, following_hbm, out_ref, panel_v, following_v, stack, total, sem):
        def copy(i):
            cut = pl.ds(pl.multiple_of(i * piece, LANES), piece)
            return pltpu.make_async_copy(following_hbm.at[:, cut], following_v.at[i], sem.at[1 + i])

        panel_copy = pltpu.make_async_copy(panel_hbm, panel_v, sem.at[0])
        panel_copy.start()
        copy(0).start()
        panel_copy.wait()
        for i in range(1, pieces):
            copy(i).start()
        high, middle, low = parts3(panel_v[...])
        for i in range(pieces):
            cut = slice(i * piece, (i + 1) * piece)
            stack[i, :width] = high[:, cut]
            stack[i, width:] = middle[:, cut]
        whole = jnp.concatenate([high, middle, low], axis=0)
        sums = last_product(whole, high) + last_product(whole, middle) + last_product(whole, low)
        total[:, :count] = jnp.zeros((width, count), jnp.float32)
        total[:, count:] = sums[:width] + sums[width : 2 * width] + sums[2 * width :]

        @pl.loop(0, pieces)
        def _(i):
            copy(i).wait()
            values = following_v[i]
            high = values.astype(jnp.bfloat16)
            low = (values - high.astype(jnp.float32)).astype(jnp.bfloat16)
            sums = last_product(stack[i], high)
            total[:, :count] += sums[:width] + sums[width:] + last_product(stack[i, :width], low)

        for j in range(columns // LANES):
            out_ref[j * width : (j + 1) * width] = total[:, j * LANES : (j + 1) * LANES]

    return pl.pallas_call(
        kernel,
        out_shape=jax.ShapeDtypeStruct((width * columns // LANES, LANES), jnp.float32),
        in_specs=[pl.BlockSpec(memory_space=pltpu.HBM)] * 2,
        out_specs=pl.BlockSpec(memory_space=pltpu.VMEM),
        scratch_shapes=[
            pltpu.VMEM((width, cells), jnp.float32),
            pltpu.VMEM((pieces, count, piece), jnp.float32),
            pltpu.VMEM((pieces, 2 * width, piece), jnp.bfloat16),
            pltpu.VMEM((width, columns), jnp.float32),
            pltpu.SemaphoreType.DMA((1 + pieces,)),
        ],
        compiler_params=pltpu.CompilerParams(vmem_limit_bytes=54656 * 1024),
        name="local_products",
    )(panel, following)


def eliminated(work, width):
    done = []
    for base in range(0, width, BLOCK):
        left = width - base
        columns = [jnp.broadcast_to(work[:, base + j : base + j + 1], (left, 2 * width)) for j in range(BLOCK)]
        rows = [work[j : j + 1] for j in range(BLOCK)]
        corner = [[columns[j][i : i + 1] for j in range(BLOCK)] for i in range(BLOCK)]
        inverses = []
        for j in range(BLOCK):
            inverses.append(1.0 / corner[j][j])
            for i in range(j + 1, BLOCK):
                factor = corner[i][j] * inverses[j]
                rows[i] = rows[i] - factor * rows[j]
                for k in range(j + 1, BLOCK):
                    corner[i][k] = corner[i][k] - factor * corner[j][k]
        if left > BLOCK:
            below = [column[BLOCK:] for column in columns]
            work = work[BLOCK:]
            for j in range(BLOCK):
                work = work - below[j] * (rows[j] * inverses[j])
                for k in range(j + 1, BLOCK):
                    below[k] = below[k] - below[j] * (corner[j][k] * inverses[j])
        done += [rows[j] / jnp.sqrt(corner[j][j]) for j in range(BLOCK)]
    return jnp.concatenate(done, axis=0)


def stacked_left(high, middle, low):
    return jnp.concatenate([high, high, high, middle, middle, low], axis=1)


def stacked_right(values):
    high, middle, low = parts3(values)
    return jnp.concatenate([high, middle, low, high, middle, high], axis=0)


def factored(gram, panel, root_rows):
    width, cells = panel.shape

    def kernel(gram_ref, panel_ref, basis_ref, upper_ref, inverse_ref):
        rows = lax.broadcasted_iota(jnp.int32, (width, 2 * width), 0)
        lanes = lax.broadcasted_iota(jnp.int32, (width, 2 * width), 1)
        unit = jnp.where(lanes == rows + width, 1.0, 0.0)
        work = eliminated(jnp.where(lanes < width, pltpu.roll(gram_ref[...], width, axis=1), unit), width)
        upper_ref[...] = jnp.where(rows <= lanes, work, 0.0)[:, :width] * (1.0 / root_rows)
        inverse = stacked_left(*parts3(work[:, width:]))
        inverse_ref[...] = inverse
        basis = jnp.dot(inverse, stacked_right(panel_ref[...]), preferred_element_type=jnp.float32)
        basis_ref[...] = basis * root_rows

    return pl.pallas_call(
        kernel,
        out_shape=(
            jax.ShapeDtypeStruct((width, cells), jnp.float32),
            jax.ShapeDtypeStruct((width, width), jnp.float32),
            jax.ShapeDtypeStruct((width, 6 * width), jnp.bfloat16),
        ),
        compiler_params=pltpu.CompilerParams(vmem_limit_bytes=32 * MIB),
        name="factored",
    )(gram, panel)


def projected(inverse, summed, root_rows):
    width = inverse.shape[0]
    count = summed.shape[0] * LANES // width - width

    def kernel(inverse_ref, summed_ref, out_ref):
        for j in range(0, count, LANES):
            size = min(LANES, count - j)
            start = j // LANES * width
            right = stacked_right(summed_ref[start : start + width])
            block = jnp.dot(inverse_ref[...], right, preferred_element_type=jnp.float32) * (1.0 / root_rows)
            out_ref[:, j : j + size] = block[:, :size]

    return pl.pallas_call(
        kernel,
        out_shape=jax.ShapeDtypeStruct((width, count), jnp.float32),
        compiler_params=pltpu.CompilerParams(vmem_limit_bytes=32 * MIB),
        name="projected",
    )(inverse, summed)


def half_of(z, y, x, core):
    return core ^ ((x + y + z) % 2)


def exchange(block, *flips):
    pairs = []
    for index, (z, y_lo, y_hi, x, core) in enumerate(np.ndindex(*SIZES)):
        y = 2 * y_hi + y_lo
        half = half_of(z, y, x, core)
        fz, fy, fx = flips[half]
        tz, ty, tx = z ^ fz, y ^ fy, x ^ fx
        tc = half_of(tz, ty, tx, half)
        pairs.append((index, int(np.ravel_multi_index((tz, ty % 2, ty // 2, tx, tc), SIZES))))
    return lax.ppermute(block, AXES, pairs)


def other_core(block):
    return lax.ppermute(block, AXES, [(i, i ^ 1) for i in range(math.prod(SIZES))])


X1, X3, Y1, Y3, Z1, Z2, Z7 = (0, 0, 1), (0, 0, 3), (0, 1, 0), (0, 3, 0), (1, 0, 0), (2, 0, 0), (7, 0, 0)

ROUNDS = [((X1, Z7),) * 2, ((X3, Z1),) * 2, ((Y1, Z2),) * 2, ((Y3, X1),) * 2, ((Z7, X3),) * 2, ((Z1, Y1),) * 2, ((Z2, Y3),) * 2]


def body(snapshot_panel, following):
    root_rows = math.sqrt(snapshot_panel.shape[1] * lax.axis_size(AXES))
    products = local_products(snapshot_panel, following)
    halves = products.reshape(2, 2, -1, LANES)
    place = (lax.axis_index("z"), 2 * lax.axis_index("y_hi") + lax.axis_index("y_lo"), lax.axis_index("x"))
    half = half_of(*place, lax.axis_index("core"))
    mine = lax.dynamic_index_in_dim(halves, half, keepdims=False)
    theirs = lax.dynamic_index_in_dim(halves, 1 - half, keepdims=False)
    one = mine[1] + other_core(theirs[1])
    two = mine[0] + other_core(theirs[0])
    for first, second in ROUNDS:
        one = one + exchange(one, *first)
        two = two + exchange(two, *second)

    def both(block):
        other = other_core(block)
        return jnp.where(half == 0, block, other), jnp.where(half == 0, other, block)

    first, last = both(one)
    basis, upper, inverse = factored(last[-snapshot_panel.shape[0] :], snapshot_panel, root_rows)
    low, high = both(two)
    projection = projected(inverse, jnp.concatenate([low, first, high, last]), root_rows)
    return basis, upper, projection


def solution(mesh):
    mesh = Mesh(mesh.devices.reshape(SIZES), AXES)
    return jax.shard_map(
        body,
        mesh=mesh,
        in_specs=(P(None, AXES), P(None, AXES)),
        out_specs=(P(None, AXES), P(), P()),
        check_vma=False,
    )
```

time: 57.8 us -> 53.2 us (0.920)
  blocking collectives: 46.5 us -> 0 us
  starting transfers between devices: 0 us -> 33.1 us
  waiting for transfers between devices: 0 us -> 10.1 us
  Pallas kernels: 10.3 us -> 8.94 us
    all_to_all x3 -> x0, blocking collectives: 46.5 us -> none  [the longest x2 28.9 us: spread(): return lax.all_to_all(copies, axes, 0, 0)]
    ppermute x0 -> x18, starting transfers between devices: none -> 33.1 us  [the longest x14 28.2 us: exchange(): return lax.ppermute(block, AXES, pairs)]
    ppermute x0 -> x18, waiting for transfers between devices: none -> 10.1 us  [the longest x14 8.94 us: exchange(): return lax.ppermute(block, AXES, pairs)]
    pallas_call x1, Pallas kernels: 7.33 us -> 5.06 us  [local_products(): pl.pallas_call(kernel, out_shape=jax.ShapeDtypeStruct((width * columns //...]
    pallas_call x1 -> x2, Pallas kernels: 2.97 us -> 3.88 us  [the longest x1 2.89 us: factored(): pl.pallas_call(kernel, out_shape=(jax.ShapeDtypeStruct((width, cells), jn...]
  transfers between devices with their start and end apart: 0 -> 18, of which waited for: 0 -> 8; matrix products, arithmetic and copies ran while one was open for 0% -> 0% of each run, Pallas kernels for 0% -> 5%
where the time goes in v3:
time: 53.2 us; the launch traced here: 53.1 us
  starting transfers between devices  33.1 us (62%)
  waiting for transfers between devices  10.1 us (19%)
  Pallas kernels  8.94 us (17%)
  between operations  0.79 us (1%)
    ppermute x14, starting transfers between devices, exchange(): return lax.ppermute(block, AXES, pairs)  28.2 us
    ppermute x14, waiting for transfers between devices, exchange(): return lax.ppermute(block, AXES, pairs)  8.94 us
    pallas_call x1, Pallas kernels, local_products(): pl.pallas_call(kernel, out_shape=jax.ShapeDtypeStruct((width * columns //...  5.06 us
    ppermute x4, starting transfers between devices, other_core(): lax.ppermute(block, AXES, [(i, i ^ 1) for i in range(math.prod(SIZES))])  4.93 us
    pallas_call x1, Pallas kernels, factored(): pl.pallas_call(kernel, out_shape=(jax.ShapeDtypeStruct((width, cells), jn...  2.89 us
    ppermute x4, waiting for transfers between devices, other_core(): lax.ppermute(block, AXES, [(i, i ^ 1) for i in range(math.prod(SIZES))])  1.16 us
  transfers between devices with their start and end apart: 18, of which 8 were waited for; matrix products, arithmetic and copies ran while one was open for 0% of the time, Pallas kernels for 5%

profile of v3, /device:TPU:1, one launch (start us, length us, event | category | flops | bytes accessed | tf_op | source)
XLA Modules:
  0.0 53.1 jit_solution(2772577796942258933)
XLA Ops:
  0.6 0.0 copy-start
  0.7 5.1 %local_products.1 = f32[512,128]{1,0:T(8,128)S(1)} custom-call(f32[64,2048]{1,0:T(8,128)} %panel_ref.1, f32[960,2048]{1,0:T(8,128)} %following_hbm.1), custom_call_target="tpu_custom_call" | custom-call | tf_op jit(solution)/shard_map/local_products/pallas_call | solution.py:72
  5.8 3.3 %collective-permute-start.9 = (f32[128,128]{1,0:T(8,128)S(1)}, f32[128,128]{1,0:T(8,128)S(1)}, u32[]{:S(2)}, u32[]{:S(2)}) collective-permute-start(f32[128,128]{1,0:T(8,128)S(1)} %get-tuple-element.11), channel_id=1, source_target_pairs={{0,1},{1,0},{2,3},{3,2},{4,5},{5,4},{6,7},{7,6},{8,9},{9,8},{10,11... | collective-permute-start | bytes 196616 | tf_op jit(solution)/shard_map/ppermute | solution.py:187
  9.1 0.1 collective-permute-start
  9.2 0.8 %collective-permute-done.9 = f32[128,128]{1,0:T(8,128)S(1)} collective-permute-done((f32[128,128]{1,0:T(8,128)S(1)}, f32[128,128]{1,0:T(8,128)S(1)}, u32[]{:S(2)}, u32[]{:S(2)}) %collective-permute-start.9) | collective-permute-done | bytes 65568 | tf_op jit(solution)/shard_map/ppermute | solution.py:187
  10.0 0.4 collective-permute-done
  10.4 4.0 %collective-permute-start.1 = (f32[128,128]{1,0:T(8,128)S(1)}, f32[128,128]{1,0:T(8,128)S(1)}, u32[]{:S(2)}, u32[]{:S(2)}) collective-permute-start(f32[128,128]{1,0:T(8,128)S(1)} %get-tuple-element.10), channel_id=1, source_target_pairs={{0,3},{1,224},{2,227},{3,0},{4,7},{5,228},{6,231},{7,4},{8,11},{9,... | collective-permute-start | bytes 196616 | tf_op jit(solution)/shard_map/ppermute | solution.py:183
  14.3 0.1 collective-permute-start.10
  14.4 2.6 %collective-permute-done.1 = f32[128,128]{1,0:T(8,128)S(1)} collective-permute-done((f32[128,128]{1,0:T(8,128)S(1)}, f32[128,128]{1,0:T(8,128)S(1)}, u32[]{:S(2)}, u32[]{:S(2)}) %collective-permute-start.1) | collective-permute-done | bytes 65568 | tf_op jit(solution)/shard_map/ppermute | solution.py:183
  17.0 1.4 %collective-permute-start.2 = (f32[128,128]{1,0:T(8,128)S(1)}, f32[128,128]{1,0:T(8,128)S(1)}, u32[]{:S(2)}, u32[]{:S(2)}) collective-permute-start(f32[128,128]{1,0:T(8,128)S(1)} %add.76), channel_id=1, source_target_pairs={{0,7},{1,32},{2,35},{3,4},{4,3},{5,36},{6,39},{7,0},{8,15},{9,40},... | collective-permute-start | bytes 196616 | tf_op jit(solution)/shard_map/ppermute | solution.py:183
  18.4 1.2 %collective-permute-done.10 = f32[128,128]{1,0:T(8,128)S(1)} collective-permute-done((f32[128,128]{1,0:T(8,128)S(1)}, f32[128,128]{1,0:T(8,128)S(1)}, u32[]{:S(2)}, u32[]{:S(2)}) %collective-permute-start.10) | collective-permute-done | bytes 65568 | tf_op jit(solution)/shard_map/ppermute | solution.py:183
  19.5 3.5 %collective-permute-start.11 = (f32[128,128]{1,0:T(8,128)S(1)}, f32[128,128]{1,0:T(8,128)S(1)}, u32[]{:S(2)}, u32[]{:S(2)}) collective-permute-start(f32[128,128]{1,0:T(8,128)S(1)} %add.84), channel_id=1, source_target_pairs={{0,7},{1,32},{2,35},{3,4},{4,3},{5,36},{6,39},{7,0},{8,15},{9,40},... | collective-permute-start | bytes 196616 | tf_op jit(solution)/shard_map/ppermute | solution.py:183
  23.0 0.0 collective-permute-done.2
  23.0 0.3 collective-permute-start.3
  23.3 1.6 %collective-permute-done.11 = f32[128,128]{1,0:T(8,128)S(1)} collective-permute-done((f32[128,128]{1,0:T(8,128)S(1)}, f32[128,128]{1,0:T(8,128)S(1)}, u32[]{:S(2)}, u32[]{:S(2)}) %collective-permute-start.11) | collective-permute-done | bytes 65568 | tf_op jit(solution)/shard_map/ppermute | solution.py:183
  25.0 2.0 %collective-permute-start.12 = (f32[128,128]{1,0:T(8,128)S(1)}, f32[128,128]{1,0:T(8,128)S(1)}, u32[]{:S(2)}, u32[]{:S(2)}) collective-permute-start(f32[128,128]{1,0:T(8,128)S(1)} %add.85), channel_id=1, source_target_pairs={{0,17},{1,65},{2,66},{3,18},{4,21},{5,69},{6,70},{7,22},{8,25},{9,... | collective-permute-start | bytes 196616 | tf_op jit(solution)/shard_map/ppermute | solution.py:183
  27.0 0.8 %collective-permute-done.3 = f32[128,128]{1,0:T(8,128)S(1)} collective-permute-done((f32[128,128]{1,0:T(8,128)S(1)}, f32[128,128]{1,0:T(8,128)S(1)}, u32[]{:S(2)}, u32[]{:S(2)}) %collective-permute-start.3) | collective-permute-done | bytes 65568 | tf_op jit(solution)/shard_map/ppermute | solution.py:183
  27.8 1.8 %collective-permute-start.4 = (f32[128,128]{1,0:T(8,128)S(1)}, f32[128,128]{1,0:T(8,128)S(1)}, u32[]{:S(2)}, u32[]{:S(2)}) collective-permute-start(f32[128,128]{1,0:T(8,128)S(1)} %add.78), channel_id=1, source_target_pairs={{0,25},{1,2},{2,1},{3,26},{4,29},{5,6},{6,5},{7,30},{8,17},{9,10},... | collective-permute-start | bytes 196616 | tf_op jit(solution)/shard_map/ppermute | solution.py:183
  29.6 0.0 collective-permute-done.12
  29.6 1.9 %collective-permute-start.13 = (f32[128,128]{1,0:T(8,128)S(1)}, f32[128,128]{1,0:T(8,128)S(1)}, u32[]{:S(2)}, u32[]{:S(2)}) collective-permute-start(f32[128,128]{1,0:T(8,128)S(1)} %add.86), channel_id=1, source_target_pairs={{0,25},{1,2},{2,1},{3,26},{4,29},{5,6},{6,5},{7,30},{8,17},{9,10},... | collective-permute-start | bytes 196616 | tf_op jit(solution)/shard_map/ppermute | solution.py:183
  31.6 0.0 collective-permute-done.4
  31.6 3.1 %collective-permute-start.5 = (f32[128,128]{1,0:T(8,128)S(1)}, f32[128,128]{1,0:T(8,128)S(1)}, u32[]{:S(2)}, u32[]{:S(2)}) collective-permute-start(f32[128,128]{1,0:T(8,128)S(1)} %add.79), channel_id=1, source_target_pairs={{0,225},{1,6},{2,5},{3,226},{4,229},{5,2},{6,1},{7,230},{8,233},{9... | collective-permute-start | bytes 196616 | tf_op jit(solution)/shard_map/ppermute | solution.py:183
  34.7 0.0 collective-permute-done.13
  34.7 1.9 %collective-permute-start.14 = (f32[128,128]{1,0:T(8,128)S(1)}, f32[128,128]{1,0:T(8,128)S(1)}, u32[]{:S(2)}, u32[]{:S(2)}) collective-permute-start(f32[128,128]{1,0:T(8,128)S(1)} %add.87), channel_id=1, source_target_pairs={{0,225},{1,6},{2,5},{3,226},{4,229},{5,2},{6,1},{7,230},{8,233},{9... | collective-permute-start | bytes 196616 | tf_op jit(solution)/shard_map/ppermute | solution.py:183
  36.6 0.0 collective-permute-done.5
  36.7 1.8 %collective-permute-start.6 = (f32[128,128]{1,0:T(8,128)S(1)}, f32[128,128]{1,0:T(8,128)S(1)}, u32[]{:S(2)}, u32[]{:S(2)}) collective-permute-start(f32[128,128]{1,0:T(8,128)S(1)} %add.80), channel_id=1, source_target_pairs={{0,33},{1,16},{2,19},{3,34},{4,37},{5,20},{6,23},{7,38},{8,41},{9,... | collective-permute-start | bytes 196616 | tf_op jit(solution)/shard_map/ppermute | solution.py:183
  38.5 1.2 %collective-permute-done.14 = f32[128,128]{1,0:T(8,128)S(1)} collective-permute-done((f32[128,128]{1,0:T(8,128)S(1)}, f32[128,128]{1,0:T(8,128)S(1)}, u32[]{:S(2)}, u32[]{:S(2)}) %collective-permute-start.14) | collective-permute-done | bytes 65568 | tf_op jit(solution)/shard_map/ppermute | solution.py:183
  39.7 1.2 %collective-permute-start.15 = (f32[128,128]{1,0:T(8,128)S(1)}, f32[128,128]{1,0:T(8,128)S(1)}, u32[]{:S(2)}, u32[]{:S(2)}) collective-permute-start(f32[128,128]{1,0:T(8,128)S(1)} %add.88), channel_id=1, source_target_pairs={{0,33},{1,16},{2,19},{3,34},{4,37},{5,20},{6,23},{7,38},{8,41},{9,... | collective-permute-start | bytes 196616 | tf_op jit(solution)/shard_map/ppermute | solution.py:183
  40.9 0.0 collective-permute-done.6
  40.9 2.8 %collective-permute-start.7 = (f32[128,128]{1,0:T(8,128)S(1)}, f32[128,128]{1,0:T(8,128)S(1)}, u32[]{:S(2)}, u32[]{:S(2)}) collective-permute-start(f32[128,128]{1,0:T(8,128)S(1)} %add.81), channel_id=1, source_target_pairs={{0,64},{1,24},{2,27},{3,67},{4,68},{5,28},{6,31},{7,71},{8,72},{9,... | collective-permute-start | bytes 196616 | tf_op jit(solution)/shard_map/ppermute | solution.py:183
  43.7 0.0 collective-permute-done.15
  43.7 2.4 %collective-permute-start.16 = (f32[128,128]{1,0:T(8,128)S(1)}, f32[128,128]{1,0:T(8,128)S(1)}, u32[]{:S(2)}, u32[]{:S(2)}) collective-permute-start(f32[128,128]{1,0:T(8,128)S(1)} %add.89), channel_id=1, source_target_pairs={{0,64},{1,24},{2,27},{3,67},{4,68},{5,28},{6,31},{7,71},{8,72},{9,... | collective-permute-start | bytes 196616 | tf_op jit(solution)/shard_map/ppermute | solution.py:183
  46.1 0.0 collective-permute-done.7
  46.1 1.1 %collective-permute-start.8 = (f32[128,128]{1,0:T(8,128)S(1)}, f32[128,128]{1,0:T(8,128)S(1)}, u32[]{:S(2)}, u32[]{:S(2)}) collective-permute-start(f32[128,128]{1,0:T(8,128)S(1)} %add.82), channel_id=1, source_target_pairs={{0,1},{1,0},{2,3},{3,2},{4,5},{5,4},{6,7},{7,6},{8,9},{9,8},{10,11... | collective-permute-start | bytes 196616 | tf_op jit(solution)/shard_map/ppermute | solution.py:187
  47.2 1.5 %collective-permute-done.16 = f32[128,128]{1,0:T(8,128)S(1)} collective-permute-done((f32[128,128]{1,0:T(8,128)S(1)}, f32[128,128]{1,0:T(8,128)S(1)}, u32[]{:S(2)}, u32[]{:S(2)}) %collective-permute-start.16) | collective-permute-done | bytes 65568 | tf_op jit(solution)/shard_map/ppermute | solution.py:183
  48.7 0.4 collective-permute-start.17
  49.2 0.0 collective-permute-done.8
  49.2 0.0 copy-done
  49.2 2.9 %factored.1 = (f32[64,2048]{1,0:T(8,128)}, f32[64,64]{1,0:T(8,128)}, bf16[64,384]{1,0:T(8,128)(2,1)S(1)}) custom-call(f32[64,128]{1,0:T(8,128)S(1)} %slice.24.gram_ref, f32[64,2048]{1,0:T(8,128)S(1)} %copy-done), custom_call_target="tpu_custom_call" | custom-call | tf_op jit(solution)/shard_map/factored/pallas_call | solution.py:138
  52.1 0.0 collective-permute-done.17
  52.1 1.0 %projected.1 = f32[64,960]{1,0:T(8,128)} custom-call(bf16[64,384]{1,0:T(8,128)(2,1)S(1)} %get-tuple-element.8.inverse_ref, f32[512,128]{1,0:T(8,128)S(1)} %pad_maximum_fusion.summed_ref), custom_call_target="tpu_custom_call" | custom-call | tf_op jit(solution)/shard_map/projected/pallas_call | solution.py:162
  (20 shorter events, 0.2 us)
Async XLA Ops:
  0.6 48.6 %copy-start = (f32[64,2048]{1,0:T(8,128)S(1)}, f32[64,2048]{1,0:T(8,128)}, u32[]{:S(2)}) copy-start(f32[64,2048]{1,0:T(8,128)} %panel_ref.1) | copy-start | bytes 1572868
  5.8 4.2 %collective-permute-start.9 = (f32[128,128]{1,0:T(8,128)S(1)}, f32[128,128]{1,0:T(8,128)S(1)}, u32[]{:S(2)}, u32[]{:S(2)}) collective-permute-start(f32[128,128]{1,0:T(8,128)S(1)} %get-tuple-element.11), channel_id=1, source_target_pairs={{0,1},{1,0},{2,3},{3,2},{4,5},{5,4},{6,7},{7,6},{8,9},{9,8},{10,11... | collective-permute-start | bytes 196616 | tf_op jit(solution)/shard_map/ppermute | solution.py:187
  9.1 1.3 %collective-permute-start = (f32[128,128]{1,0:T(8,128)S(1)}, f32[128,128]{1,0:T(8,128)S(1)}, u32[]{:S(2)}, u32[]{:S(2)}) collective-permute-start(f32[128,128]{1,0:T(8,128)S(1)} %get-tuple-element.12), channel_id=1, source_target_pairs={{0,1},{1,0},{2,3},{3,2},{4,5},{5,4},{6,7},{7,6},{8,9},{9,8},{10,11... | collective-permute-start | bytes 196616 | tf_op jit(solution)/shard_map/ppermute | solution.py:187
  10.4 6.6 %collective-permute-start.1 = (f32[128,128]{1,0:T(8,128)S(1)}, f32[128,128]{1,0:T(8,128)S(1)}, u32[]{:S(2)}, u32[]{:S(2)}) collective-permute-start(f32[128,128]{1,0:T(8,128)S(1)} %get-tuple-element.10), channel_id=1, source_target_pairs={{0,3},{1,224},{2,227},{3,0},{4,7},{5,228},{6,231},{7,4},{8,11},{9,... | collective-permute-start | bytes 196616 | tf_op jit(solution)/shard_map/ppermute | solution.py:183
  14.3 5.2 %collective-permute-start.10 = (f32[128,128]{1,0:T(8,128)S(1)}, f32[128,128]{1,0:T(8,128)S(1)}, u32[]{:S(2)}, u32[]{:S(2)}) collective-permute-start(f32[128,128]{1,0:T(8,128)S(1)} %get-tuple-element.9), channel_id=1, source_target_pairs={{0,3},{1,224},{2,227},{3,0},{4,7},{5,228},{6,231},{7,4},{8,11},{9,... | collective-permute-start | bytes 196616 | tf_op jit(solution)/shard_map/ppermute | solution.py:183
  17.0 6.0 %collective-permute-start.2 = (f32[128,128]{1,0:T(8,128)S(1)}, f32[128,128]{1,0:T(8,128)S(1)}, u32[]{:S(2)}, u32[]{:S(2)}) collective-permute-start(f32[128,128]{1,0:T(8,128)S(1)} %add.76), channel_id=1, source_target_pairs={{0,7},{1,32},{2,35},{3,4},{4,3},{5,36},{6,39},{7,0},{8,15},{9,40},... | collective-permute-start | bytes 196616 | tf_op jit(solution)/shard_map/ppermute | solution.py:183
  19.5 5.4 %collective-permute-start.11 = (f32[128,128]{1,0:T(8,128)S(1)}, f32[128,128]{1,0:T(8,128)S(1)}, u32[]{:S(2)}, u32[]{:S(2)}) collective-permute-start(f32[128,128]{1,0:T(8,128)S(1)} %add.84), channel_id=1, source_target_pairs={{0,7},{1,32},{2,35},{3,4},{4,3},{5,36},{6,39},{7,0},{8,15},{9,40},... | collective-permute-start | bytes 196616 | tf_op jit(solution)/shard_map/ppermute | solution.py:183
  23.0 4.8 %collective-permute-start.3 = (f32[128,128]{1,0:T(8,128)S(1)}, f32[128,128]{1,0:T(8,128)S(1)}, u32[]{:S(2)}, u32[]{:S(2)}) collective-permute-start(f32[128,128]{1,0:T(8,128)S(1)} %add.77), channel_id=1, source_target_pairs={{0,17},{1,65},{2,66},{3,18},{4,21},{5,69},{6,70},{7,22},{8,25},{9,... | collective-permute-start | bytes 196616 | tf_op jit(solution)/shard_map/ppermute | solution.py:183
  25.0 4.7 %collective-permute-start.12 = (f32[128,128]{1,0:T(8,128)S(1)}, f32[128,128]{1,0:T(8,128)S(1)}, u32[]{:S(2)}, u32[]{:S(2)}) collective-permute-start(f32[128,128]{1,0:T(8,128)S(1)} %add.85), channel_id=1, source_target_pairs={{0,17},{1,65},{2,66},{3,18},{4,21},{5,69},{6,70},{7,22},{8,25},{9,... | collective-permute-start | bytes 196616 | tf_op jit(solution)/shard_map/ppermute | solution.py:183
  27.8 3.8 %collective-permute-start.4 = (f32[128,128]{1,0:T(8,128)S(1)}, f32[128,128]{1,0:T(8,128)S(1)}, u32[]{:S(2)}, u32[]{:S(2)}) collective-permute-start(f32[128,128]{1,0:T(8,128)S(1)} %add.78), channel_id=1, source_target_pairs={{0,25},{1,2},{2,1},{3,26},{4,29},{5,6},{6,5},{7,30},{8,17},{9,10},... | collective-permute-start | bytes 196616 | tf_op jit(solution)/shard_map/ppermute | solution.py:183
  29.6 5.0 %collective-permute-start.13 = (f32[128,128]{1,0:T(8,128)S(1)}, f32[128,128]{1,0:T(8,128)S(1)}, u32[]{:S(2)}, u32[]{:S(2)}) collective-permute-start(f32[128,128]{1,0:T(8,128)S(1)} %add.86), channel_id=1, source_target_pairs={{0,25},{1,2},{2,1},{3,26},{4,29},{5,6},{6,5},{7,30},{8,17},{9,10},... | collective-permute-start | bytes 196616 | tf_op jit(solution)/shard_map/ppermute | solution.py:183
  31.6 5.0 %collective-permute-start.5 = (f32[128,128]{1,0:T(8,128)S(1)}, f32[128,128]{1,0:T(8,128)S(1)}, u32[]{:S(2)}, u32[]{:S(2)}) collective-permute-start(f32[128,128]{1,0:T(8,128)S(1)} %add.79), channel_id=1, source_target_pairs={{0,225},{1,6},{2,5},{3,226},{4,229},{5,2},{6,1},{7,230},{8,233},{9... | collective-permute-start | bytes 196616 | tf_op jit(solution)/shard_map/ppermute | solution.py:183
  34.7 5.0 %collective-permute-start.14 = (f32[128,128]{1,0:T(8,128)S(1)}, f32[128,128]{1,0:T(8,128)S(1)}, u32[]{:S(2)}, u32[]{:S(2)}) collective-permute-start(f32[128,128]{1,0:T(8,128)S(1)} %add.87), channel_id=1, source_target_pairs={{0,225},{1,6},{2,5},{3,226},{4,229},{5,2},{6,1},{7,230},{8,233},{9... | collective-permute-start | bytes 196616 | tf_op jit(solution)/shard_map/ppermute | solution.py:183
  36.7 4.2 %collective-permute-start.6 = (f32[128,128]{1,0:T(8,128)S(1)}, f32[128,128]{1,0:T(8,128)S(1)}, u32[]{:S(2)}, u32[]{:S(2)}) collective-permute-start(f32[128,128]{1,0:T(8,128)S(1)} %add.80), channel_id=1, source_target_pairs={{0,33},{1,16},{2,19},{3,34},{4,37},{5,20},{6,23},{7,38},{8,41},{9,... | collective-permute-start | bytes 196616 | tf_op jit(solution)/shard_map/ppermute | solution.py:183
  39.7 4.0 %collective-permute-start.15 = (f32[128,128]{1,0:T(8,128)S(1)}, f32[128,128]{1,0:T(8,128)S(1)}, u32[]{:S(2)}, u32[]{:S(2)}) collective-permute-start(f32[128,128]{1,0:T(8,128)S(1)} %add.88), channel_id=1, source_target_pairs={{0,33},{1,16},{2,19},{3,34},{4,37},{5,20},{6,23},{7,38},{8,41},{9,... | collective-permute-start | bytes 196616 | tf_op jit(solution)/shard_map/ppermute | solution.py:183
  40.9 5.2 %collective-permute-start.7 = (f32[128,128]{1,0:T(8,128)S(1)}, f32[128,128]{1,0:T(8,128)S(1)}, u32[]{:S(2)}, u32[]{:S(2)}) collective-permute-start(f32[128,128]{1,0:T(8,128)S(1)} %add.81), channel_id=1, source_target_pairs={{0,64},{1,24},{2,27},{3,67},{4,68},{5,28},{6,31},{7,71},{8,72},{9,... | collective-permute-start | bytes 196616 | tf_op jit(solution)/shard_map/ppermute | solution.py:183
  43.7 5.0 %collective-permute-start.16 = (f32[128,128]{1,0:T(8,128)S(1)}, f32[128,128]{1,0:T(8,128)S(1)}, u32[]{:S(2)}, u32[]{:S(2)}) collective-permute-start(f32[128,128]{1,0:T(8,128)S(1)} %add.89), channel_id=1, source_target_pairs={{0,64},{1,24},{2,27},{3,67},{4,68},{5,28},{6,31},{7,71},{8,72},{9,... | collective-permute-start | bytes 196616 | tf_op jit(solution)/shard_map/ppermute | solution.py:183
  46.1 3.0 %collective-permute-start.8 = (f32[128,128]{1,0:T(8,128)S(1)}, f32[128,128]{1,0:T(8,128)S(1)}, u32[]{:S(2)}, u32[]{:S(2)}) collective-permute-start(f32[128,128]{1,0:T(8,128)S(1)} %add.82), channel_id=1, source_target_pairs={{0,1},{1,0},{2,3},{3,2},{4,5},{5,4},{6,7},{7,6},{8,9},{9,8},{10,11... | collective-permute-start | bytes 196616 | tf_op jit(solution)/shard_map/ppermute | solution.py:187
  48.7 3.3 %collective-permute-start.17 = (f32[128,128]{1,0:T(8,128)S(1)}, f32[128,128]{1,0:T(8,128)S(1)}, u32[]{:S(2)}, u32[]{:S(2)}) collective-permute-start(f32[128,128]{1,0:T(8,128)S(1)} %add.90), channel_id=1, source_target_pairs={{0,1},{1,0},{2,3},{3,2},{4,5},{5,4},{6,7},{7,6},{8,9},{9,8},{10,11... | collective-permute-start | bytes 196616 | tf_op jit(solution)/shard_map/ppermute | solution.py:187

commit v4 on v3

--- a/solution.py
+++ b/solution.py
@@ -51,7 +51,8 @@
         for i in range(pieces):
             cut = slice(i * piece, (i + 1) * piece)
             stack[i, :width] = high[:, cut]
-            stack[i, width:] = middle[:, cut]
+            stack[i, width : 2 * width] = middle[:, cut]
+            stack[i, 2 * width :] = low[:, cut]
         whole = jnp.concatenate([high, middle, low], axis=0)
         sums = last_product(whole, high) + last_product(whole, middle) + last_product(whole, low)
         total[:, :count] = jnp.zeros((width, count), jnp.float32)
@@ -63,8 +64,8 @@
             values = following_v[i]
             high = values.astype(jnp.bfloat16)
             low = (values - high.astype(jnp.float32)).astype(jnp.bfloat16)
-            sums = last_product(stack[i], high)
-            total[:, :count] += sums[:width] + sums[width:] + last_product(stack[i, :width], low)
+            sums = last_product(stack[i], high) + last_product(stack[i], low)
+            total[:, :count] += sums[:width] + sums[width : 2 * width] + sums[2 * width :]
 
         for j in range(columns // LANES):
             out_ref[j * width : (j + 1) * width] = total[:, j * LANES : (j + 1) * LANES]
@@ -77,7 +78,7 @@
         scratch_shapes=[
             pltpu.VMEM((width, cells), jnp.float32),
             pltpu.VMEM((pieces, count, piece), jnp.float32),
-            pltpu.VMEM((pieces, 2 * width, piece), jnp.bfloat16),
+            pltpu.VMEM((pieces, 3 * width, piece), jnp.bfloat16),
             pltpu.VMEM((width, columns), jnp.float32),
             pltpu.SemaphoreType.DMA((1 + pieces,)),
         ],
@@ -189,7 +190,7 @@
 
 X1, X3, Y1, Y3, Z1, Z2, Z7 = (0, 0, 1), (0, 0, 3), (0, 1, 0), (0, 3, 0), (1, 0, 0), (2, 0, 0), (7, 0, 0)
 
-ROUNDS = [((X1, Z7),) * 2, ((X3, Z1),) * 2, ((Y1, Z2),) * 2, ((Y3, X1),) * 2, ((Z7, X3),) * 2, ((Z1, Y1),) * 2, ((Z2, Y3),) * 2]
+ROUNDS = [((X1, Z1),) * 2, ((Z1, X1),) * 2, ((Y1, Z2),) * 2, ((X3, Y1),) * 2, ((Y3, Z7),) * 2, ((Z2, X3),) * 2, ((Z7, Y3),) * 2]
 
 
 def body(snapshot_panel, following):

time: 53.2 us -> 52 us (0.977)
  starting transfers between devices: 33.1 us -> 29.4 us
  waiting for transfers between devices: 10.1 us -> 12.2 us
    ppermute x14, starting transfers between devices: 28.2 us -> 25.2 us  [exchange(): return lax.ppermute(block, AXES, pairs)]
    ppermute x14, waiting for transfers between devices: 8.94 us -> 11 us  [exchange(): return lax.ppermute(block, AXES, pairs)]
    ppermute x4, starting transfers between devices: 4.93 us -> 4.18 us  [other_core(): lax.ppermute(block, AXES, [(i, i ^ 1) for i in range(math.prod(SIZES))])]
  transfers between devices with their start and end apart: 18 -> 18, of which waited for: 8 -> 12; matrix products, arithmetic and copies ran while one was open for 0% -> 0% of each run, Pallas kernels for 5% -> 6%
where the time goes in v4:
time: 52 us; the launch traced here: 51.6 us
  starting transfers between devices  29.4 us (57%)
  waiting for transfers between devices  12.2 us (23%)
  Pallas kernels  9.02 us (17%)
  between operations  0.8 us (2%)
    ppermute x14, starting transfers between devices, exchange(): return lax.ppermute(block, AXES, pairs)  25.2 us
    ppermute x14, waiting for transfers between devices, exchange(): return lax.ppermute(block, AXES, pairs)  11 us
    pallas_call x1, Pallas kernels, local_products(): pl.pallas_call(kernel, out_shape=jax.ShapeDtypeStruct((width * columns //...  5.15 us
    ppermute x4, starting transfers between devices, other_core(): lax.ppermute(block, AXES, [(i, i ^ 1) for i in range(math.prod(SIZES))])  4.18 us
    pallas_call x1, Pallas kernels, factored(): pl.pallas_call(kernel, out_shape=(jax.ShapeDtypeStruct((width, cells), jn...  2.88 us
    ppermute x4, waiting for transfers between devices, other_core(): lax.ppermute(block, AXES, [(i, i ^ 1) for i in range(math.prod(SIZES))])  1.16 us
  transfers between devices with their start and end apart: 18, of which 12 were waited for; matrix products, arithmetic and copies ran while one was open for 0% of the time, Pallas kernels for 6%

profile of v4, /device:TPU:1, one launch (start us, length us, event | category | flops | bytes accessed | tf_op | source)
XLA Modules:
  0.0 51.6 jit_solution(5829055421310299856)
XLA Ops:
  0.6 0.0 copy-start
  0.7 5.1 %local_products.1 = f32[512,128]{1,0:T(8,128)S(1)} custom-call(f32[64,2048]{1,0:T(8,128)} %panel_ref.1, f32[960,2048]{1,0:T(8,128)} %following_hbm.1), custom_call_target="tpu_custom_call" | custom-call | tf_op jit(solution)/shard_map/local_products/pallas_call | solution.py:73
  5.8 3.3 %collective-permute-start.9 = (f32[128,128]{1,0:T(8,128)S(1)}, f32[128,128]{1,0:T(8,128)S(1)}, u32[]{:S(2)}, u32[]{:S(2)}) collective-permute-start(f32[128,128]{1,0:T(8,128)S(1)} %get-tuple-element.11), channel_id=1, source_target_pairs={{0,1},{1,0},{2,3},{3,2},{4,5},{5,4},{6,7},{7,6},{8,9},{9,8},{10,11... | collective-permute-start | bytes 196616 | tf_op jit(solution)/shard_map/ppermute | solution.py:188
  9.2 0.1 collective-permute-start
  9.3 0.8 %collective-permute-done.9 = f32[128,128]{1,0:T(8,128)S(1)} collective-permute-done((f32[128,128]{1,0:T(8,128)S(1)}, f32[128,128]{1,0:T(8,128)S(1)}, u32[]{:S(2)}, u32[]{:S(2)}) %collective-permute-start.9) | collective-permute-done | bytes 65568 | tf_op jit(solution)/shard_map/ppermute | solution.py:188
  10.1 0.4 collective-permute-done
  10.4 0.1 collective-permute-start.1
  10.6 1.7 %collective-permute-start.10 = (f32[128,128]{1,0:T(8,128)S(1)}, f32[128,128]{1,0:T(8,128)S(1)}, u32[]{:S(2)}, u32[]{:S(2)}) collective-permute-start(f32[128,128]{1,0:T(8,128)S(1)} %get-tuple-element.9), channel_id=1, source_target_pairs={{0,3},{1,32},{2,35},{3,0},{4,7},{5,36},{6,39},{7,4},{8,11},{9,40},... | collective-permute-start | bytes 196616 | tf_op jit(solution)/shard_map/ppermute | solution.py:184
  12.3 2.2 %collective-permute-done.1 = f32[128,128]{1,0:T(8,128)S(1)} collective-permute-done((f32[128,128]{1,0:T(8,128)S(1)}, f32[128,128]{1,0:T(8,128)S(1)}, u32[]{:S(2)}, u32[]{:S(2)}) %collective-permute-start.1) | collective-permute-done | bytes 65568 | tf_op jit(solution)/shard_map/ppermute | solution.py:184
  14.5 0.1 collective-permute-start.2
  14.6 0.3 collective-permute-done.10
  14.9 1.5 %collective-permute-start.11 = (f32[128,128]{1,0:T(8,128)S(1)}, f32[128,128]{1,0:T(8,128)S(1)}, u32[]{:S(2)}, u32[]{:S(2)}) collective-permute-start(f32[128,128]{1,0:T(8,128)S(1)} %add.84), channel_id=1, source_target_pairs={{0,33},{1,2},{2,1},{3,34},{4,37},{5,6},{6,5},{7,38},{8,41},{9,10},... | collective-permute-start | bytes 196616 | tf_op jit(solution)/shard_map/ppermute | solution.py:184
  16.5 2.0 %collective-permute-done.2 = f32[128,128]{1,0:T(8,128)S(1)} collective-permute-done((f32[128,128]{1,0:T(8,128)S(1)}, f32[128,128]{1,0:T(8,128)S(1)}, u32[]{:S(2)}, u32[]{:S(2)}) %collective-permute-start.2) | collective-permute-done | bytes 65568 | tf_op jit(solution)/shard_map/ppermute | solution.py:184
  18.5 1.1 %collective-permute-start.3 = (f32[128,128]{1,0:T(8,128)S(1)}, f32[128,128]{1,0:T(8,128)S(1)}, u32[]{:S(2)}, u32[]{:S(2)}) collective-permute-start(f32[128,128]{1,0:T(8,128)S(1)} %add.77), channel_id=1, source_target_pairs={{0,17},{1,65},{2,66},{3,18},{4,21},{5,69},{6,70},{7,22},{8,25},{9,... | collective-permute-start | bytes 196616 | tf_op jit(solution)/shard_map/ppermute | solution.py:184
  19.6 0.0 collective-permute-done.11
  19.6 1.8 %collective-permute-start.12 = (f32[128,128]{1,0:T(8,128)S(1)}, f32[128,128]{1,0:T(8,128)S(1)}, u32[]{:S(2)}, u32[]{:S(2)}) collective-permute-start(f32[128,128]{1,0:T(8,128)S(1)} %add.85), channel_id=1, source_target_pairs={{0,17},{1,65},{2,66},{3,18},{4,21},{5,69},{6,70},{7,22},{8,25},{9,... | collective-permute-start | bytes 196616 | tf_op jit(solution)/shard_map/ppermute | solution.py:184
  21.3 2.0 %collective-permute-done.3 = f32[128,128]{1,0:T(8,128)S(1)} collective-permute-done((f32[128,128]{1,0:T(8,128)S(1)}, f32[128,128]{1,0:T(8,128)S(1)}, u32[]{:S(2)}, u32[]{:S(2)}) %collective-permute-start.3) | collective-permute-done | bytes 65568 | tf_op jit(solution)/shard_map/ppermute | solution.py:184
  23.3 0.2 collective-permute-start.4
  23.5 0.5 collective-permute-done.12
  24.0 3.2 %collective-permute-start.13 = (f32[128,128]{1,0:T(8,128)S(1)}, f32[128,128]{1,0:T(8,128)S(1)}, u32[]{:S(2)}, u32[]{:S(2)}) collective-permute-start(f32[128,128]{1,0:T(8,128)S(1)} %add.86), channel_id=1, source_target_pairs={{0,7},{1,16},{2,19},{3,4},{4,3},{5,20},{6,23},{7,0},{8,15},{9,24},... | collective-permute-start | bytes 196616 | tf_op jit(solution)/shard_map/ppermute | solution.py:184
  27.2 0.2 collective-permute-done.4
  27.4 4.2 %collective-permute-start.5 = (f32[128,128]{1,0:T(8,128)S(1)}, f32[128,128]{1,0:T(8,128)S(1)}, u32[]{:S(2)}, u32[]{:S(2)}) collective-permute-start(f32[128,128]{1,0:T(8,128)S(1)} %add.79), channel_id=1, source_target_pairs={{0,25},{1,224},{2,227},{3,26},{4,29},{5,228},{6,231},{7,30},{8,17}... | collective-permute-start | bytes 196616 | tf_op jit(solution)/shard_map/ppermute | solution.py:184
  31.6 0.0 collective-permute-done.13
  31.6 1.4 %collective-permute-start.14 = (f32[128,128]{1,0:T(8,128)S(1)}, f32[128,128]{1,0:T(8,128)S(1)}, u32[]{:S(2)}, u32[]{:S(2)}) collective-permute-start(f32[128,128]{1,0:T(8,128)S(1)} %add.87), channel_id=1, source_target_pairs={{0,25},{1,224},{2,227},{3,26},{4,29},{5,228},{6,231},{7,30},{8,17}... | collective-permute-start | bytes 196616 | tf_op jit(solution)/shard_map/ppermute | solution.py:184
  33.0 0.8 %collective-permute-done.5 = f32[128,128]{1,0:T(8,128)S(1)} collective-permute-done((f32[128,128]{1,0:T(8,128)S(1)}, f32[128,128]{1,0:T(8,128)S(1)}, u32[]{:S(2)}, u32[]{:S(2)}) %collective-permute-start.5) | collective-permute-done | bytes 65568 | tf_op jit(solution)/shard_map/ppermute | solution.py:184
  33.8 2.4 %collective-permute-start.6 = (f32[128,128]{1,0:T(8,128)S(1)}, f32[128,128]{1,0:T(8,128)S(1)}, u32[]{:S(2)}, u32[]{:S(2)}) collective-permute-start(f32[128,128]{1,0:T(8,128)S(1)} %add.80), channel_id=1, source_target_pairs={{0,64},{1,6},{2,5},{3,67},{4,68},{5,2},{6,1},{7,71},{8,72},{9,14},... | collective-permute-start | bytes 196616 | tf_op jit(solution)/shard_map/ppermute | solution.py:184
  36.2 0.6 %collective-permute-done.14 = f32[128,128]{1,0:T(8,128)S(1)} collective-permute-done((f32[128,128]{1,0:T(8,128)S(1)}, f32[128,128]{1,0:T(8,128)S(1)}, u32[]{:S(2)}, u32[]{:S(2)}) %collective-permute-start.14) | collective-permute-done | bytes 65568 | tf_op jit(solution)/shard_map/ppermute | solution.py:184
  36.7 2.4 %collective-permute-start.15 = (f32[128,128]{1,0:T(8,128)S(1)}, f32[128,128]{1,0:T(8,128)S(1)}, u32[]{:S(2)}, u32[]{:S(2)}) collective-permute-start(f32[128,128]{1,0:T(8,128)S(1)} %add.88), channel_id=1, source_target_pairs={{0,64},{1,6},{2,5},{3,67},{4,68},{5,2},{6,1},{7,71},{8,72},{9,14},... | collective-permute-start | bytes 196616 | tf_op jit(solution)/shard_map/ppermute | solution.py:184
  39.2 0.0 collective-permute-done.6
  39.2 3.3 %collective-permute-start.7 = (f32[128,128]{1,0:T(8,128)S(1)}, f32[128,128]{1,0:T(8,128)S(1)}, u32[]{:S(2)}, u32[]{:S(2)}) collective-permute-start(f32[128,128]{1,0:T(8,128)S(1)} %add.81), channel_id=1, source_target_pairs={{0,225},{1,24},{2,27},{3,226},{4,229},{5,28},{6,31},{7,230},{8,233... | collective-permute-start | bytes 196616 | tf_op jit(solution)/shard_map/ppermute | solution.py:184
  42.5 0.0 collective-permute-done.15
  42.5 1.9 %collective-permute-start.16 = (f32[128,128]{1,0:T(8,128)S(1)}, f32[128,128]{1,0:T(8,128)S(1)}, u32[]{:S(2)}, u32[]{:S(2)}) collective-permute-start(f32[128,128]{1,0:T(8,128)S(1)} %add.89), channel_id=1, source_target_pairs={{0,225},{1,24},{2,27},{3,226},{4,229},{5,28},{6,31},{7,230},{8,233... | collective-permute-start | bytes 196616 | tf_op jit(solution)/shard_map/ppermute | solution.py:184
  44.4 0.3 collective-permute-done.7
  44.7 0.6 %collective-permute-start.8 = (f32[128,128]{1,0:T(8,128)S(1)}, f32[128,128]{1,0:T(8,128)S(1)}, u32[]{:S(2)}, u32[]{:S(2)}) collective-permute-start(f32[128,128]{1,0:T(8,128)S(1)} %add.82), channel_id=1, source_target_pairs={{0,1},{1,0},{2,3},{3,2},{4,5},{5,4},{6,7},{7,6},{8,9},{9,8},{10,11... | collective-permute-start | bytes 196616 | tf_op jit(solution)/shard_map/ppermute | solution.py:188
  45.3 2.2 %collective-permute-done.16 = f32[128,128]{1,0:T(8,128)S(1)} collective-permute-done((f32[128,128]{1,0:T(8,128)S(1)}, f32[128,128]{1,0:T(8,128)S(1)}, u32[]{:S(2)}, u32[]{:S(2)}) %collective-permute-start.16) | collective-permute-done | bytes 65568 | tf_op jit(solution)/shard_map/ppermute | solution.py:184
  47.5 0.2 collective-permute-start.17
  47.7 0.0 collective-permute-done.8
  47.7 0.0 copy-done
  47.7 2.9 %factored.1 = (f32[64,2048]{1,0:T(8,128)}, f32[64,64]{1,0:T(8,128)}, bf16[64,384]{1,0:T(8,128)(2,1)S(1)}) custom-call(f32[64,128]{1,0:T(8,128)S(1)} %slice.24.gram_ref, f32[64,2048]{1,0:T(8,128)S(1)} %copy-done), custom_call_target="tpu_custom_call" | custom-call | tf_op jit(solution)/shard_map/factored/pallas_call | solution.py:139
  50.6 0.0 collective-permute-done.17
  50.6 1.0 %projected.1 = f32[64,960]{1,0:T(8,128)} custom-call(bf16[64,384]{1,0:T(8,128)(2,1)S(1)} %get-tuple-element.8.inverse_ref, f32[512,128]{1,0:T(8,128)S(1)} %pad_maximum_fusion.summed_ref), custom_call_target="tpu_custom_call" | custom-call | tf_op jit(solution)/shard_map/projected/pallas_call | solution.py:163
  (20 shorter events, 0.2 us)
Async XLA Ops:
  0.6 47.1 %copy-start = (f32[64,2048]{1,0:T(8,128)S(1)}, f32[64,2048]{1,0:T(8,128)}, u32[]{:S(2)}) copy-start(f32[64,2048]{1,0:T(8,128)} %panel_ref.1) | copy-start | bytes 1572868
  5.8 4.2 %collective-permute-start.9 = (f32[128,128]{1,0:T(8,128)S(1)}, f32[128,128]{1,0:T(8,128)S(1)}, u32[]{:S(2)}, u32[]{:S(2)}) collective-permute-start(f32[128,128]{1,0:T(8,128)S(1)} %get-tuple-element.11), channel_id=1, source_target_pairs={{0,1},{1,0},{2,3},{3,2},{4,5},{5,4},{6,7},{7,6},{8,9},{9,8},{10,11... | collective-permute-start | bytes 196616 | tf_op jit(solution)/shard_map/ppermute | solution.py:188
  9.2 1.3 %collective-permute-start = (f32[128,128]{1,0:T(8,128)S(1)}, f32[128,128]{1,0:T(8,128)S(1)}, u32[]{:S(2)}, u32[]{:S(2)}) collective-permute-start(f32[128,128]{1,0:T(8,128)S(1)} %get-tuple-element.12), channel_id=1, source_target_pairs={{0,1},{1,0},{2,3},{3,2},{4,5},{5,4},{6,7},{7,6},{8,9},{9,8},{10,11... | collective-permute-start | bytes 196616 | tf_op jit(solution)/shard_map/ppermute | solution.py:188
  10.4 4.1 %collective-permute-start.1 = (f32[128,128]{1,0:T(8,128)S(1)}, f32[128,128]{1,0:T(8,128)S(1)}, u32[]{:S(2)}, u32[]{:S(2)}) collective-permute-start(f32[128,128]{1,0:T(8,128)S(1)} %get-tuple-element.10), channel_id=1, source_target_pairs={{0,3},{1,32},{2,35},{3,0},{4,7},{5,36},{6,39},{7,4},{8,11},{9,40},... | collective-permute-start | bytes 196616 | tf_op jit(solution)/shard_map/ppermute | solution.py:184
  10.6 4.4 %collective-permute-start.10 = (f32[128,128]{1,0:T(8,128)S(1)}, f32[128,128]{1,0:T(8,128)S(1)}, u32[]{:S(2)}, u32[]{:S(2)}) collective-permute-start(f32[128,128]{1,0:T(8,128)S(1)} %get-tuple-element.9), channel_id=1, source_target_pairs={{0,3},{1,32},{2,35},{3,0},{4,7},{5,36},{6,39},{7,4},{8,11},{9,40},... | collective-permute-start | bytes 196616 | tf_op jit(solution)/shard_map/ppermute | solution.py:184
  14.5 3.9 %collective-permute-start.2 = (f32[128,128]{1,0:T(8,128)S(1)}, f32[128,128]{1,0:T(8,128)S(1)}, u32[]{:S(2)}, u32[]{:S(2)}) collective-permute-start(f32[128,128]{1,0:T(8,128)S(1)} %add.76), channel_id=1, source_target_pairs={{0,33},{1,2},{2,1},{3,34},{4,37},{5,6},{6,5},{7,38},{8,41},{9,10},... | collective-permute-start | bytes 196616 | tf_op jit(solution)/shard_map/ppermute | solution.py:184
  14.9 4.6 %collective-permute-start.11 = (f32[128,128]{1,0:T(8,128)S(1)}, f32[128,128]{1,0:T(8,128)S(1)}, u32[]{:S(2)}, u32[]{:S(2)}) collective-permute-start(f32[128,128]{1,0:T(8,128)S(1)} %add.84), channel_id=1, source_target_pairs={{0,33},{1,2},{2,1},{3,34},{4,37},{5,6},{6,5},{7,38},{8,41},{9,10},... | collective-permute-start | bytes 196616 | tf_op jit(solution)/shard_map/ppermute | solution.py:184
  18.5 4.8 %collective-permute-start.3 = (f32[128,128]{1,0:T(8,128)S(1)}, f32[128,128]{1,0:T(8,128)S(1)}, u32[]{:S(2)}, u32[]{:S(2)}) collective-permute-start(f32[128,128]{1,0:T(8,128)S(1)} %add.77), channel_id=1, source_target_pairs={{0,17},{1,65},{2,66},{3,18},{4,21},{5,69},{6,70},{7,22},{8,25},{9,... | collective-permute-start | bytes 196616 | tf_op jit(solution)/shard_map/ppermute | solution.py:184
  19.6 4.4 %collective-permute-start.12 = (f32[128,128]{1,0:T(8,128)S(1)}, f32[128,128]{1,0:T(8,128)S(1)}, u32[]{:S(2)}, u32[]{:S(2)}) collective-permute-start(f32[128,128]{1,0:T(8,128)S(1)} %add.85), channel_id=1, source_target_pairs={{0,17},{1,65},{2,66},{3,18},{4,21},{5,69},{6,70},{7,22},{8,25},{9,... | collective-permute-start | bytes 196616 | tf_op jit(solution)/shard_map/ppermute | solution.py:184
  23.3 4.1 %collective-permute-start.4 = (f32[128,128]{1,0:T(8,128)S(1)}, f32[128,128]{1,0:T(8,128)S(1)}, u32[]{:S(2)}, u32[]{:S(2)}) collective-permute-start(f32[128,128]{1,0:T(8,128)S(1)} %add.78), channel_id=1, source_target_pairs={{0,7},{1,16},{2,19},{3,4},{4,3},{5,20},{6,23},{7,0},{8,15},{9,24},... | collective-permute-start | bytes 196616 | tf_op jit(solution)/shard_map/ppermute | solution.py:184
  24.0 7.6 %collective-permute-start.13 = (f32[128,128]{1,0:T(8,128)S(1)}, f32[128,128]{1,0:T(8,128)S(1)}, u32[]{:S(2)}, u32[]{:S(2)}) collective-permute-start(f32[128,128]{1,0:T(8,128)S(1)} %add.86), channel_id=1, source_target_pairs={{0,7},{1,16},{2,19},{3,4},{4,3},{5,20},{6,23},{7,0},{8,15},{9,24},... | collective-permute-start | bytes 196616 | tf_op jit(solution)/shard_map/ppermute | solution.py:184
  27.4 6.4 %collective-permute-start.5 = (f32[128,128]{1,0:T(8,128)S(1)}, f32[128,128]{1,0:T(8,128)S(1)}, u32[]{:S(2)}, u32[]{:S(2)}) collective-permute-start(f32[128,128]{1,0:T(8,128)S(1)} %add.79), channel_id=1, source_target_pairs={{0,25},{1,224},{2,227},{3,26},{4,29},{5,228},{6,231},{7,30},{8,17}... | collective-permute-start | bytes 196616 | tf_op jit(solution)/shard_map/ppermute | solution.py:184
  31.6 5.1 %collective-permute-start.14 = (f32[128,128]{1,0:T(8,128)S(1)}, f32[128,128]{1,0:T(8,128)S(1)}, u32[]{:S(2)}, u32[]{:S(2)}) collective-permute-start(f32[128,128]{1,0:T(8,128)S(1)} %add.87), channel_id=1, source_target_pairs={{0,25},{1,224},{2,227},{3,26},{4,29},{5,228},{6,231},{7,30},{8,17}... | collective-permute-start | bytes 196616 | tf_op jit(solution)/shard_map/ppermute | solution.py:184
  33.8 5.4 %collective-permute-start.6 = (f32[128,128]{1,0:T(8,128)S(1)}, f32[128,128]{1,0:T(8,128)S(1)}, u32[]{:S(2)}, u32[]{:S(2)}) collective-permute-start(f32[128,128]{1,0:T(8,128)S(1)} %add.80), channel_id=1, source_target_pairs={{0,64},{1,6},{2,5},{3,67},{4,68},{5,2},{6,1},{7,71},{8,72},{9,14},... | collective-permute-start | bytes 196616 | tf_op jit(solution)/shard_map/ppermute | solution.py:184
  36.7 5.7 %collective-permute-start.15 = (f32[128,128]{1,0:T(8,128)S(1)}, f32[128,128]{1,0:T(8,128)S(1)}, u32[]{:S(2)}, u32[]{:S(2)}) collective-permute-start(f32[128,128]{1,0:T(8,128)S(1)} %add.88), channel_id=1, source_target_pairs={{0,64},{1,6},{2,5},{3,67},{4,68},{5,2},{6,1},{7,71},{8,72},{9,14},... | collective-permute-start | bytes 196616 | tf_op jit(solution)/shard_map/ppermute | solution.py:184
  39.2 5.5 %collective-permute-start.7 = (f32[128,128]{1,0:T(8,128)S(1)}, f32[128,128]{1,0:T(8,128)S(1)}, u32[]{:S(2)}, u32[]{:S(2)}) collective-permute-start(f32[128,128]{1,0:T(8,128)S(1)} %add.81), channel_id=1, source_target_pairs={{0,225},{1,24},{2,27},{3,226},{4,229},{5,28},{6,31},{7,230},{8,233... | collective-permute-start | bytes 196616 | tf_op jit(solution)/shard_map/ppermute | solution.py:184
  42.5 5.0 %collective-permute-start.16 = (f32[128,128]{1,0:T(8,128)S(1)}, f32[128,128]{1,0:T(8,128)S(1)}, u32[]{:S(2)}, u32[]{:S(2)}) collective-permute-start(f32[128,128]{1,0:T(8,128)S(1)} %add.89), channel_id=1, source_target_pairs={{0,225},{1,24},{2,27},{3,226},{4,229},{5,28},{6,31},{7,230},{8,233... | collective-permute-start | bytes 196616 | tf_op jit(solution)/shard_map/ppermute | solution.py:184
  44.7 2.9 %collective-permute-start.8 = (f32[128,128]{1,0:T(8,128)S(1)}, f32[128,128]{1,0:T(8,128)S(1)}, u32[]{:S(2)}, u32[]{:S(2)}) collective-permute-start(f32[128,128]{1,0:T(8,128)S(1)} %add.82), channel_id=1, source_target_pairs={{0,1},{1,0},{2,3},{3,2},{4,5},{5,4},{6,7},{7,6},{8,9},{9,8},{10,11... | collective-permute-start | bytes 196616 | tf_op jit(solution)/shard_map/ppermute | solution.py:188
  47.5 3.1 %collective-permute-start.17 = (f32[128,128]{1,0:T(8,128)S(1)}, f32[128,128]{1,0:T(8,128)S(1)}, u32[]{:S(2)}, u32[]{:S(2)}) collective-permute-start(f32[128,128]{1,0:T(8,128)S(1)} %add.90), channel_id=1, source_target_pairs={{0,1},{1,0},{2,3},{3,2},{4,5},{5,4},{6,7},{7,6},{8,9},{9,8},{10,11... | collective-permute-start | bytes 196616 | tf_op jit(solution)/shard_map/ppermute | solution.py:188

commit v5 on v4

--- a/solution.py
+++ b/solution.py
@@ -122,50 +122,70 @@
     return jnp.concatenate([high, middle, low, high, middle, high], axis=0)
 
 
-def factored(gram, panel, root_rows):
-    width, cells = panel.shape
-
-    def kernel(gram_ref, panel_ref, basis_ref, upper_ref, inverse_ref):
+def factored(half, own, other, width, root_rows):
+    start = own.shape[0] - width
+
+    def kernel(half_ref, own_ref, other_ref, upper_ref, inverse_ref):
         rows = lax.broadcasted_iota(jnp.int32, (width, 2 * width), 0)
         lanes = lax.broadcasted_iota(jnp.int32, (width, 2 * width), 1)
         unit = jnp.where(lanes == rows + width, 1.0, 0.0)
-        work = eliminated(jnp.where(lanes < width, pltpu.roll(gram_ref[...], width, axis=1), unit), width)
+        block = jnp.where(half_ref[0] == 1, own_ref[start:], other_ref[start:])
+        work = eliminated(jnp.where(lanes < width, pltpu.roll(block, width, axis=1), unit), width)
         upper_ref[...] = jnp.where(rows <= lanes, work, 0.0)[:, :width] * (1.0 / root_rows)
-        inverse = stacked_left(*parts3(work[:, width:]))
-        inverse_ref[...] = inverse
-        basis = jnp.dot(inverse, stacked_right(panel_ref[...]), preferred_element_type=jnp.float32)
-        basis_ref[...] = basis * root_rows
+        inverse_ref[...] = stacked_left(*parts3(work[:, width:]))
 
     return pl.pallas_call(
         kernel,
         out_shape=(
-            jax.ShapeDtypeStruct((width, cells), jnp.float32),
             jax.ShapeDtypeStruct((width, width), jnp.float32),
             jax.ShapeDtypeStruct((width, 6 * width), jnp.bfloat16),
         ),
+        in_specs=[pl.BlockSpec(memory_space=pltpu.SMEM)] + [pl.BlockSpec(memory_space=pltpu.VMEM)] * 2,
         compiler_params=pltpu.CompilerParams(vmem_limit_bytes=32 * MIB),
         name="factored",
-    )(gram, panel)
-
-
-def projected(inverse, summed, root_rows):
+    )(half, own, other)
+
+
+def solved(half, inverse, panel, sums, root_rows):
     width = inverse.shape[0]
-    count = summed.shape[0] * LANES // width - width
-
-    def kernel(inverse_ref, summed_ref, out_ref):
+    quarter = sums[0][0].shape[0]
+    count = 4 * quarter * LANES // width - width
+
+    def kernel(half_ref, inverse_ref, panel_ref, own0, other0, own1, other1, basis_hbm, out_hbm, basis, out, sem):
+        basis[...] = (
+            jnp.dot(inverse_ref[...], stacked_right(panel_ref[...]), preferred_element_type=jnp.float32) * root_rows
+        )
+        basis_copy = pltpu.make_async_copy(basis, basis_hbm, sem.at[0])
+        basis_copy.start()
         for j in range(0, count, LANES):
             size = min(LANES, count - j)
-            start = j // LANES * width
-            right = stacked_right(summed_ref[start : start + width])
+            place, start = divmod(j // LANES * width, quarter)
+            own, other = ((own0, other0), (own1, other1))[place % 2]
+            rows = slice(start, start + width)
+            right = stacked_right(jnp.where(half_ref[0] == place // 2, own[rows], other[rows]))
             block = jnp.dot(inverse_ref[...], right, preferred_element_type=jnp.float32) * (1.0 / root_rows)
-            out_ref[:, j : j + size] = block[:, :size]
+            out[:, j : j + size] = block[:, :size]
+        out_copy = pltpu.make_async_copy(out, out_hbm, sem.at[1])
+        out_copy.start()
+        basis_copy.wait()
+        out_copy.wait()
 
     return pl.pallas_call(
         kernel,
-        out_shape=jax.ShapeDtypeStruct((width, count), jnp.float32),
+        out_shape=(
+            jax.ShapeDtypeStruct(panel.shape, jnp.float32),
+            jax.ShapeDtypeStruct((width, count), jnp.float32),
+        ),
+        in_specs=[pl.BlockSpec(memory_space=pltpu.SMEM)] + [pl.BlockSpec(memory_space=pltpu.VMEM)] * 6,
+        out_specs=(pl.BlockSpec(memory_space=pltpu.HBM),) * 2,
+        scratch_shapes=[
+            pltpu.VMEM(panel.shape, jnp.float32),
+            pltpu.VMEM((width, count), jnp.float32),
+            pltpu.SemaphoreType.DMA((2,)),
+        ],
         compiler_params=pltpu.CompilerParams(vmem_limit_bytes=32 * MIB),
-        name="projected",
-    )(inverse, summed)
+        name="solved",
+    )(half, inverse, panel, *sums[0], *sums[1])
 
 
 def half_of(z, y, x, core):
@@ -207,14 +227,11 @@
         one = one + exchange(one, *first)
         two = two + exchange(two, *second)
 
-    def both(block):
-        other = other_core(block)
-        return jnp.where(half == 0, block, other), jnp.where(half == 0, other, block)
-
-    first, last = both(one)
-    basis, upper, inverse = factored(last[-snapshot_panel.shape[0] :], snapshot_panel, root_rows)
-    low, high = both(two)
-    projection = projected(inverse, jnp.concatenate([low, first, high, last]), root_rows)
+    flag = half.astype(jnp.int32).reshape(1)
+    one = one, other_core(one)
+    upper, inverse = factored(flag, *one, snapshot_panel.shape[0], root_rows)
+    two = two, other_core(two)
+    basis, projection = solved(flag, inverse, snapshot_panel, (two, one), root_rows)
     return basis, upper, projection
 
 

time: 52 us -> 51.6 us (level)
  transfers between devices with their start and end apart: 18 -> 18, of which waited for: 12 -> 12; matrix products, arithmetic and copies ran while one was open for 0% -> 0% of each run, Pallas kernels for 6% -> 4%
where the time goes in v5:
time: 51.6 us; the launch traced here: 51.2 us
  starting transfers between devices  29.3 us (57%)
  waiting for transfers between devices  12.3 us (24%)
  Pallas kernels  8.72 us (17%)
  between operations  0.77 us (1%)
    ppermute x14, starting transfers between devices, exchange(): return lax.ppermute(block, AXES, pairs)  25.1 us
    ppermute x14, waiting for transfers between devices, exchange(): return lax.ppermute(block, AXES, pairs)  11.1 us
    pallas_call x1, Pallas kernels, local_products(): pl.pallas_call(kernel, out_shape=jax.ShapeDtypeStruct((width * columns //...  5.14 us
    ppermute x4, starting transfers between devices, other_core(): lax.ppermute(block, AXES, [(i, i ^ 1) for i in range(math.prod(SIZES))])  4.19 us
    pallas_call x1, Pallas kernels, factored(): pl.pallas_call(kernel, out_shape=(jax.ShapeDtypeStruct((width, width), jn...  2.27 us
    pallas_call x1, Pallas kernels, solved(): pl.pallas_call(kernel, out_shape=(jax.ShapeDtypeStruct(panel.shape, jnp.f...  1.31 us
    ppermute x4, waiting for transfers between devices, other_core(): lax.ppermute(block, AXES, [(i, i ^ 1) for i in range(math.prod(SIZES))])  1.16 us
  transfers between devices with their start and end apart: 18, of which 12 were waited for; matrix products, arithmetic and copies ran while one was open for 0% of the time, Pallas kernels for 4%

profile of v5, /device:TPU:1, one launch (start us, length us, event | category | flops | bytes accessed | tf_op | source)
XLA Modules:
  0.0 51.2 jit_solution(6692904206583096390)
XLA Ops:
  0.6 0.0 copy-start
  0.7 5.1 %local_products.1 = f32[512,128]{1,0:T(8,128)S(1)} custom-call(f32[64,2048]{1,0:T(8,128)} %panel_ref.1, f32[960,2048]{1,0:T(8,128)} %following_hbm.1), custom_call_target="tpu_custom_call" | custom-call | tf_op jit(solution)/shard_map/local_products/pallas_call | solution.py:73
  5.8 3.3 %collective-permute-start.9 = (f32[128,128]{1,0:T(8,128)S(1)}, f32[128,128]{1,0:T(8,128)S(1)}, u32[]{:S(2)}, u32[]{:S(2)}) collective-permute-start(f32[128,128]{1,0:T(8,128)S(1)} %get-tuple-element.13), channel_id=1, source_target_pairs={{0,1},{1,0},{2,3},{3,2},{4,5},{5,4},{6,7},{7,6},{8,9},{9,8},{10,11... | collective-permute-start | bytes 196616 | tf_op jit(solution)/shard_map/ppermute | solution.py:208
  9.2 0.1 collective-permute-start
  9.3 0.8 %collective-permute-done.9 = f32[128,128]{1,0:T(8,128)S(1)} collective-permute-done((f32[128,128]{1,0:T(8,128)S(1)}, f32[128,128]{1,0:T(8,128)S(1)}, u32[]{:S(2)}, u32[]{:S(2)}) %collective-permute-start.9) | collective-permute-done | bytes 65568 | tf_op jit(solution)/shard_map/ppermute | solution.py:208
  10.1 0.4 collective-permute-done
  10.5 0.1 collective-permute-start.1
  10.6 1.7 %collective-permute-start.10 = (f32[128,128]{1,0:T(8,128)S(1)}, f32[128,128]{1,0:T(8,128)S(1)}, u32[]{:S(2)}, u32[]{:S(2)}) collective-permute-start(f32[128,128]{1,0:T(8,128)S(1)} %get-tuple-element.11), channel_id=1, source_target_pairs={{0,3},{1,32},{2,35},{3,0},{4,7},{5,36},{6,39},{7,4},{8,11},{9,40},... | collective-permute-start | bytes 196616 | tf_op jit(solution)/shard_map/ppermute | solution.py:204
  12.3 2.2 %collective-permute-done.1 = f32[128,128]{1,0:T(8,128)S(1)} collective-permute-done((f32[128,128]{1,0:T(8,128)S(1)}, f32[128,128]{1,0:T(8,128)S(1)}, u32[]{:S(2)}, u32[]{:S(2)}) %collective-permute-start.1) | collective-permute-done | bytes 65568 | tf_op jit(solution)/shard_map/ppermute | solution.py:204
  14.5 0.1 collective-permute-start.2
  14.6 0.3 collective-permute-done.10
  14.9 1.5 %collective-permute-start.11 = (f32[128,128]{1,0:T(8,128)S(1)}, f32[128,128]{1,0:T(8,128)S(1)}, u32[]{:S(2)}, u32[]{:S(2)}) collective-permute-start(f32[128,128]{1,0:T(8,128)S(1)} %add.84), channel_id=1, source_target_pairs={{0,33},{1,2},{2,1},{3,34},{4,37},{5,6},{6,5},{7,38},{8,41},{9,10},... | collective-permute-start | bytes 196616 | tf_op jit(solution)/shard_map/ppermute | solution.py:204
  16.5 2.0 %collective-permute-done.2 = f32[128,128]{1,0:T(8,128)S(1)} collective-permute-done((f32[128,128]{1,0:T(8,128)S(1)}, f32[128,128]{1,0:T(8,128)S(1)}, u32[]{:S(2)}, u32[]{:S(2)}) %collective-permute-start.2) | collective-permute-done | bytes 65568 | tf_op jit(solution)/shard_map/ppermute | solution.py:204
  18.5 1.1 %collective-permute-start.3 = (f32[128,128]{1,0:T(8,128)S(1)}, f32[128,128]{1,0:T(8,128)S(1)}, u32[]{:S(2)}, u32[]{:S(2)}) collective-permute-start(f32[128,128]{1,0:T(8,128)S(1)} %add.77), channel_id=1, source_target_pairs={{0,17},{1,65},{2,66},{3,18},{4,21},{5,69},{6,70},{7,22},{8,25},{9,... | collective-permute-start | bytes 196616 | tf_op jit(solution)/shard_map/ppermute | solution.py:204
  19.6 0.0 collective-permute-done.11
  19.6 1.8 %collective-permute-start.12 = (f32[128,128]{1,0:T(8,128)S(1)}, f32[128,128]{1,0:T(8,128)S(1)}, u32[]{:S(2)}, u32[]{:S(2)}) collective-permute-start(f32[128,128]{1,0:T(8,128)S(1)} %add.85), channel_id=1, source_target_pairs={{0,17},{1,65},{2,66},{3,18},{4,21},{5,69},{6,70},{7,22},{8,25},{9,... | collective-permute-start | bytes 196616 | tf_op jit(solution)/shard_map/ppermute | solution.py:204
  21.4 2.0 %collective-permute-done.3 = f32[128,128]{1,0:T(8,128)S(1)} collective-permute-done((f32[128,128]{1,0:T(8,128)S(1)}, f32[128,128]{1,0:T(8,128)S(1)}, u32[]{:S(2)}, u32[]{:S(2)}) %collective-permute-start.3) | collective-permute-done | bytes 65568 | tf_op jit(solution)/shard_map/ppermute | solution.py:204
  23.3 0.2 collective-permute-start.4
  23.5 0.5 %collective-permute-done.12 = f32[128,128]{1,0:T(8,128)S(1)} collective-permute-done((f32[128,128]{1,0:T(8,128)S(1)}, f32[128,128]{1,0:T(8,128)S(1)}, u32[]{:S(2)}, u32[]{:S(2)}) %collective-permute-start.12) | collective-permute-done | bytes 65568 | tf_op jit(solution)/shard_map/ppermute | solution.py:204
  24.0 3.2 %collective-permute-start.13 = (f32[128,128]{1,0:T(8,128)S(1)}, f32[128,128]{1,0:T(8,128)S(1)}, u32[]{:S(2)}, u32[]{:S(2)}) collective-permute-start(f32[128,128]{1,0:T(8,128)S(1)} %add.86), channel_id=1, source_target_pairs={{0,7},{1,16},{2,19},{3,4},{4,3},{5,20},{6,23},{7,0},{8,15},{9,24},... | collective-permute-start | bytes 196616 | tf_op jit(solution)/shard_map/ppermute | solution.py:204
  27.2 0.2 collective-permute-done.4
  27.4 4.2 %collective-permute-start.5 = (f32[128,128]{1,0:T(8,128)S(1)}, f32[128,128]{1,0:T(8,128)S(1)}, u32[]{:S(2)}, u32[]{:S(2)}) collective-permute-start(f32[128,128]{1,0:T(8,128)S(1)} %add.79), channel_id=1, source_target_pairs={{0,25},{1,224},{2,227},{3,26},{4,29},{5,228},{6,231},{7,30},{8,17}... | collective-permute-start | bytes 196616 | tf_op jit(solution)/shard_map/ppermute | solution.py:204
  31.6 0.0 collective-permute-done.13
  31.6 1.4 %collective-permute-start.14 = (f32[128,128]{1,0:T(8,128)S(1)}, f32[128,128]{1,0:T(8,128)S(1)}, u32[]{:S(2)}, u32[]{:S(2)}) collective-permute-start(f32[128,128]{1,0:T(8,128)S(1)} %add.87), channel_id=1, source_target_pairs={{0,25},{1,224},{2,227},{3,26},{4,29},{5,228},{6,231},{7,30},{8,17}... | collective-permute-start | bytes 196616 | tf_op jit(solution)/shard_map/ppermute | solution.py:204
  33.0 0.8 %collective-permute-done.5 = f32[128,128]{1,0:T(8,128)S(1)} collective-permute-done((f32[128,128]{1,0:T(8,128)S(1)}, f32[128,128]{1,0:T(8,128)S(1)}, u32[]{:S(2)}, u32[]{:S(2)}) %collective-permute-start.5) | collective-permute-done | bytes 65568 | tf_op jit(solution)/shard_map/ppermute | solution.py:204
  33.8 2.3 %collective-permute-start.6 = (f32[128,128]{1,0:T(8,128)S(1)}, f32[128,128]{1,0:T(8,128)S(1)}, u32[]{:S(2)}, u32[]{:S(2)}) collective-permute-start(f32[128,128]{1,0:T(8,128)S(1)} %add.80), channel_id=1, source_target_pairs={{0,64},{1,6},{2,5},{3,67},{4,68},{5,2},{6,1},{7,71},{8,72},{9,14},... | collective-permute-start | bytes 196616 | tf_op jit(solution)/shard_map/ppermute | solution.py:204
  36.1 0.6 %collective-permute-done.14 = f32[128,128]{1,0:T(8,128)S(1)} collective-permute-done((f32[128,128]{1,0:T(8,128)S(1)}, f32[128,128]{1,0:T(8,128)S(1)}, u32[]{:S(2)}, u32[]{:S(2)}) %collective-permute-start.14) | collective-permute-done | bytes 65568 | tf_op jit(solution)/shard_map/ppermute | solution.py:204
  36.8 2.4 %collective-permute-start.15 = (f32[128,128]{1,0:T(8,128)S(1)}, f32[128,128]{1,0:T(8,128)S(1)}, u32[]{:S(2)}, u32[]{:S(2)}) collective-permute-start(f32[128,128]{1,0:T(8,128)S(1)} %add.88), channel_id=1, source_target_pairs={{0,64},{1,6},{2,5},{3,67},{4,68},{5,2},{6,1},{7,71},{8,72},{9,14},... | collective-permute-start | bytes 196616 | tf_op jit(solution)/shard_map/ppermute | solution.py:204
  39.2 0.0 collective-permute-done.6
  39.2 3.3 %collective-permute-start.7 = (f32[128,128]{1,0:T(8,128)S(1)}, f32[128,128]{1,0:T(8,128)S(1)}, u32[]{:S(2)}, u32[]{:S(2)}) collective-permute-start(f32[128,128]{1,0:T(8,128)S(1)} %add.81), channel_id=1, source_target_pairs={{0,225},{1,24},{2,27},{3,226},{4,229},{5,28},{6,31},{7,230},{8,233... | collective-permute-start | bytes 196616 | tf_op jit(solution)/shard_map/ppermute | solution.py:204
  42.5 0.0 collective-permute-done.15
  42.5 1.9 %collective-permute-start.16 = (f32[128,128]{1,0:T(8,128)S(1)}, f32[128,128]{1,0:T(8,128)S(1)}, u32[]{:S(2)}, u32[]{:S(2)}) collective-permute-start(f32[128,128]{1,0:T(8,128)S(1)} %add.89), channel_id=1, source_target_pairs={{0,225},{1,24},{2,27},{3,226},{4,229},{5,28},{6,31},{7,230},{8,233... | collective-permute-start | bytes 196616 | tf_op jit(solution)/shard_map/ppermute | solution.py:204
  44.4 0.3 collective-permute-done.7
  44.7 0.6 %collective-permute-start.8 = (f32[128,128]{1,0:T(8,128)S(1)}, f32[128,128]{1,0:T(8,128)S(1)}, u32[]{:S(2)}, u32[]{:S(2)}) collective-permute-start(f32[128,128]{1,0:T(8,128)S(1)} %add.82.own_ref.own1), channel_id=1, source_target_pairs={{0,1},{1,0},{2,3},{3,2},{4,5},{5,4},{6,7},{7,6},{8,9},{9,8},{10,11... | collective-permute-start | bytes 196616 | tf_op jit(solution)/shard_map/ppermute | solution.py:208
  45.3 2.2 %collective-permute-done.16 = f32[128,128]{1,0:T(8,128)S(1)} collective-permute-done((f32[128,128]{1,0:T(8,128)S(1)}, f32[128,128]{1,0:T(8,128)S(1)}, u32[]{:S(2)}, u32[]{:S(2)}) %collective-permute-start.16) | collective-permute-done | bytes 65568 | tf_op jit(solution)/shard_map/ppermute | solution.py:204
  47.5 0.2 collective-permute-start.17
  47.6 0.0 collective-permute-done.8.other_ref.other1
  47.6 2.3 %factored.1 = (f32[64,64]{1,0:T(8,128)}, bf16[64,384]{1,0:T(8,128)(2,1)S(1)}) custom-call(s32[1]{0:T(128)} %bitcast.half_ref, f32[128,128]{1,0:T(8,128)S(1)} %add.82.own_ref.own1, f32[128,128]{1,0:T(8,128)S(1)} %collective-permute-done.8.other_ref.other1), custom_call_target="tpu_custom_call" | custom-call | tf_op jit(solution)/shard_map/factored/pallas_call | solution.py:137
  49.9 0.0 collective-permute-done.17.other0
  49.9 0.0 copy-done
  49.9 1.3 %solved.1 = (f32[64,2048]{1,0:T(8,128)}, f32[64,960]{1,0:T(8,128)}) custom-call(s32[1]{0:T(128)} %bitcast.half_ref, bf16[64,384]{1,0:T(8,128)(2,1)S(1)} %get-tuple-element.7.inverse_ref, f32[64,2048]{1,0:T(8,128)S(1)} %copy-done, f32[128,128]{1,0:T(8,128)S(1)} %add.90.own0, f32[128,128]{1,0:T(8,128)S(1)} %collective-permute-done.17.other0, ...), custom_call_target="tpu_custom_call" | custom-call | tf_op jit(solution)/shard_map/solved/pallas_call | solution.py:173
  (16 shorter events, 0.2 us)
Async XLA Ops:
  0.6 49.3 %copy-start = (f32[64,2048]{1,0:T(8,128)S(1)}, f32[64,2048]{1,0:T(8,128)}, u32[]{:S(2)}) copy-start(f32[64,2048]{1,0:T(8,128)} %panel_ref.1) | copy-start | bytes 1572868
  5.8 4.2 %collective-permute-start.9 = (f32[128,128]{1,0:T(8,128)S(1)}, f32[128,128]{1,0:T(8,128)S(1)}, u32[]{:S(2)}, u32[]{:S(2)}) collective-permute-start(f32[128,128]{1,0:T(8,128)S(1)} %get-tuple-element.13), channel_id=1, source_target_pairs={{0,1},{1,0},{2,3},{3,2},{4,5},{5,4},{6,7},{7,6},{8,9},{9,8},{10,11... | collective-permute-start | bytes 196616 | tf_op jit(solution)/shard_map/ppermute | solution.py:208
  9.2 1.3 %collective-permute-start = (f32[128,128]{1,0:T(8,128)S(1)}, f32[128,128]{1,0:T(8,128)S(1)}, u32[]{:S(2)}, u32[]{:S(2)}) collective-permute-start(f32[128,128]{1,0:T(8,128)S(1)} %get-tuple-element.14), channel_id=1, source_target_pairs={{0,1},{1,0},{2,3},{3,2},{4,5},{5,4},{6,7},{7,6},{8,9},{9,8},{10,11... | collective-permute-start | bytes 196616 | tf_op jit(solution)/shard_map/ppermute | solution.py:208
  10.5 4.1 %collective-permute-start.1 = (f32[128,128]{1,0:T(8,128)S(1)}, f32[128,128]{1,0:T(8,128)S(1)}, u32[]{:S(2)}, u32[]{:S(2)}) collective-permute-start(f32[128,128]{1,0:T(8,128)S(1)} %get-tuple-element.12), channel_id=1, source_target_pairs={{0,3},{1,32},{2,35},{3,0},{4,7},{5,36},{6,39},{7,4},{8,11},{9,40},... | collective-permute-start | bytes 196616 | tf_op jit(solution)/shard_map/ppermute | solution.py:204
  10.6 4.4 %collective-permute-start.10 = (f32[128,128]{1,0:T(8,128)S(1)}, f32[128,128]{1,0:T(8,128)S(1)}, u32[]{:S(2)}, u32[]{:S(2)}) collective-permute-start(f32[128,128]{1,0:T(8,128)S(1)} %get-tuple-element.11), channel_id=1, source_target_pairs={{0,3},{1,32},{2,35},{3,0},{4,7},{5,36},{6,39},{7,4},{8,11},{9,40},... | collective-permute-start | bytes 196616 | tf_op jit(solution)/shard_map/ppermute | solution.py:204
  14.5 3.9 %collective-permute-start.2 = (f32[128,128]{1,0:T(8,128)S(1)}, f32[128,128]{1,0:T(8,128)S(1)}, u32[]{:S(2)}, u32[]{:S(2)}) collective-permute-start(f32[128,128]{1,0:T(8,128)S(1)} %add.76), channel_id=1, source_target_pairs={{0,33},{1,2},{2,1},{3,34},{4,37},{5,6},{6,5},{7,38},{8,41},{9,10},... | collective-permute-start | bytes 196616 | tf_op jit(solution)/shard_map/ppermute | solution.py:204
  14.9 4.6 %collective-permute-start.11 = (f32[128,128]{1,0:T(8,128)S(1)}, f32[128,128]{1,0:T(8,128)S(1)}, u32[]{:S(2)}, u32[]{:S(2)}) collective-permute-start(f32[128,128]{1,0:T(8,128)S(1)} %add.84), channel_id=1, source_target_pairs={{0,33},{1,2},{2,1},{3,34},{4,37},{5,6},{6,5},{7,38},{8,41},{9,10},... | collective-permute-start | bytes 196616 | tf_op jit(solution)/shard_map/ppermute | solution.py:204
  18.5 4.8 %collective-permute-start.3 = (f32[128,128]{1,0:T(8,128)S(1)}, f32[128,128]{1,0:T(8,128)S(1)}, u32[]{:S(2)}, u32[]{:S(2)}) collective-permute-start(f32[128,128]{1,0:T(8,128)S(1)} %add.77), channel_id=1, source_target_pairs={{0,17},{1,65},{2,66},{3,18},{4,21},{5,69},{6,70},{7,22},{8,25},{9,... | collective-permute-start | bytes 196616 | tf_op jit(solution)/shard_map/ppermute | solution.py:204
  19.6 4.4 %collective-permute-start.12 = (f32[128,128]{1,0:T(8,128)S(1)}, f32[128,128]{1,0:T(8,128)S(1)}, u32[]{:S(2)}, u32[]{:S(2)}) collective-permute-start(f32[128,128]{1,0:T(8,128)S(1)} %add.85), channel_id=1, source_target_pairs={{0,17},{1,65},{2,66},{3,18},{4,21},{5,69},{6,70},{7,22},{8,25},{9,... | collective-permute-start | bytes 196616 | tf_op jit(solution)/shard_map/ppermute | solution.py:204
  23.3 4.1 %collective-permute-start.4 = (f32[128,128]{1,0:T(8,128)S(1)}, f32[128,128]{1,0:T(8,128)S(1)}, u32[]{:S(2)}, u32[]{:S(2)}) collective-permute-start(f32[128,128]{1,0:T(8,128)S(1)} %add.78), channel_id=1, source_target_pairs={{0,7},{1,16},{2,19},{3,4},{4,3},{5,20},{6,23},{7,0},{8,15},{9,24},... | collective-permute-start | bytes 196616 | tf_op jit(solution)/shard_map/ppermute | solution.py:204
  24.0 7.6 %collective-permute-start.13 = (f32[128,128]{1,0:T(8,128)S(1)}, f32[128,128]{1,0:T(8,128)S(1)}, u32[]{:S(2)}, u32[]{:S(2)}) collective-permute-start(f32[128,128]{1,0:T(8,128)S(1)} %add.86), channel_id=1, source_target_pairs={{0,7},{1,16},{2,19},{3,4},{4,3},{5,20},{6,23},{7,0},{8,15},{9,24},... | collective-permute-start | bytes 196616 | tf_op jit(solution)/shard_map/ppermute | solution.py:204
  27.4 6.4 %collective-permute-start.5 = (f32[128,128]{1,0:T(8,128)S(1)}, f32[128,128]{1,0:T(8,128)S(1)}, u32[]{:S(2)}, u32[]{:S(2)}) collective-permute-start(f32[128,128]{1,0:T(8,128)S(1)} %add.79), channel_id=1, source_target_pairs={{0,25},{1,224},{2,227},{3,26},{4,29},{5,228},{6,231},{7,30},{8,17}... | collective-permute-start | bytes 196616 | tf_op jit(solution)/shard_map/ppermute | solution.py:204
  31.6 5.1 %collective-permute-start.14 = (f32[128,128]{1,0:T(8,128)S(1)}, f32[128,128]{1,0:T(8,128)S(1)}, u32[]{:S(2)}, u32[]{:S(2)}) collective-permute-start(f32[128,128]{1,0:T(8,128)S(1)} %add.87), channel_id=1, source_target_pairs={{0,25},{1,224},{2,227},{3,26},{4,29},{5,228},{6,231},{7,30},{8,17}... | collective-permute-start | bytes 196616 | tf_op jit(solution)/shard_map/ppermute | solution.py:204
  33.8 5.4 %collective-permute-start.6 = (f32[128,128]{1,0:T(8,128)S(1)}, f32[128,128]{1,0:T(8,128)S(1)}, u32[]{:S(2)}, u32[]{:S(2)}) collective-permute-start(f32[128,128]{1,0:T(8,128)S(1)} %add.80), channel_id=1, source_target_pairs={{0,64},{1,6},{2,5},{3,67},{4,68},{5,2},{6,1},{7,71},{8,72},{9,14},... | collective-permute-start | bytes 196616 | tf_op jit(solution)/shard_map/ppermute | solution.py:204
  36.8 5.7 %collective-permute-start.15 = (f32[128,128]{1,0:T(8,128)S(1)}, f32[128,128]{1,0:T(8,128)S(1)}, u32[]{:S(2)}, u32[]{:S(2)}) collective-permute-start(f32[128,128]{1,0:T(8,128)S(1)} %add.88), channel_id=1, source_target_pairs={{0,64},{1,6},{2,5},{3,67},{4,68},{5,2},{6,1},{7,71},{8,72},{9,14},... | collective-permute-start | bytes 196616 | tf_op jit(solution)/shard_map/ppermute | solution.py:204
  39.2 5.5 %collective-permute-start.7 = (f32[128,128]{1,0:T(8,128)S(1)}, f32[128,128]{1,0:T(8,128)S(1)}, u32[]{:S(2)}, u32[]{:S(2)}) collective-permute-start(f32[128,128]{1,0:T(8,128)S(1)} %add.81), channel_id=1, source_target_pairs={{0,225},{1,24},{2,27},{3,226},{4,229},{5,28},{6,31},{7,230},{8,233... | collective-permute-start | bytes 196616 | tf_op jit(solution)/shard_map/ppermute | solution.py:204
  42.5 5.0 %collective-permute-start.16 = (f32[128,128]{1,0:T(8,128)S(1)}, f32[128,128]{1,0:T(8,128)S(1)}, u32[]{:S(2)}, u32[]{:S(2)}) collective-permute-start(f32[128,128]{1,0:T(8,128)S(1)} %add.89), channel_id=1, source_target_pairs={{0,225},{1,24},{2,27},{3,226},{4,229},{5,28},{6,31},{7,230},{8,233... | collective-permute-start | bytes 196616 | tf_op jit(solution)/shard_map/ppermute | solution.py:204
  44.7 2.9 %collective-permute-start.8 = (f32[128,128]{1,0:T(8,128)S(1)}, f32[128,128]{1,0:T(8,128)S(1)}, u32[]{:S(2)}, u32[]{:S(2)}) collective-permute-start(f32[128,128]{1,0:T(8,128)S(1)} %add.82.own_ref.own1), channel_id=1, source_target_pairs={{0,1},{1,0},{2,3},{3,2},{4,5},{5,4},{6,7},{7,6},{8,9},{9,8},{10,11... | collective-permute-start | bytes 196616 | tf_op jit(solution)/shard_map/ppermute | solution.py:208
  47.5 2.5 %collective-permute-start.17 = (f32[128,128]{1,0:T(8,128)S(1)}, f32[128,128]{1,0:T(8,128)S(1)}, u32[]{:S(2)}, u32[]{:S(2)}) collective-permute-start(f32[128,128]{1,0:T(8,128)S(1)} %add.90.own0), channel_id=1, source_target_pairs={{0,1},{1,0},{2,3},{3,2},{4,5},{5,4},{6,7},{7,6},{8,9},{9,8},{10,11... | collective-permute-start | bytes 196616 | tf_op jit(solution)/shard_map/ppermute | solution.py:208

commit v6 on v5

--- a/solution.py
+++ b/solution.py
@@ -96,7 +96,7 @@
         corner = [[columns[j][i : i + 1] for j in range(BLOCK)] for i in range(BLOCK)]
         inverses = []
         for j in range(BLOCK):
-            inverses.append(1.0 / corner[j][j])
+            inverses.append(pl.reciprocal(corner[j][j]))
             for i in range(j + 1, BLOCK):
                 factor = corner[i][j] * inverses[j]
                 rows[i] = rows[i] - factor * rows[j]
@@ -222,7 +222,8 @@
     mine = lax.dynamic_index_in_dim(halves, half, keepdims=False)
     theirs = lax.dynamic_index_in_dim(halves, 1 - half, keepdims=False)
     one = mine[1] + other_core(theirs[1])
-    two = mine[0] + other_core(theirs[0])
+    sent, _ = lax.optimization_barrier((theirs[0], one))
+    two = mine[0] + other_core(sent)
     for first, second in ROUNDS:
         one = one + exchange(one, *first)
         two = two + exchange(two, *second)

time: 51.6 us -> 51.6 us (level)
  starting transfers between devices: 29.3 us -> 28.1 us
  waiting for transfers between devices: 12.3 us -> 13.5 us
    ppermute x14, starting transfers between devices: 25.1 us -> 23.6 us  [exchange(): return lax.ppermute(block, AXES, pairs)]
    ppermute x4, waiting for transfers between devices: 1.16 us -> 1.81 us  [other_core(): lax.ppermute(block, AXES, [(i, i ^ 1) for i in range(math.prod(SIZES))])]
    ppermute x14, waiting for transfers between devices: 11.1 us -> 11.7 us  [exchange(): return lax.ppermute(block, AXES, pairs)]
where the time goes in v6:
time: 51.6 us; the launch traced here: 51.2 us
  starting transfers between devices  28.1 us (54%)
  waiting for transfers between devices  13.5 us (26%)
  Pallas kernels  8.72 us (17%)
  between operations  0.77 us (1%)
    ppermute x14, starting transfers between devices, exchange(): return lax.ppermute(block, AXES, pairs)  23.6 us
    ppermute x14, waiting for transfers between devices, exchange(): return lax.ppermute(block, AXES, pairs)  11.7 us
    pallas_call x1, Pallas kernels, local_products(): pl.pallas_call(kernel, out_shape=jax.ShapeDtypeStruct((width * columns //...  5.14 us
    ppermute x4, starting transfers between devices, other_core(): lax.ppermute(block, AXES, [(i, i ^ 1) for i in range(math.prod(SIZES))])  4.53 us
    pallas_call x1, Pallas kernels, factored(): pl.pallas_call(kernel, out_shape=(jax.ShapeDtypeStruct((width, width), jn...  2.27 us
    ppermute x4, waiting for transfers between devices, other_core(): lax.ppermute(block, AXES, [(i, i ^ 1) for i in range(math.prod(SIZES))])  1.81 us
    pallas_call x1, Pallas kernels, solved(): pl.pallas_call(kernel, out_shape=(jax.ShapeDtypeStruct(panel.shape, jnp.f...  1.31 us
  transfers between devices with their start and end apart: 18, of which 12 were waited for; matrix products, arithmetic and copies ran while one was open for 0% of the time, Pallas kernels for 4%

profile of v6, /device:TPU:1, one launch (start us, length us, event | category | flops | bytes accessed | tf_op | source)
XLA Modules:
  0.0 51.2 jit_solution(17109981664504257397)
XLA Ops:
  0.6 0.0 copy-start
  0.7 5.1 %local_products.1 = f32[512,128]{1,0:T(8,128)S(1)} custom-call(f32[64,2048]{1,0:T(8,128)} %panel_ref.1, f32[960,2048]{1,0:T(8,128)} %following_hbm.1), custom_call_target="tpu_custom_call" | custom-call | tf_op jit(solution)/shard_map/local_products/pallas_call | solution.py:73
  5.8 3.3 %collective-permute-start = (f32[128,128]{1,0:T(8,128)S(1)}, f32[128,128]{1,0:T(8,128)S(1)}, u32[]{:S(2)}, u32[]{:S(2)}) collective-permute-start(f32[128,128]{1,0:T(8,128)S(1)} %get-tuple-element.14), channel_id=1, source_target_pairs={{0,1},{1,0},{2,3},{3,2},{4,5},{5,4},{6,7},{7,6},{8,9},{9,8},{10,11... | collective-permute-start | bytes 196616 | tf_op jit(solution)/shard_map/ppermute | solution.py:208
  9.2 0.9 %collective-permute-done = f32[128,128]{1,0:T(8,128)S(1)} collective-permute-done((f32[128,128]{1,0:T(8,128)S(1)}, f32[128,128]{1,0:T(8,128)S(1)}, u32[]{:S(2)}, u32[]{:S(2)}) %collective-permute-start) | collective-permute-done | bytes 65568 | tf_op jit(solution)/shard_map/ppermute | solution.py:208
  10.1 0.4 collective-permute-start.9
  10.5 0.0 collective-permute-start.1
  10.5 0.9 %collective-permute-done.9 = f32[128,128]{1,0:T(8,128)S(1)} collective-permute-done((f32[128,128]{1,0:T(8,128)S(1)}, f32[128,128]{1,0:T(8,128)S(1)}, u32[]{:S(2)}, u32[]{:S(2)}) %collective-permute-start.9) | collective-permute-done | bytes 65568 | tf_op jit(solution)/shard_map/ppermute | solution.py:208
  11.4 0.9 %collective-permute-start.10 = (f32[128,128]{1,0:T(8,128)S(1)}, f32[128,128]{1,0:T(8,128)S(1)}, u32[]{:S(2)}, u32[]{:S(2)}) collective-permute-start(f32[128,128]{1,0:T(8,128)S(1)} %fusion), channel_id=1, source_target_pairs={{0,3},{1,32},{2,35},{3,0},{4,7},{5,36},{6,39},{7,4},{8,11},{9,40},... | collective-permute-start | bytes 196616 | tf_op jit(solution)/shard_map/ppermute | solution.py:204
  12.4 2.1 %collective-permute-done.1 = f32[128,128]{1,0:T(8,128)S(1)} collective-permute-done((f32[128,128]{1,0:T(8,128)S(1)}, f32[128,128]{1,0:T(8,128)S(1)}, u32[]{:S(2)}, u32[]{:S(2)}) %collective-permute-start.1) | collective-permute-done | bytes 65568 | tf_op jit(solution)/shard_map/ppermute | solution.py:204
  14.5 0.1 collective-permute-start.2
  14.6 0.6 %collective-permute-done.10 = f32[128,128]{1,0:T(8,128)S(1)} collective-permute-done((f32[128,128]{1,0:T(8,128)S(1)}, f32[128,128]{1,0:T(8,128)S(1)}, u32[]{:S(2)}, u32[]{:S(2)}) %collective-permute-start.10) | collective-permute-done | bytes 65568 | tf_op jit(solution)/shard_map/ppermute | solution.py:204
  15.2 1.2 %collective-permute-start.11 = (f32[128,128]{1,0:T(8,128)S(1)}, f32[128,128]{1,0:T(8,128)S(1)}, u32[]{:S(2)}, u32[]{:S(2)}) collective-permute-start(f32[128,128]{1,0:T(8,128)S(1)} %add.84), channel_id=1, source_target_pairs={{0,33},{1,2},{2,1},{3,34},{4,37},{5,6},{6,5},{7,38},{8,41},{9,10},... | collective-permute-start | bytes 196616 | tf_op jit(solution)/shard_map/ppermute | solution.py:204
  16.5 2.1 %collective-permute-done.2 = f32[128,128]{1,0:T(8,128)S(1)} collective-permute-done((f32[128,128]{1,0:T(8,128)S(1)}, f32[128,128]{1,0:T(8,128)S(1)}, u32[]{:S(2)}, u32[]{:S(2)}) %collective-permute-start.2) | collective-permute-done | bytes 65568 | tf_op jit(solution)/shard_map/ppermute | solution.py:204
  18.6 0.9 %collective-permute-start.3 = (f32[128,128]{1,0:T(8,128)S(1)}, f32[128,128]{1,0:T(8,128)S(1)}, u32[]{:S(2)}, u32[]{:S(2)}) collective-permute-start(f32[128,128]{1,0:T(8,128)S(1)} %add.77), channel_id=1, source_target_pairs={{0,17},{1,65},{2,66},{3,18},{4,21},{5,69},{6,70},{7,22},{8,25},{9,... | collective-permute-start | bytes 196616 | tf_op jit(solution)/shard_map/ppermute | solution.py:204
  19.6 0.0 collective-permute-done.11
  19.6 1.8 %collective-permute-start.12 = (f32[128,128]{1,0:T(8,128)S(1)}, f32[128,128]{1,0:T(8,128)S(1)}, u32[]{:S(2)}, u32[]{:S(2)}) collective-permute-start(f32[128,128]{1,0:T(8,128)S(1)} %add.85), channel_id=1, source_target_pairs={{0,17},{1,65},{2,66},{3,18},{4,21},{5,69},{6,70},{7,22},{8,25},{9,... | collective-permute-start | bytes 196616 | tf_op jit(solution)/shard_map/ppermute | solution.py:204
  21.4 2.0 %collective-permute-done.3 = f32[128,128]{1,0:T(8,128)S(1)} collective-permute-done((f32[128,128]{1,0:T(8,128)S(1)}, f32[128,128]{1,0:T(8,128)S(1)}, u32[]{:S(2)}, u32[]{:S(2)}) %collective-permute-start.3) | collective-permute-done | bytes 65568 | tf_op jit(solution)/shard_map/ppermute | solution.py:204
  23.4 0.1 collective-permute-start.4
  23.5 0.6 %collective-permute-done.12 = f32[128,128]{1,0:T(8,128)S(1)} collective-permute-done((f32[128,128]{1,0:T(8,128)S(1)}, f32[128,128]{1,0:T(8,128)S(1)}, u32[]{:S(2)}, u32[]{:S(2)}) %collective-permute-start.12) | collective-permute-done | bytes 65568 | tf_op jit(solution)/shard_map/ppermute | solution.py:204
  24.1 3.0 %collective-permute-start.13 = (f32[128,128]{1,0:T(8,128)S(1)}, f32[128,128]{1,0:T(8,128)S(1)}, u32[]{:S(2)}, u32[]{:S(2)}) collective-permute-start(f32[128,128]{1,0:T(8,128)S(1)} %add.86), channel_id=1, source_target_pairs={{0,7},{1,16},{2,19},{3,4},{4,3},{5,20},{6,23},{7,0},{8,15},{9,24},... | collective-permute-start | bytes 196616 | tf_op jit(solution)/shard_map/ppermute | solution.py:204
  27.2 0.3 collective-permute-done.4
  27.5 4.1 %collective-permute-start.5 = (f32[128,128]{1,0:T(8,128)S(1)}, f32[128,128]{1,0:T(8,128)S(1)}, u32[]{:S(2)}, u32[]{:S(2)}) collective-permute-start(f32[128,128]{1,0:T(8,128)S(1)} %add.79), channel_id=1, source_target_pairs={{0,25},{1,224},{2,227},{3,26},{4,29},{5,228},{6,231},{7,30},{8,17}... | collective-permute-start | bytes 196616 | tf_op jit(solution)/shard_map/ppermute | solution.py:204
  31.6 0.0 collective-permute-done.13
  31.6 1.4 %collective-permute-start.14 = (f32[128,128]{1,0:T(8,128)S(1)}, f32[128,128]{1,0:T(8,128)S(1)}, u32[]{:S(2)}, u32[]{:S(2)}) collective-permute-start(f32[128,128]{1,0:T(8,128)S(1)} %add.87), channel_id=1, source_target_pairs={{0,25},{1,224},{2,227},{3,26},{4,29},{5,228},{6,231},{7,30},{8,17}... | collective-permute-start | bytes 196616 | tf_op jit(solution)/shard_map/ppermute | solution.py:204
  33.0 0.8 %collective-permute-done.5 = f32[128,128]{1,0:T(8,128)S(1)} collective-permute-done((f32[128,128]{1,0:T(8,128)S(1)}, f32[128,128]{1,0:T(8,128)S(1)}, u32[]{:S(2)}, u32[]{:S(2)}) %collective-permute-start.5) | collective-permute-done | bytes 65568 | tf_op jit(solution)/shard_map/ppermute | solution.py:204
  33.8 2.3 %collective-permute-start.6 = (f32[128,128]{1,0:T(8,128)S(1)}, f32[128,128]{1,0:T(8,128)S(1)}, u32[]{:S(2)}, u32[]{:S(2)}) collective-permute-start(f32[128,128]{1,0:T(8,128)S(1)} %add.80), channel_id=1, source_target_pairs={{0,64},{1,6},{2,5},{3,67},{4,68},{5,2},{6,1},{7,71},{8,72},{9,14},... | collective-permute-start | bytes 196616 | tf_op jit(solution)/shard_map/ppermute | solution.py:204
  36.1 0.6 %collective-permute-done.14 = f32[128,128]{1,0:T(8,128)S(1)} collective-permute-done((f32[128,128]{1,0:T(8,128)S(1)}, f32[128,128]{1,0:T(8,128)S(1)}, u32[]{:S(2)}, u32[]{:S(2)}) %collective-permute-start.14) | collective-permute-done | bytes 65568 | tf_op jit(solution)/shard_map/ppermute | solution.py:204
  36.8 2.4 %collective-permute-start.15 = (f32[128,128]{1,0:T(8,128)S(1)}, f32[128,128]{1,0:T(8,128)S(1)}, u32[]{:S(2)}, u32[]{:S(2)}) collective-permute-start(f32[128,128]{1,0:T(8,128)S(1)} %add.88), channel_id=1, source_target_pairs={{0,64},{1,6},{2,5},{3,67},{4,68},{5,2},{6,1},{7,71},{8,72},{9,14},... | collective-permute-start | bytes 196616 | tf_op jit(solution)/shard_map/ppermute | solution.py:204
  39.2 0.0 collective-permute-done.6
  39.2 3.3 %collective-permute-start.7 = (f32[128,128]{1,0:T(8,128)S(1)}, f32[128,128]{1,0:T(8,128)S(1)}, u32[]{:S(2)}, u32[]{:S(2)}) collective-permute-start(f32[128,128]{1,0:T(8,128)S(1)} %add.81), channel_id=1, source_target_pairs={{0,225},{1,24},{2,27},{3,226},{4,229},{5,28},{6,31},{7,230},{8,233... | collective-permute-start | bytes 196616 | tf_op jit(solution)/shard_map/ppermute | solution.py:204
  42.5 0.0 collective-permute-done.15
  42.5 1.9 %collective-permute-start.16 = (f32[128,128]{1,0:T(8,128)S(1)}, f32[128,128]{1,0:T(8,128)S(1)}, u32[]{:S(2)}, u32[]{:S(2)}) collective-permute-start(f32[128,128]{1,0:T(8,128)S(1)} %add.89), channel_id=1, source_target_pairs={{0,225},{1,24},{2,27},{3,226},{4,229},{5,28},{6,31},{7,230},{8,233... | collective-permute-start | bytes 196616 | tf_op jit(solution)/shard_map/ppermute | solution.py:204
  44.4 0.3 collective-permute-done.7
  44.7 0.6 %collective-permute-start.8 = (f32[128,128]{1,0:T(8,128)S(1)}, f32[128,128]{1,0:T(8,128)S(1)}, u32[]{:S(2)}, u32[]{:S(2)}) collective-permute-start(f32[128,128]{1,0:T(8,128)S(1)} %add.82.own_ref.own1), channel_id=1, source_target_pairs={{0,1},{1,0},{2,3},{3,2},{4,5},{5,4},{6,7},{7,6},{8,9},{9,8},{10,11... | collective-permute-start | bytes 196616 | tf_op jit(solution)/shard_map/ppermute | solution.py:208
  45.3 2.2 %collective-permute-done.16 = f32[128,128]{1,0:T(8,128)S(1)} collective-permute-done((f32[128,128]{1,0:T(8,128)S(1)}, f32[128,128]{1,0:T(8,128)S(1)}, u32[]{:S(2)}, u32[]{:S(2)}) %collective-permute-start.16) | collective-permute-done | bytes 65568 | tf_op jit(solution)/shard_map/ppermute | solution.py:204
  47.5 0.2 collective-permute-start.17
  47.6 0.0 collective-permute-done.8.other_ref.other1
  47.6 2.3 %factored.1 = (f32[64,64]{1,0:T(8,128)}, bf16[64,384]{1,0:T(8,128)(2,1)S(1)}) custom-call(s32[1]{0:T(128)} %bitcast.half_ref, f32[128,128]{1,0:T(8,128)S(1)} %add.82.own_ref.own1, f32[128,128]{1,0:T(8,128)S(1)} %collective-permute-done.8.other_ref.other1), custom_call_target="tpu_custom_call" | custom-call | tf_op jit(solution)/shard_map/factored/pallas_call | solution.py:137
  49.9 0.0 collective-permute-done.17.other0
  49.9 0.0 copy-done
  49.9 1.3 %solved.1 = (f32[64,2048]{1,0:T(8,128)}, f32[64,960]{1,0:T(8,128)}) custom-call(s32[1]{0:T(128)} %bitcast.half_ref, bf16[64,384]{1,0:T(8,128)(2,1)S(1)} %get-tuple-element.8.inverse_ref, f32[64,2048]{1,0:T(8,128)S(1)} %copy-done, f32[128,128]{1,0:T(8,128)S(1)} %add.90.own0, f32[128,128]{1,0:T(8,128)S(1)} %collective-permute-done.17.other0, ...), custom_call_target="tpu_custom_call" | custom-call | tf_op jit(solution)/shard_map/solved/pallas_call | solution.py:173
  (17 shorter events, 0.2 us)
Async XLA Ops:
  0.6 49.3 %copy-start = (f32[64,2048]{1,0:T(8,128)S(1)}, f32[64,2048]{1,0:T(8,128)}, u32[]{:S(2)}) copy-start(f32[64,2048]{1,0:T(8,128)} %panel_ref.1) | copy-start | bytes 1572868
  5.8 4.2 %collective-permute-start = (f32[128,128]{1,0:T(8,128)S(1)}, f32[128,128]{1,0:T(8,128)S(1)}, u32[]{:S(2)}, u32[]{:S(2)}) collective-permute-start(f32[128,128]{1,0:T(8,128)S(1)} %get-tuple-element.14), channel_id=1, source_target_pairs={{0,1},{1,0},{2,3},{3,2},{4,5},{5,4},{6,7},{7,6},{8,9},{9,8},{10,11... | collective-permute-start | bytes 196616 | tf_op jit(solution)/shard_map/ppermute | solution.py:208
  10.1 1.3 %collective-permute-start.9 = (f32[128,128]{1,0:T(8,128)S(1)}, f32[128,128]{1,0:T(8,128)S(1)}, u32[]{:S(2)}, u32[]{:S(2)}) collective-permute-start(f32[128,128]{1,0:T(8,128)S(1)} %get-tuple-element.9), channel_id=1, source_target_pairs={{0,1},{1,0},{2,3},{3,2},{4,5},{5,4},{6,7},{7,6},{8,9},{9,8},{10,11... | collective-permute-start | bytes 196616 | tf_op jit(solution)/shard_map/ppermute | solution.py:208
  10.5 4.0 %collective-permute-start.1 = (f32[128,128]{1,0:T(8,128)S(1)}, f32[128,128]{1,0:T(8,128)S(1)}, u32[]{:S(2)}, u32[]{:S(2)}) collective-permute-start(f32[128,128]{1,0:T(8,128)S(1)} %fusion.1), channel_id=1, source_target_pairs={{0,3},{1,32},{2,35},{3,0},{4,7},{5,36},{6,39},{7,4},{8,11},{9,40},... | collective-permute-start | bytes 196616 | tf_op jit(solution)/shard_map/ppermute | solution.py:204
  11.4 3.8 %collective-permute-start.10 = (f32[128,128]{1,0:T(8,128)S(1)}, f32[128,128]{1,0:T(8,128)S(1)}, u32[]{:S(2)}, u32[]{:S(2)}) collective-permute-start(f32[128,128]{1,0:T(8,128)S(1)} %fusion), channel_id=1, source_target_pairs={{0,3},{1,32},{2,35},{3,0},{4,7},{5,36},{6,39},{7,4},{8,11},{9,40},... | collective-permute-start | bytes 196616 | tf_op jit(solution)/shard_map/ppermute | solution.py:204
  14.5 4.1 %collective-permute-start.2 = (f32[128,128]{1,0:T(8,128)S(1)}, f32[128,128]{1,0:T(8,128)S(1)}, u32[]{:S(2)}, u32[]{:S(2)}) collective-permute-start(f32[128,128]{1,0:T(8,128)S(1)} %add.76), channel_id=1, source_target_pairs={{0,33},{1,2},{2,1},{3,34},{4,37},{5,6},{6,5},{7,38},{8,41},{9,10},... | collective-permute-start | bytes 196616 | tf_op jit(solution)/shard_map/ppermute | solution.py:204
  15.2 4.3 %collective-permute-start.11 = (f32[128,128]{1,0:T(8,128)S(1)}, f32[128,128]{1,0:T(8,128)S(1)}, u32[]{:S(2)}, u32[]{:S(2)}) collective-permute-start(f32[128,128]{1,0:T(8,128)S(1)} %add.84), channel_id=1, source_target_pairs={{0,33},{1,2},{2,1},{3,34},{4,37},{5,6},{6,5},{7,38},{8,41},{9,10},... | collective-permute-start | bytes 196616 | tf_op jit(solution)/shard_map/ppermute | solution.py:204
  18.6 4.8 %collective-permute-start.3 = (f32[128,128]{1,0:T(8,128)S(1)}, f32[128,128]{1,0:T(8,128)S(1)}, u32[]{:S(2)}, u32[]{:S(2)}) collective-permute-start(f32[128,128]{1,0:T(8,128)S(1)} %add.77), channel_id=1, source_target_pairs={{0,17},{1,65},{2,66},{3,18},{4,21},{5,69},{6,70},{7,22},{8,25},{9,... | collective-permute-start | bytes 196616 | tf_op jit(solution)/shard_map/ppermute | solution.py:204
  19.6 4.5 %collective-permute-start.12 = (f32[128,128]{1,0:T(8,128)S(1)}, f32[128,128]{1,0:T(8,128)S(1)}, u32[]{:S(2)}, u32[]{:S(2)}) collective-permute-start(f32[128,128]{1,0:T(8,128)S(1)} %add.85), channel_id=1, source_target_pairs={{0,17},{1,65},{2,66},{3,18},{4,21},{5,69},{6,70},{7,22},{8,25},{9,... | collective-permute-start | bytes 196616 | tf_op jit(solution)/shard_map/ppermute | solution.py:204
  23.4 4.1 %collective-permute-start.4 = (f32[128,128]{1,0:T(8,128)S(1)}, f32[128,128]{1,0:T(8,128)S(1)}, u32[]{:S(2)}, u32[]{:S(2)}) collective-permute-start(f32[128,128]{1,0:T(8,128)S(1)} %add.78), channel_id=1, source_target_pairs={{0,7},{1,16},{2,19},{3,4},{4,3},{5,20},{6,23},{7,0},{8,15},{9,24},... | collective-permute-start | bytes 196616 | tf_op jit(solution)/shard_map/ppermute | solution.py:204
  24.1 7.5 %collective-permute-start.13 = (f32[128,128]{1,0:T(8,128)S(1)}, f32[128,128]{1,0:T(8,128)S(1)}, u32[]{:S(2)}, u32[]{:S(2)}) collective-permute-start(f32[128,128]{1,0:T(8,128)S(1)} %add.86), channel_id=1, source_target_pairs={{0,7},{1,16},{2,19},{3,4},{4,3},{5,20},{6,23},{7,0},{8,15},{9,24},... | collective-permute-start | bytes 196616 | tf_op jit(solution)/shard_map/ppermute | solution.py:204
  27.5 6.2 %collective-permute-start.5 = (f32[128,128]{1,0:T(8,128)S(1)}, f32[128,128]{1,0:T(8,128)S(1)}, u32[]{:S(2)}, u32[]{:S(2)}) collective-permute-start(f32[128,128]{1,0:T(8,128)S(1)} %add.79), channel_id=1, source_target_pairs={{0,25},{1,224},{2,227},{3,26},{4,29},{5,228},{6,231},{7,30},{8,17}... | collective-permute-start | bytes 196616 | tf_op jit(solution)/shard_map/ppermute | solution.py:204
  31.6 5.1 %collective-permute-start.14 = (f32[128,128]{1,0:T(8,128)S(1)}, f32[128,128]{1,0:T(8,128)S(1)}, u32[]{:S(2)}, u32[]{:S(2)}) collective-permute-start(f32[128,128]{1,0:T(8,128)S(1)} %add.87), channel_id=1, source_target_pairs={{0,25},{1,224},{2,227},{3,26},{4,29},{5,228},{6,231},{7,30},{8,17}... | collective-permute-start | bytes 196616 | tf_op jit(solution)/shard_map/ppermute | solution.py:204
  33.8 5.4 %collective-permute-start.6 = (f32[128,128]{1,0:T(8,128)S(1)}, f32[128,128]{1,0:T(8,128)S(1)}, u32[]{:S(2)}, u32[]{:S(2)}) collective-permute-start(f32[128,128]{1,0:T(8,128)S(1)} %add.80), channel_id=1, source_target_pairs={{0,64},{1,6},{2,5},{3,67},{4,68},{5,2},{6,1},{7,71},{8,72},{9,14},... | collective-permute-start | bytes 196616 | tf_op jit(solution)/shard_map/ppermute | solution.py:204
  36.8 5.7 %collective-permute-start.15 = (f32[128,128]{1,0:T(8,128)S(1)}, f32[128,128]{1,0:T(8,128)S(1)}, u32[]{:S(2)}, u32[]{:S(2)}) collective-permute-start(f32[128,128]{1,0:T(8,128)S(1)} %add.88), channel_id=1, source_target_pairs={{0,64},{1,6},{2,5},{3,67},{4,68},{5,2},{6,1},{7,71},{8,72},{9,14},... | collective-permute-start | bytes 196616 | tf_op jit(solution)/shard_map/ppermute | solution.py:204
  39.2 5.5 %collective-permute-start.7 = (f32[128,128]{1,0:T(8,128)S(1)}, f32[128,128]{1,0:T(8,128)S(1)}, u32[]{:S(2)}, u32[]{:S(2)}) collective-permute-start(f32[128,128]{1,0:T(8,128)S(1)} %add.81), channel_id=1, source_target_pairs={{0,225},{1,24},{2,27},{3,226},{4,229},{5,28},{6,31},{7,230},{8,233... | collective-permute-start | bytes 196616 | tf_op jit(solution)/shard_map/ppermute | solution.py:204
  42.5 5.0 %collective-permute-start.16 = (f32[128,128]{1,0:T(8,128)S(1)}, f32[128,128]{1,0:T(8,128)S(1)}, u32[]{:S(2)}, u32[]{:S(2)}) collective-permute-start(f32[128,128]{1,0:T(8,128)S(1)} %add.89), channel_id=1, source_target_pairs={{0,225},{1,24},{2,27},{3,226},{4,229},{5,28},{6,31},{7,230},{8,233... | collective-permute-start | bytes 196616 | tf_op jit(solution)/shard_map/ppermute | solution.py:204
  44.7 2.9 %collective-permute-start.8 = (f32[128,128]{1,0:T(8,128)S(1)}, f32[128,128]{1,0:T(8,128)S(1)}, u32[]{:S(2)}, u32[]{:S(2)}) collective-permute-start(f32[128,128]{1,0:T(8,128)S(1)} %add.82.own_ref.own1), channel_id=1, source_target_pairs={{0,1},{1,0},{2,3},{3,2},{4,5},{5,4},{6,7},{7,6},{8,9},{9,8},{10,11... | collective-permute-start | bytes 196616 | tf_op jit(solution)/shard_map/ppermute | solution.py:208
  47.5 2.5 %collective-permute-start.17 = (f32[128,128]{1,0:T(8,128)S(1)}, f32[128,128]{1,0:T(8,128)S(1)}, u32[]{:S(2)}, u32[]{:S(2)}) collective-permute-start(f32[128,128]{1,0:T(8,128)S(1)} %add.90.own0), channel_id=1, source_target_pairs={{0,1},{1,0},{2,3},{3,2},{4,5},{5,4},{6,7},{7,6},{8,9},{9,8},{10,11... | collective-permute-start | bytes 196616 | tf_op jit(solution)/shard_map/ppermute | solution.py:208
